TPU v7x, 32 devices: a whole 2x2x4 slice. The times are simulated.
32 devices in a mesh: dp: 8 (over z, y), tensor: 4 (over x, core).
Axes of the slice: x: 2, y: 2, z: 4, core: 2. Of those that a mesh axis runs over, the one named last changes fastest.
Arguments:
- tokens: bfloat16 [4096, 768], P('dp'), may hold values from -6 to 6
- lengths: int32 [8, 3], P('dp'), may hold values from 1 to 384, 512 in all within a row
- routes: int32 [4096, 2], P('dp'), may hold values from 0 to 63, all different within a row; in each aligned block of 512 rows (0 to 511, 512 to 1023, ...) at most 32 rows name the same one
- rel_bucket: int32 [384], replicated, may hold values from 0 to 31, as said below
- norm1: bfloat16 [768], replicated, may hold values from 0.5 to 1.5
- w_query: bfloat16 [768, 768], P(None, 'tensor'), may hold values from -0.21875 to 0.21875
- w_key: bfloat16 [768, 768], P(None, 'tensor'), may hold values from -0.21875 to 0.21875
- w_value: bfloat16 [768, 768], P(None, 'tensor'), may hold values from -0.21875 to 0.21875
- output_weight: bfloat16 [768, 768], P('tensor'), may hold values from -1.75 to 1.75
- position_bias_table: bfloat16 [12, 32], P('tensor'), may hold values from -4 to 4
- norm2: bfloat16 [768], replicated, may hold values from 0.5 to 1.5
- router: bfloat16 [768, 64], replicated, may hold values from -0.14941406 to 0.14941406
- expert_in: bfloat16 [64, 768, 3072], P('dp', None, 'tensor'), may hold values from -0.21875 to 0.21875
- expert_out: bfloat16 [64, 3072, 768], P('dp', 'tensor'), may hold values from -0.109375 to 0.109375
- cotangent: bfloat16 [4096, 768], P('dp'), may hold values from -6 to 6
Outputs:
- layer_out: bfloat16 [4096, 768], P('dp')
- grad_tokens: float32 [4096, 768], P('dp')
- grad_norm1: float32 [768], replicated
- grad_query: float32 [768, 768], P(None, 'tensor')
- grad_key: float32 [768, 768], P(None, 'tensor')
- grad_value: float32 [768, 768], P(None, 'tensor')
- grad_output: float32 [768, 768], P('tensor')
- gradient_bias_table: float32 [12, 32], P('tensor')
- grad_norm2: float32 [768], replicated
- grad_router: float32 [768, 64], replicated
- grad_expert_in: float32 [64, 768, 3072], P('dp', None, 'tensor')
- grad_expert_out: float32 [64, 3072, 768], P('dp', 'tensor')
Inputs may be any that keep to these rules, and one draw needn't show every extreme that they name: `lengths`: each row sums to 512 and its largest entry is 384. `routes`: a token names 2 different experts; among the tokens of one index of dp no expert is named more than 32 times, a bound that some block reaches. `rel_bucket`: nondecreasing in the offset; offsets below 16 are their own bucket; the last offset has bucket 32 - 1.
All inputs are finite; a program needn't handle non-finite values.
Results may differ from a plain program's by a relative error of at most 0.017.
Values may be sent and summed in bfloat16 or wider, within the bound.
No kernel may reach another device: no remote copies, remote signals or barrier semaphores. Data moves between devices by JAX's collectives and lax.ppermute only.
A program may use at most 192 MiB of HBM per device.

v0:
```python
import jax
import jax.numpy as jnp
from jax import lax
from jax.sharding import PartitionSpec as P

epsilon = 1e-06
masked_value = -1e30


def segment_ids(lengths_row, token_count):
    seq_ends = jnp.cumsum(lengths_row)
    positions = jnp.arange(token_count, dtype=jnp.int32)
    return jnp.sum((positions[:, None] >= seq_ends[None, :]).astype(jnp.int32), axis=1)


def route_slots(routes, experts):
    flat_routes = routes.reshape(-1)
    route_hits = (flat_routes[:, None] == jnp.arange(experts, dtype=jnp.int32)[None, :]).astype(
        jnp.int32
    )
    slot_rank = jnp.cumsum(route_hits, axis=0) - 1
    return jnp.sum(slot_rank * route_hits, axis=1).reshape(routes.shape)


def place_rows(rows_pair, routes, slot_index, experts, capacity):
    buffer = jnp.zeros((experts, capacity, rows_pair.shape[2]), rows_pair.dtype)
    return buffer.at[routes, slot_index].set(rows_pair)


def inner_rows(left_side, right_side):
    return lax.dot_general(
        left_side, right_side, (((0,), (0,)), ((), ())), preferred_element_type=jnp.float32
    )


def outer_cols(left_side, right_side):
    return lax.dot_general(
        left_side, right_side, (((1,), (1,)), ((), ())), preferred_element_type=jnp.float32
    )


def block_context(rel_bucket, segment, row_start, row_count, buckets):
    token_count = segment.shape[0]
    query_index = row_start + jnp.arange(row_count, dtype=jnp.int32)
    key_index = jnp.arange(token_count, dtype=jnp.int32)
    offset = jnp.clip(query_index[:, None] - key_index[None, :], 0, rel_bucket.shape[0] - 1)
    bucket = jnp.take(rel_bucket, offset)
    bucket_indicator = (
        jnp.arange(buckets, dtype=jnp.int32)[:, None, None] == bucket[None, :, :]
    ).astype(jnp.bfloat16)
    allowed = (segment[:, None] == segment[None, :]) & (query_index[:, None] >= key_index[None, :])
    return (bucket_indicator, allowed)


def block_scores(
    query_block, key_heads, bucket_indicator, position_bias_table, allowed, score_scale
):
    raw_scores = (
        jnp.einsum("qhd,khd->hqk", query_block, key_heads, preferred_element_type=jnp.float32)
        * score_scale
    )
    raw_scores = raw_scores + jnp.einsum(
        "zd,dpv->zpv", position_bias_table, bucket_indicator, preferred_element_type=jnp.float32
    )
    return jnp.where(allowed[None], raw_scores, masked_value)


def norm_back(values, scale_inv, gain, grad_out):
    weighted = grad_out * gain
    grad_in = scale_inv * weighted - values * scale_inv**3 * jnp.mean(
        values * weighted, axis=-1, keepdims=True
    )
    grad_gain = jnp.sum(grad_out * values * scale_inv, axis=0)
    return (grad_in, grad_gain)


def gelu_tanh(values):
    return jax.nn.gelu(values, approximate=True)


def body(
    tokens,
    lengths,
    routes,
    rel_bucket,
    norm1,
    w_query,
    w_key,
    w_value,
    output_weight,
    position_bias_table,
    norm2,
    router,
    expert_in,
    expert_out,
    cotangent,
):
    token_count, model_width = tokens.shape
    local_heads, buckets = position_bias_table.shape
    head_size = w_query.shape[1] // local_heads
    experts = router.shape[1]
    top_count = routes.shape[1]
    capacity = 2 * top_count * token_count // experts
    row_count = min(512, token_count)
    score_scale = head_size ** (-0.5)
    gain_one = norm1.astype(jnp.float32)
    gain_two = norm2.astype(jnp.float32)
    inputs = tokens.astype(jnp.float32)
    segment = segment_ids(lengths[0], token_count)
    scale_one = lax.rsqrt(jnp.mean(inputs * inputs, axis=-1, keepdims=True) + epsilon)
    first_normed = (inputs * scale_one * gain_one).astype(jnp.bfloat16)
    query_proj = jnp.dot(first_normed, w_query, preferred_element_type=jnp.float32).astype(
        jnp.bfloat16
    )
    key_proj = jnp.dot(first_normed, w_key, preferred_element_type=jnp.float32).astype(jnp.bfloat16)
    value_proj = jnp.dot(first_normed, w_value, preferred_element_type=jnp.float32).astype(
        jnp.bfloat16
    )
    query_heads = query_proj.reshape(token_count, local_heads, head_size)
    key_heads = key_proj.reshape(token_count, local_heads, head_size)
    value_heads = value_proj.reshape(token_count, local_heads, head_size)
    block_index = 0
    row_start = block_index * row_count
    bucket_indicator, allowed = block_context(rel_bucket, segment, row_start, row_count, buckets)
    scores = block_scores(
        query_heads, key_heads, bucket_indicator, position_bias_table, allowed, score_scale
    )
    row_peak = jnp.max(scores, axis=2, keepdims=True)
    lifted = jnp.exp(scores - row_peak)
    row_total = jnp.sum(lifted, axis=2, keepdims=True)
    weights = (lifted / row_total).astype(jnp.bfloat16)
    attended_blocks = jnp.einsum(
        "hqk,khd->qhd", weights, value_heads, preferred_element_type=jnp.float32
    )
    log_sums = [row_peak + jnp.log(row_total)]
    attended = attended_blocks.reshape(token_count, local_heads * head_size).astype(jnp.bfloat16)
    branch = lax.psum(
        jnp.dot(attended, output_weight, preferred_element_type=jnp.float32), "tensor"
    )
    hidden_state = inputs + branch
    scale_two = lax.rsqrt(jnp.mean(hidden_state * hidden_state, axis=-1, keepdims=True) + epsilon)
    second_normed = (hidden_state * scale_two * gain_two).astype(jnp.bfloat16)
    logits = jnp.dot(second_normed, router, preferred_element_type=jnp.float32)
    chosen = jnp.take_along_axis(logits, routes, axis=1)
    gate_weights = jax.nn.softmax(chosen, axis=1)
    slot_index = route_slots(routes, experts)
    outgoing = place_rows(
        jnp.broadcast_to(second_normed[:, None, :], (token_count, top_count, model_width)),
        routes,
        slot_index,
        experts,
        capacity,
    )
    arrived = lax.all_to_all(outgoing, "dp", split_axis=0, concat_axis=1, tiled=True)
    pre_gelu = jnp.einsum("erd,edf->erf", arrived, expert_in, preferred_element_type=jnp.float32)
    activated = gelu_tanh(pre_gelu).astype(jnp.bfloat16)
    produced = jnp.einsum("erf,efd->erd", activated, expert_out, preferred_element_type=jnp.float32)
    returned = lax.all_to_all(
        produced.astype(jnp.bfloat16), "dp", split_axis=1, concat_axis=0, tiled=True
    ).astype(produced.dtype)
    expert_rows = lax.psum(returned[routes, slot_index].astype(jnp.bfloat16), "tensor").astype(
        jnp.float32
    )
    result = hidden_state + jnp.sum(gate_weights[:, :, None] * expert_rows, axis=1)
    layer_out = result.astype(jnp.bfloat16)
    grad_out = cotangent.astype(jnp.float32)
    grad_gate = jnp.sum(expert_rows * grad_out[:, None, :], axis=2)
    grad_chosen = gate_weights * (
        grad_gate - jnp.sum(gate_weights * grad_gate, axis=1, keepdims=True)
    )
    expert_ids = jnp.arange(experts, dtype=jnp.int32)
    grad_logits = jnp.sum(
        (routes[:, :, None] == expert_ids).astype(jnp.float32) * grad_chosen[:, :, None], axis=1
    )
    normed_wide = second_normed.astype(jnp.float32)
    router_wide = router.astype(jnp.float32)
    grad_router = jnp.dot(normed_wide.T, grad_logits, precision=lax.Precision.HIGHEST)
    grad_from_router = jnp.dot(grad_logits, router_wide.T, precision=lax.Precision.HIGHEST)
    grad_rows = (gate_weights[:, :, None] * grad_out[:, None, :]).astype(jnp.bfloat16)
    grad_arrived = lax.all_to_all(
        place_rows(grad_rows, routes, slot_index, experts, capacity),
        "dp",
        split_axis=0,
        concat_axis=1,
        tiled=True,
    )
    grad_act = jnp.einsum(
        "erd,efd->erf", grad_arrived, expert_out, preferred_element_type=jnp.float32
    )
    grad_pre = jax.vjp(gelu_tanh, pre_gelu)[1](grad_act)[0].astype(jnp.bfloat16)
    grad_expert_out = jnp.einsum(
        "erf,erd->efd", activated, grad_arrived, preferred_element_type=jnp.float32
    )
    grad_expert_in = jnp.einsum(
        "erd,erf->edf", arrived, grad_pre, preferred_element_type=jnp.float32
    )
    grad_inputs = jnp.einsum(
        "erf,edf->erd", grad_pre, expert_in, preferred_element_type=jnp.float32
    )
    grad_returned = lax.all_to_all(
        grad_inputs.astype(jnp.bfloat16), "dp", split_axis=1, concat_axis=0, tiled=True
    ).astype(grad_inputs.dtype)
    grad_expert_tokens = jnp.sum(grad_returned[routes, slot_index], axis=1)
    grad_normed_two = (
        lax.psum(grad_expert_tokens.astype(jnp.bfloat16), "tensor").astype(jnp.float32)
        + grad_from_router
    )
    grad_hidden, grad_norm2 = norm_back(hidden_state, scale_two, gain_two, grad_normed_two)
    grad_hidden = grad_out + grad_hidden
    grad_branch = grad_hidden.astype(jnp.bfloat16)
    grad_w_output = inner_rows(attended, grad_branch)
    grad_attended = outer_cols(grad_branch, output_weight).astype(jnp.bfloat16)
    grad_attended_heads = grad_attended.reshape(token_count, local_heads, head_size)
    block_index = 0
    row_start = block_index * row_count
    bucket_indicator, allowed = block_context(rel_bucket, segment, row_start, row_count, buckets)
    scores = block_scores(
        query_heads, key_heads, bucket_indicator, position_bias_table, allowed, score_scale
    )
    probs = jnp.exp(scores - log_sums[block_index])
    probs_low = probs.astype(jnp.bfloat16)
    grad_value_sum = jnp.einsum(
        "hqk,qhd->khd", probs_low, grad_attended_heads, preferred_element_type=jnp.float32
    )
    grad_probs = jnp.einsum(
        "qhd,khd->hqk", grad_attended_heads, value_heads, preferred_element_type=jnp.float32
    )
    row_delta = jnp.sum(probs * grad_probs, axis=2, keepdims=True)
    gradient_attention_scores = (probs * (grad_probs - row_delta)).astype(jnp.bfloat16)
    grad_query_blocks = (
        jnp.einsum(
            "hqk,khd->qhd", gradient_attention_scores, key_heads, preferred_element_type=jnp.float32
        )
        * score_scale
    )
    grad_key_sum = (
        jnp.einsum(
            "hqk,qhd->khd",
            gradient_attention_scores,
            query_heads,
            preferred_element_type=jnp.float32,
        )
        * score_scale
    )
    gradient_bias_table = jnp.einsum(
        "ruo,vuo->rv",
        gradient_attention_scores,
        bucket_indicator,
        preferred_element_type=jnp.float32,
    )
    grad_query_low = grad_query_blocks.reshape(token_count, local_heads * head_size).astype(
        jnp.bfloat16
    )
    grad_key_low = grad_key_sum.reshape(token_count, local_heads * head_size).astype(jnp.bfloat16)
    grad_value_low = grad_value_sum.reshape(token_count, local_heads * head_size).astype(
        jnp.bfloat16
    )
    grad_w_query = inner_rows(first_normed, grad_query_low)
    grad_w_key = inner_rows(first_normed, grad_key_low)
    grad_w_value = inner_rows(first_normed, grad_value_low)
    gradient_normalized_piece = (
        outer_cols(grad_query_low, w_query)
        + outer_cols(grad_key_low, w_key)
        + outer_cols(grad_value_low, w_value)
    )
    grad_normed_one = lax.psum(gradient_normalized_piece.astype(jnp.bfloat16), "tensor").astype(
        jnp.float32
    )
    grad_input, grad_norm1 = norm_back(inputs, scale_one, gain_one, grad_normed_one)
    grad_tokens = grad_hidden + grad_input
    summed = lax.psum(
        (
            grad_w_query,
            grad_w_key,
            grad_w_value,
            grad_w_output,
            gradient_bias_table,
            grad_norm1,
            grad_norm2,
            grad_router,
        ),
        "dp",
    )
    return (
        layer_out,
        grad_tokens,
        summed[5],
        summed[0],
        summed[1],
        summed[2],
        summed[3],
        summed[4],
        summed[6],
        summed[7],
        grad_expert_in,
        grad_expert_out,
    )


def solution(mesh):
    in_specs = (
        P("dp", None),
        P("dp", None),
        P("dp", None),
        P(),
        P(),
        P(None, "tensor"),
        P(None, "tensor"),
        P(None, "tensor"),
        P("tensor", None),
        P("tensor", None),
        P(),
        P(),
        P("dp", None, "tensor"),
        P("dp", "tensor", None),
        P("dp", None),
    )
    out_specs = (
        P("dp", None),
        P("dp", None),
        P(),
        P(None, "tensor"),
        P(None, "tensor"),
        P(None, "tensor"),
        P("tensor", None),
        P("tensor", None),
        P(),
        P(),
        P("dp", None, "tensor"),
        P("dp", "tensor", None),
    )
    return jax.shard_map(body, mesh=mesh, in_specs=in_specs, out_specs=out_specs, check_vma=False)
```

profile of v0, /device:TPU:1, one launch (start us, length us, event | category | flops | bytes accessed | tf_op | source)
XLA Modules:
  0.0 2364.2 jit_solution(16426477172795028012)
XLA Ops:
  11.1 2.4 convolution_convert_fusion.4
  17.2 1631.4 %gather_fusion.3 = s32[262144]{0:T(1024)S(1)} fusion(s32[384]{0:T(512)S(1)} %copy-done.1, s32[262144]{0:T(1024)S(1)} %broadcast_clamp_fusion), kind=kCustom, calls=%fused_computation.clone | custom fusion | bytes 3145728 | tf_op jit(solution)/shard_map/jit(_take)/gather | solution.py:47
  1649.3 5.1 fusion.1
  1660.9 18.0 reduce-window.19
  1680.9 24.4 %all-reduce.8.cloned.1.call-done = f32[512,768]{1,0:T(8,128)} async-done(((f32[512,768]{1,0:T(8,128)}), f32[512,768]{1,0:T(8,128)}) %all-reduce.8.cloned.1.call-update) | async-done | bytes 1572880 | tf_op jit(solution)/shard_map/psum | solution.py:137
  1709.6 8.6 gather_fusion.2
  1720.1 3.4 multiply_convert_fusion.2
  1724.2 7.6 scatter_custom_fusion.1
  1731.7 5.2 all-to-all-start.2
  1737.0 3.1 broadcast_in_dim.31
  1740.1 4.7 reshape.324
  1744.7 7.9 scatter_custom_fusion
  1752.6 54.0 %all-to-all-done.2 = bf16[64,32,768]{2,1,0:T(8,128)(2,1)S(1)} async-done(((bf16[64,32,768]{2,1,0:T(8,128)(2,1)}), bf16[64,32,768]{2,1,0:T(8,128)(2,1)S(1)}, u32[]{:S(2)}, u32[]{:S(2)}) %all-to-all-start.2) | async-done | bytes 3145760 | tf_op jit(solution)/shard_map/all_to_all | solution.py:180
  1808.3 14.7 all-to-all-start
  1823.0 2.2 copy.197
  1825.2 67.3 %all-to-all-done = bf16[64,32,768]{2,1,0:T(8,128)(2,1)} async-done(((bf16[64,32,768]{2,1,0:T(8,128)(2,1)}), bf16[64,32,768]{2,1,0:T(8,128)(2,1)}, u32[]{:S(2)}, u32[]{:S(2)}) %all-to-all-start) | async-done | bytes 3145760 | tf_op jit(solution)/shard_map/all_to_all | solution.py:154
  1892.5 2.2 copy.193
  1894.7 12.7 fusion.74
  1907.3 12.0 fusion.10
  1919.4 11.1 convolution_convert_fusion
  1930.5 3.4 copy.198
  1933.9 5.1 all-to-all-start.3
  1939.0 8.3 convolution_convert_fusion.1
  1947.4 3.4 copy.194
  1950.8 58.3 %all-to-all-done.3 = bf16[8,256,768]{2,0,1:T(8,128)(2,1)S(1)} async-done(((bf16[8,256,768]{2,0,1:T(8,128)(2,1)}), bf16[8,256,768]{2,0,1:T(8,128)(2,1)S(1)}, u32[]{:S(2)}, u32[]{:S(2)}) %all-to-all-start.3) | async-done | bytes 3145760 | tf_op jit(solution)/shard_map/all_to_all | solution.py:200
  2009.0 4.5 all-to-all-start.1
  2015.6 3.6 copy.199
  2019.2 14.1 gather_fusion.1
  2033.3 3.0 reshape.313
  2036.4 46.6 %all-to-all-done.1 = bf16[8,256,768]{2,0,1:T(8,128)(2,1)} async-done(((bf16[8,256,768]{2,0,1:T(8,128)(2,1)}), bf16[8,256,768]{2,0,1:T(8,128)(2,1)}, u32[]{:S(2)}, u32[]{:S(2)}) %all-to-all-start.1) | async-done | bytes 3145760 | tf_op jit(solution)/shard_map/all_to_all | solution.py:158
  2083.0 2.7 copy.195
  2085.7 13.9 gather_fusion
  2099.6 4.5 reshape.336
  2104.1 6.7 reduce_sum.151
  2111.7 55.1 %all-reduce.14.cloned.1.call-done = (bf16[512,2,768]{2,1,0:T(2,128)(2,1)}, bf16[512,768]{1,0:T(8,128)(2,1)}) async-done(((bf16[512,2,768]{2,1,0:T(2,128)(2,1)}, bf16[512,768]{1,0:T(8,128)(2,1)}), (bf16[512,2,768]{2,1,0:T(2,128)(2,1)}, bf16[512,768]{1,0:T(8,128)(2,1)})) %all-reduce.14.cloned.1.call-update) | async-done | bytes 2359312 | tf_op jit(solution)/shard_map/psum | solution.py:161
  2166.9 9.9 fusion.12
  2179.3 2.4 multiply_reduce_fusion.1
  2181.8 2.7 subtract_add_fusion
  2194.5 2.3 fusion.77
  2196.8 2.1 fusion.50
  2198.9 12.7 fusion.78
  2211.6 12.8 fusion.60
  2224.4 7.2 fusion.41
  2231.6 2.1 fusion.28
  2233.7 31.7 %all-reduce = (f32[768]{0:T(1024)}, f32[3,32]{1,0:T(4,128)}, f32[768]{0:T(1024)}) all-reduce(f32[768]{0:T(1024)S(1)} %get-tuple-element.15, f32[3,32]{1,0:T(4,128)S(1)} %fusion.41, f32[768]{0:T(1024)S(1)} %get-tuple-element.13), channel_id=1, replica_groups=mesh['dp'=8,'tensor'=4] {'dp'}, use_global_device_ids=true, to_apply=%region_26.28 | all-reduce | flops 1632 | bytes 13056 | tf_op jit(solution)/shard_map/psum | solution.py:271
  2265.4 3.0 fusion.19
  2268.4 81.8 %all-reduce.12.cloned.1.call-done = (f32[768,192]{0,1:T(8,128)}, f32[768,192]{0,1:T(8,128)}, f32[768,192]{0,1:T(8,128)}, f32[192,768]{1,0:T(8,128)}, f32[768,64]{0,1:T(8,128)}) async-done(((f32[768,192]{0,1:T(8,128)}, f32[768,192]{0,1:T(8,128)}, f32[768,192]{0,1:T(8,128)}, f32[192,768]{1,0:T(8,128)}, f32[768,64]{0,1:T(8,128)}), (f32[768,192]{0,1:T(8,128)}, f32[768,192]{0,1:T(8,128)}, f32[768,192]{0,1:T(8,128)}, ...) | async-done | bytes 2555920 | tf_op jit(solution)/shard_map/psum | solution.py:271
  2350.2 2.0 copy.231
  (199 shorter events, 45.5 us)
Async XLA Ops:
  7.2 1651.5 %copy-start = (bf16[192,768]{1,0:T(8,128)(2,1)S(1)}, bf16[192,768]{1,0:T(8,128)(2,1)}, u32[]{:S(2)}) copy-start(bf16[192,768]{1,0:T(8,128)(2,1)} %param.25) | copy-start | bytes 884740
  7.2 6.3 copy-start.12
  7.2 6.3 copy-start.34
  7.2 7.4 copy-start.31
  7.2 1698.0 %all-reduce.8.cloned.1.call-start = ((), (), s32[]{:S(2)}) async-start(), calls=%async_computation.4 | async-start | bytes 3145728 | tf_op jit(solution)/shard_map/psum | solution.py:137
  10.4 5.4 copy-start.48
  11.1 4.7 copy-start.43
  14.7 2.5 copy-start.1
  1649.3 5.2 copy-start.20
  1649.3 5.2 copy-start.22
  1649.3 5.2 copy-start.24
  1649.3 5.2 copy-start.26
  1656.2 1.8 copy-start.2
  1656.2 1.8 copy-start.40
  1658.0 2.3 copy-start.39
  1658.1 2.8 copy-start.51
  1660.3 19.6 copy-start.52
  1660.3 19.7 copy-start.53
  1660.3 20.5 copy-start.18
  1660.8 46.8 %copy-start.41 = (f32[768]{0:T(1024)}, f32[768]{0:T(1024)S(1)}, u32[]{:S(2)}) copy-start(f32[768]{0:T(1024)S(1)} %convert_element_type.162) | copy-start | bytes 9220
  1660.9 44.4 %copy-start.13 = (bf16[512,768]{1,0:T(8,128)(2,1)S(1)}, bf16[512,768]{1,0:T(8,128)(2,1)}, u32[]{:S(2)}) copy-start(bf16[512,768]{1,0:T(8,128)(2,1)} %param.17) | copy-start | bytes 2359300
  1680.9 39.2 %copy-start.9 = (f32[512,768]{1,0:T(8,128)}, f32[512,768]{1,0:T(8,128)S(1)}, u32[]{:S(2)}) copy-start(f32[512,768]{1,0:T(8,128)S(1)} %convert_element_type.174) | copy-start | bytes 4718596
  1680.9 28.4 %copy-start.29 = (bf16[768,64]{0,1:T(8,128)(2,1)S(1)}, bf16[768,64]{0,1:T(8,128)(2,1)}, u32[]{:S(2)}) copy-start(bf16[768,64]{0,1:T(8,128)(2,1)} %param.28) | copy-start | bytes 294916
  1707.6 10.7 copy-start.45
  1731.7 74.9 %all-to-all-start.2 = ((bf16[64,32,768]{2,1,0:T(8,128)(2,1)}), bf16[64,32,768]{2,1,0:T(8,128)(2,1)S(1)}, u32[]{:S(2)}, u32[]{:S(2)}) async-start(bf16[64,32,768]{2,1,0:T(8,128)(2,1)} %bitcast.126), calls=%async_computation.2 | async-start | bytes 6291456 | tf_op jit(solution)/shard_map/all_to_all | solution.py:180
  1808.3 84.2 %all-to-all-start = ((bf16[64,32,768]{2,1,0:T(8,128)(2,1)}), bf16[64,32,768]{2,1,0:T(8,128)(2,1)}, u32[]{:S(2)}, u32[]{:S(2)}) async-start(bf16[64,32,768]{2,1,0:T(8,128)(2,1)} %bitcast.125), calls=%async_computation | async-start | bytes 6291456 | tf_op jit(solution)/shard_map/all_to_all | solution.py:154
  1825.2 69.5 %copy-start.4 = (bf16[8,8,32,768]{3,2,1,0:T(8,128)(2,1)}, bf16[8,8,32,768]{3,2,1,0:T(8,128)(2,1)S(1)}, u32[]{:S(2)}) copy-start(bf16[8,8,32,768]{3,2,1,0:T(8,128)(2,1)S(1)} %copy.197) | copy-start | bytes 9437188
  1894.7 12.7 copy-start.8
  1919.4 11.2 copy-start.16
  1933.9 75.1 %all-to-all-start.3 = ((bf16[8,256,768]{2,0,1:T(8,128)(2,1)}), bf16[8,256,768]{2,0,1:T(8,128)(2,1)S(1)}, u32[]{:S(2)}, u32[]{:S(2)}) async-start(bf16[8,256,768]{2,0,1:T(8,128)(2,1)} %copy.198), calls=%async_computation.3 | async-start | bytes 6291456 | tf_op jit(solution)/shard_map/all_to_all | solution.py:200
  2009.0 74.0 %all-to-all-start.1 = ((bf16[8,256,768]{2,0,1:T(8,128)(2,1)}), bf16[8,256,768]{2,0,1:T(8,128)(2,1)}, u32[]{:S(2)}, u32[]{:S(2)}) async-start(bf16[8,256,768]{2,0,1:T(8,128)(2,1)} %copy.194), calls=%async_computation.1 | async-start | bytes 6291456 | tf_op jit(solution)/shard_map/all_to_all | solution.py:158
  2013.6 153.3 %all-reduce.14.cloned.1.call-start = ((), (), s32[]{:S(2)}) async-start(), calls=%async_computation.7 | async-start | bytes 4718592 | tf_op jit(solution)/shard_map/psum | solution.py:161
  2104.1 62.7 %copy-start.10 = (f32[512,768]{1,0:T(8,128)S(1)}, f32[512,768]{1,0:T(8,128)}, u32[]{:S(2)}) copy-start(f32[512,768]{1,0:T(8,128)} %copy-done.9) | copy-start | bytes 4718596
  2110.8 68.5 %copy-start.7 = (f32[512,768]{1,0:T(8,128)S(1)}, f32[512,768]{1,0:T(8,128)}, u32[]{:S(2)}) copy-start(f32[512,768]{1,0:T(8,128)} %copy-done.6) | copy-start | bytes 4718596
  2110.8 68.5 %copy-start.30 = (bf16[768,64]{0,1:T(8,128)(2,1)S(1)}, bf16[768,64]{0,1:T(8,128)(2,1)}, u32[]{:S(2)}) copy-start(bf16[768,64]{0,1:T(8,128)(2,1)} %param.28) | copy-start | bytes 294916
  2110.9 120.8 %all-reduce.10.cloned.1.call-start = ((), (), s32[]{:S(2)}) async-start(), calls=%async_computation.5 | async-start | bytes 1572864 | tf_op jit(solution)/shard_map/psum | solution.py:266
  2177.8 3.9 copy-start.17
  2179.3 2.4 copy-start.19
  2181.8 3.1 copy-start.3
  2187.2 2.4 copy-start.33
  2188.2 3.1 copy-start.35
  2190.0 3.0 copy-start.32
  2194.3 155.9 %all-reduce.12.cloned.1.call-start = ((), (), s32[]{:S(2)}) async-start(), calls=%async_computation.6 | async-start | bytes 5111808 | tf_op jit(solution)/shard_map/psum | solution.py:271
  2198.9 12.7 copy-start.5
  2211.6 12.8 copy-start.21
  2224.4 41.0 %copy-start.50 = (f32[512]{0:T(512)S(1)}, f32[512]{0:T(512)}, u32[]{:S(2)}) copy-start(f32[512]{0:T(512)} %get-tuple-element.38) | copy-start | bytes 6148
  2350.2 5.8 copy-start.28
  2350.2 6.6 copy-start.38
  (15 other events, 15.8 us)
Sparse Core Ops, SparseCore 0:
  1660.4 44.7 all-reduce.7
  2110.9 55.8 all-reduce.13
  2194.4 33.5 all-reduce.9
  2233.1 116.9 all-reduce.11
where the time goes:
time: 2370 us; the launch traced here: 2360 us
  local copies, waits for them, and re-layouts  1740 us (73%)
  waiting for transfers between devices  388 us (16%)
  matrix products  106 us (4%)
  other arithmetic  57.6 us (2%)
  blocking collectives  31.7 us (1%)
  starting transfers between devices  29.9 us (1%)
    gather x2, local copies, waits for them, and re-layouts, block_context(): bucket = jnp.take(rel_bucket, offset)  1630 us
    psum x1, waiting for transfers between devices, body(): lax.psum((grad_w_query, grad_w_key, grad_w_value, grad_w_output, gradient...  81.8 us
    all_to_all x1, waiting for transfers between devices, body(): lax.all_to_all(outgoing, 'dp', split_axis=0, concat_axis=1, tiled=True)  67.3 us
    all_to_all x1, waiting for transfers between devices, body(): lax.all_to_all(grad_inputs.astype(jnp.bfloat16), 'dp', split_axis=1, conc...  58.3 us
    psum x1, waiting for transfers between devices, body(): lax.psum(returned[routes, slot_index].astype(jnp.bfloat16), 'tensor')  55.1 us
    all_to_all x1, waiting for transfers between devices, body(): lax.all_to_all(place_rows(grad_rows, routes, slot_index, experts, capacit...  54 us
  transfers between devices with their start and end apart: 8, of which 7 were waited for; matrix products, arithmetic and copies ran while one was open for 5% of the time, Pallas kernels for 0%

commit v1 on v0

--- a/solution.py
+++ b/solution.py
@@ -44,9 +44,11 @@
     query_index = row_start + jnp.arange(row_count, dtype=jnp.int32)
     key_index = jnp.arange(token_count, dtype=jnp.int32)
     offset = jnp.clip(query_index[:, None] - key_index[None, :], 0, rel_bucket.shape[0] - 1)
-    bucket = jnp.take(rel_bucket, offset)
+    bucket_ids = jnp.arange(buckets, dtype=jnp.int32)
+    bucket_start = jnp.sum((rel_bucket[None, :] < bucket_ids[:, None]).astype(jnp.int32), axis=1)
+    bucket_end = jnp.sum((rel_bucket[None, :] <= bucket_ids[:, None]).astype(jnp.int32), axis=1)
     bucket_indicator = (
-        jnp.arange(buckets, dtype=jnp.int32)[:, None, None] == bucket[None, :, :]
+        (offset[None] >= bucket_start[:, None, None]) & (offset[None] < bucket_end[:, None, None])
     ).astype(jnp.bfloat16)
     allowed = (segment[:, None] == segment[None, :]) & (query_index[:, None] >= key_index[None, :])
     return (bucket_indicator, allowed)

time: 2370 us -> 738 us (0.31)
  local copies, waits for them, and re-layouts: 1740 us -> 105 us
    gather x2 -> x0, local copies, waits for them, and re-layouts: 1630 us -> none  [block_context(): bucket = jnp.take(rel_bucket, offset)]
  transfers between devices with their start and end apart: 8 -> 8, of which waited for: 7 -> 8; matrix products, arithmetic and copies ran while one was open for 5% -> 16% of each run, Pallas kernels for 0% -> 0%
where the time goes in v1:
time: 738 us; the launch traced here: 731 us
  waiting for transfers between devices  385 us (52%)
  matrix products  107 us (14%)
  local copies, waits for them, and re-layouts  105 us (14%)
  other arithmetic  56.8 us (8%)
  blocking collectives  31.9 us (4%)
  starting transfers between devices  30.3 us (4%)
  between operations  14.9 us (2%)
    psum x1, waiting for transfers between devices, body(): lax.psum((grad_w_query, grad_w_key, grad_w_value, grad_w_output, gradient...  85.1 us
    all_to_all x1, waiting for transfers between devices, body(): lax.all_to_all(outgoing, 'dp', split_axis=0, concat_axis=1, tiled=True)  67.3 us
    all_to_all x1, waiting for transfers between devices, body(): lax.all_to_all(grad_inputs.astype(jnp.bfloat16), 'dp', split_axis=1, conc...  58.3 us
    all_to_all x1, waiting for transfers between devices, body(): lax.all_to_all(place_rows(grad_rows, routes, slot_index, experts, capacit...  54.1 us
    all_to_all x1, waiting for transfers between devices, body(): lax.all_to_all(produced.astype(jnp.bfloat16), 'dp', split_axis=1, concat_...  46.6 us
    psum x1, waiting for transfers between devices, body(): lax.psum(returned[routes, slot_index].astype(jnp.bfloat16), 'tensor')  42.8 us
    psum x1, blocking collectives, body(): lax.psum((grad_w_query, grad_w_key, grad_w_value, grad_w_output, gradient...  31.9 us
    unnamed x128, local copies, waits for them, and re-layouts  28.1 us
  transfers between devices with their start and end apart: 8, of which 8 were waited for; matrix products, arithmetic and copies ran while one was open for 16% of the time, Pallas kernels for 0%

profile of v1, /device:TPU:1, one launch (start us, length us, event | category | flops | bytes accessed | tf_op | source)
XLA Modules:
  0.0 730.9 jit_solution(12426340022251670472)
XLA Ops:
  15.2 7.6 %fusion.1 = f32[512,512,3]{0,2,1:T(4,128)S(1)} fusion(s32[512,512]{0,1:T(8,128)S(1)} %subtract_clamp_fusion, s32[32]{0:T(128)S(1)} %get-tuple-element.19, s32[32]{0:T(128)S(1)} %get-tuple-element.18, bf16[3,32]{1,0:T(4,128)(2,1)S(1)} %copy-done.58), kind=kOutput, calls=%fused_computation.7 | convolution fusion | flops 75497472 | bytes 4194752 | tf_op jit(solution)/shard_map/zd,dpv->zpv/dot_general | solution.py:64
  29.1 18.0 %reduce-window.19 = s32[64,8,128]{2,1,0:T(8,128)S(1)} reduce-window(s32[64,8,128]{2,1,0:T(8,128)S(1)} %fusion.54, s32[]{:T(128)} %constant.23.clone.1), window={size=1x1x128 pad=0_0x0_0x127_0}, to_apply=%region_11.12 | reduce-window | flops 8323072 | bytes 524292 | tf_op jit(solution)/shard_map/reduce-window.1
  50.3 23.2 %all-reduce.8.cloned.1.call-done = f32[512,768]{1,0:T(8,128)} async-done(((f32[512,768]{1,0:T(8,128)}), f32[512,768]{1,0:T(8,128)}) %all-reduce.8.cloned.1.call-update) | async-done | bytes 1572880 | tf_op jit(solution)/shard_map/psum | solution.py:139
  77.9 8.6 %gather_fusion.2 = f32[1024]{0:T(1024)S(1)} fusion(f32[512,64]{0,1:T(8,128)S(1)} %fusion.72, s32[1024]{0:T(1024)S(1)} %reshape.318), kind=kCustom, calls=%fused_computation.2 | custom fusion | bytes 16384 | tf_op jit(solution)/shard_map/jit(take_along_axis)/gather | solution.py:146
  87.1 3.8 multiply_convert_fusion.2
  91.0 3.7 reshape.332
  94.6 7.6 %scatter_custom_fusion.1 = bf16[2048,768]{1,0:T(8,128)(2,1)} fusion(s32[1024]{0:T(1024)S(1)} %reshape.324, bf16[1024,768]{1,0:T(8,128)(2,1)S(1)} %reshape.332, bf16[]{:T(256)} %constant.57.clone.1), kind=kCustom, calls=%fused_computation.59 | custom fusion | bytes 3145730
  102.2 5.2 all-to-all-start.2
  107.5 3.1 broadcast_in_dim.20
  110.5 4.7 reshape.326
  115.2 7.9 %scatter_custom_fusion = bf16[2048,768]{1,0:T(8,128)(2,1)} fusion(s32[1024]{0:T(1024)S(1)} %reshape.324, bf16[1024,768]{1,0:T(8,128)(2,1)} %reshape.326, bf16[]{:T(256)} %constant.57.clone.1), kind=kCustom, calls=%fused_computation.61 | custom fusion | bytes 3146240
  123.1 54.1 %all-to-all-done.2 = bf16[64,32,768]{2,1,0:T(8,128)(2,1)S(1)} async-done(((bf16[64,32,768]{2,1,0:T(8,128)(2,1)}), bf16[64,32,768]{2,1,0:T(8,128)(2,1)S(1)}, u32[]{:S(2)}, u32[]{:S(2)}) %all-to-all-start.2) | async-done | bytes 3145760 | tf_op jit(solution)/shard_map/all_to_all | solution.py:182
  178.8 14.7 %all-to-all-start = ((bf16[64,32,768]{2,1,0:T(8,128)(2,1)}), bf16[64,32,768]{2,1,0:T(8,128)(2,1)}, u32[]{:S(2)}, u32[]{:S(2)}) async-start(bf16[64,32,768]{2,1,0:T(8,128)(2,1)} %bitcast.122), calls=%async_computation | async-start | bytes 6291456 | tf_op jit(solution)/shard_map/all_to_all | solution.py:156
  193.5 2.2 copy.191
  195.7 67.3 %all-to-all-done = bf16[64,32,768]{2,1,0:T(8,128)(2,1)} async-done(((bf16[64,32,768]{2,1,0:T(8,128)(2,1)}), bf16[64,32,768]{2,1,0:T(8,128)(2,1)}, u32[]{:S(2)}, u32[]{:S(2)}) %all-to-all-start) | async-done | bytes 3145760 | tf_op jit(solution)/shard_map/all_to_all | solution.py:156
  263.0 2.2 copy.187
  265.2 12.6 %fusion.73 = f32[8,256,768]{2,1,0:T(8,128)} fusion(bf16[8,256,768]{2,1,0:T(8,128)(2,1)S(1)} %bitcast.117, bf16[8,768,768]{2,1,0:T(8,128)(2,1)} %param.28), kind=kOutput, calls=%fused_computation.136 | convolution fusion | flops 2415919104 | bytes 18874368 | tf_op jit(solution)/shard_map/erd,efd->erf/dot_general | solution.py:189
  277.8 12.0 %fusion.14 = (bf16[8,256,768]{2,1,0:T(8,128)(2,1)S(1)}, f32[8,256,768]{2,1,0:T(8,128)}) fusion(f32[8,256,768]{2,1,0:T(8,128)} %fusion.73, bf16[8,256,768]{2,1,0:T(8,128)(2,1)S(1)} %bitcast.119, bf16[8,768,768]{2,1,0:T(8,128)(2,1)} %param.27), kind=kOutput, calls=%fused_computation.22 | convolution fusion | flops 2447376384 | bytes 28311552 | tf_op jit(solution)/shard_map/erd,edf->erf/dot_general | solution.py:157
  289.9 11.1 %convolution_convert_fusion = bf16[8,256,768]{2,1,0:T(8,128)(2,1)S(1)} fusion(bf16[8,256,768]{2,1,0:T(8,128)(2,1)S(1)} %get-tuple-element.45, bf16[8,768,768]{2,1,0:T(8,128)(2,1)} %param.27), kind=kOutput, calls=%fused_computation.44 | convolution fusion | flops 2417491968 | bytes 15728640 | tf_op jit(solution)/shard_map/erf,edf->erd/dot_general | solution.py:199
  301.0 3.4 copy.192
  304.4 5.1 all-to-all-start.3
  309.5 8.3 %convolution_convert_fusion.1 = bf16[8,256,768]{2,1,0:T(8,128)(2,1)S(1)} fusion(bf16[8,768,768]{2,1,0:T(8,128)(2,1)} %param.28, f32[8,256,768]{2,1,0:T(8,128)} %get-tuple-element.46), kind=kOutput, calls=%fused_computation.45 | convolution fusion | flops 2431647744 | bytes 18874368 | tf_op jit(solution)/shard_map/erf,efd->erd/dot_general | solution.py:159
  317.9 3.4 copy.188
  321.3 58.3 %all-to-all-done.3 = bf16[8,256,768]{2,0,1:T(8,128)(2,1)S(1)} async-done(((bf16[8,256,768]{2,0,1:T(8,128)(2,1)}), bf16[8,256,768]{2,0,1:T(8,128)(2,1)S(1)}, u32[]{:S(2)}, u32[]{:S(2)}) %all-to-all-start.3) | async-done | bytes 3145760 | tf_op jit(solution)/shard_map/all_to_all | solution.py:202
  379.5 4.5 all-to-all-start.1
  386.1 3.6 copy.193
  389.7 14.1 %gather_fusion.1 = f32[1024,768]{1,0:T(8,128)S(1)} fusion(f32[64,32,768]{2,1,0:T(8,128)} %bitcast.115, s32[1024]{0:T(1024)S(1)} %reshape.306), kind=kCustom, calls=%fused_computation.1 | custom fusion | bytes 6299648 | tf_op jit(solution)/shard_map/gather | solution.py:205
  403.8 3.0 reshape.315
  406.9 46.6 %all-to-all-done.1 = bf16[8,256,768]{2,0,1:T(8,128)(2,1)} async-done(((bf16[8,256,768]{2,0,1:T(8,128)(2,1)}), bf16[8,256,768]{2,0,1:T(8,128)(2,1)}, u32[]{:S(2)}, u32[]{:S(2)}) %all-to-all-start.1) | async-done | bytes 3145760 | tf_op jit(solution)/shard_map/all_to_all | solution.py:160
  453.5 2.7 copy.189
  456.2 13.9 %gather_fusion = bf16[1024,768]{1,0:T(8,128)(2,1)} fusion(bf16[64,32,768]{2,1,0:T(8,128)(2,1)S(1)} %bitcast.116, s32[1024]{0:T(1024)S(1)} %reshape.306), kind=kCustom, calls=%fused_computation | custom fusion | bytes 3153920 | tf_op jit(solution)/shard_map/gather | solution.py:163
  470.1 4.5 reshape.336
  474.6 6.7 reduce_sum.179
  481.9 12.7 %fusion.59 = f32[8,768,768]{2,1,0:T(8,128)} fusion(bf16[8,256,768]{2,1,0:T(8,128)(2,1)S(1)} %bitcast.118, f32[8,256,768]{2,1,0:T(8,128)} %get-tuple-element.46), kind=kOutput, calls=%fused_computation.128 | convolution fusion | flops 2430074880 | bytes 28311552 | tf_op jit(solution)/shard_map/erf,erd->efd/dot_general | solution.py:193
  494.6 42.8 %all-reduce.14.cloned.1.call-done = (bf16[512,2,768]{2,1,0:T(2,128)(2,1)}, bf16[512,768]{1,0:T(8,128)(2,1)}) async-done(((bf16[512,2,768]{2,1,0:T(2,128)(2,1)}, bf16[512,768]{1,0:T(8,128)(2,1)}), (bf16[512,2,768]{2,1,0:T(2,128)(2,1)}, bf16[512,768]{1,0:T(8,128)(2,1)})) %all-reduce.14.cloned.1.call-update) | async-done | bytes 2359312 | tf_op jit(solution)/shard_map/psum | solution.py:163
  537.4 9.6 %fusion.16 = (f32[512,2]{1,0:T(8,128)S(1)}, f32[512,768]{1,0:T(8,128)}) fusion(bf16[512,2,768]{2,1,0:T(2,128)(2,1)} %get-tuple-element.28, f32[512,768]{1,0:T(8,128)} %copy-done.8, f32[512,2]{1,0:T(8,128)} %copy-done.15), kind=kLoop, calls=%fused_computation.33 | loop fusion | flops 3537920 | bytes 4726784 | tf_op jit(solution)/shard_map/reduce_sum | solution.py:169
  548.6 2.6 subtract_add_fusion
  561.3 2.3 fusion.76
  563.6 2.1 fusion.49
  565.7 12.6 %fusion.77 = f32[8,768,768]{2,1,0:T(8,128)} fusion(bf16[8,256,768]{2,1,0:T(8,128)(2,1)} %bitcast.120, bf16[8,256,768]{2,1,0:T(8,128)(2,1)} %copy-done.13), kind=kOutput, calls=%fused_computation.140 | convolution fusion | flops 2415919104 | bytes 25165824 | tf_op jit(solution)/shard_map/erd,erf->edf/dot_general | solution.py:196
  578.4 8.8 %fusion.45 = f32[3,32]{1,0:T(4,128)S(1)} fusion(s32[512,512]{0,1:T(8,128)S(1)} %copy-done.18, s32[32]{0:T(128)S(1)} %copy-done.56, s32[32]{0:T(128)S(1)} %copy-done.54, bf16[3,512,512]{1,2,0:T(8,128)(2,1)S(1)} %multiply_convert_fusion.1), kind=kOutput, calls=%fused_computation.83 | convolution fusion | flops 75497472 | bytes 2622080 | tf_op jit(solution)/shard_map/ruo,vuo->rv/dot_general | solution.py:247
  587.2 7.6 %all-reduce.10.cloned.1.call-done = bf16[512,768]{1,0:T(8,128)(2,1)} async-done(((bf16[512,768]{1,0:T(8,128)(2,1)}), bf16[512,768]{1,0:T(8,128)(2,1)}) %all-reduce.10.cloned.1.call-update) | async-done | bytes 786448 | tf_op jit(solution)/shard_map/psum | solution.py:268
  594.8 2.1 fusion.32
  596.9 31.9 %all-reduce = (f32[768]{0:T(1024)}, f32[3,32]{1,0:T(4,128)}, f32[768]{0:T(1024)}) all-reduce(f32[768]{0:T(1024)S(1)} %get-tuple-element.14, f32[3,32]{1,0:T(4,128)S(1)} %fusion.45, f32[768]{0:T(1024)S(1)} %get-tuple-element.12), channel_id=1, replica_groups=mesh['dp'=8,'tensor'=4] {'dp'}, use_global_device_ids=true, to_apply=%region_28.29 | all-reduce | flops 1632 | bytes 13056 | tf_op jit(solution)/shard_map/psum | solution.py:273
  628.8 3.0 fusion.23
  631.8 85.1 %all-reduce.12.cloned.1.call-done = (f32[768,192]{0,1:T(8,128)}, f32[768,192]{0,1:T(8,128)}, f32[768,192]{0,1:T(8,128)}, f32[192,768]{1,0:T(8,128)}, f32[768,64]{0,1:T(8,128)}) async-done(((f32[768,192]{0,1:T(8,128)}, f32[768,192]{0,1:T(8,128)}, f32[768,192]{0,1:T(8,128)}, f32[192,768]{1,0:T(8,128)}, f32[768,64]{0,1:T(8,128)}), (f32[768,192]{0,1:T(8,128)}, f32[768,192]{0,1:T(8,128)}, f32[768,192]{0,1:T(8,128)}, ...) | async-done | bytes 2555920 | tf_op jit(solution)/shard_map/psum | solution.py:273
  716.9 2.0 copy.224
  720.8 1.9 copy.226
  (202 shorter events, 41.0 us)
Async XLA Ops:
  7.2 19.8 %copy-start = (bf16[192,768]{1,0:T(8,128)(2,1)S(1)}, bf16[192,768]{1,0:T(8,128)(2,1)}, u32[]{:S(2)}) copy-start(bf16[192,768]{1,0:T(8,128)(2,1)} %param.23) | copy-start | bytes 884740
  7.2 6.7 copy-start.10
  7.2 6.7 copy-start.31
  7.2 7.2 copy-start.28
  7.2 66.3 %all-reduce.8.cloned.1.call-start = ((), (), s32[]{:S(2)}) async-start(), calls=%async_computation.4 | async-start | bytes 3145728 | tf_op jit(solution)/shard_map/psum | solution.py:139
  7.4 7.8 %copy-start.17 = (s32[512,512]{0,1:T(8,128)}, s32[512,512]{0,1:T(8,128)S(1)}, u32[]{:S(2)}) copy-start(s32[512,512]{0,1:T(8,128)S(1)} %subtract_clamp_fusion) | copy-start | bytes 3145732
  8.6 6.6 copy-start.53
  8.6 6.6 copy-start.55
  10.9 4.3 copy-start.58
  11.5 11.3 %copy-start.47 = (f32[512]{0:T(512)}, f32[512]{0:T(512)S(1)}, u32[]{:S(2)}) copy-start(f32[512]{0:T(512)S(1)} %get-tuple-element.40) | copy-start | bytes 6148
  12.2 10.6 %copy-start.41 = (f32[768]{0:T(1024)}, f32[768]{0:T(1024)S(1)}, u32[]{:S(2)}) copy-start(f32[768]{0:T(1024)S(1)} %convert_element_type.160) | copy-start | bytes 9220
  13.9 8.9 %copy-start.23 = (bf16[512,192]{0,1:T(8,128)(2,1)}, bf16[512,192]{0,1:T(8,128)(2,1)S(1)}, u32[]{:S(2)}) copy-start(bf16[512,192]{0,1:T(8,128)(2,1)S(1)} %convolution_convert_fusion.4) | copy-start | bytes 589828
  14.5 8.4 %copy-start.21 = (bf16[512,192]{0,1:T(8,128)(2,1)}, bf16[512,192]{0,1:T(8,128)(2,1)S(1)}, u32[]{:S(2)}) copy-start(bf16[512,192]{0,1:T(8,128)(2,1)S(1)} %convolution_convert_fusion.3) | copy-start | bytes 589828
  15.0 10.1 %copy-start.33 = (bf16[512,192]{0,1:T(8,128)(2,1)}, bf16[512,192]{0,1:T(8,128)(2,1)S(1)}, u32[]{:S(2)}) copy-start(bf16[512,192]{0,1:T(8,128)(2,1)S(1)} %convolution_convert_fusion.5) | copy-start | bytes 589828
  26.3 2.8 copy-start.51
  28.5 19.6 %copy-start.52 = (s32[2]{0:T(128)S(1)}, s32[2]{0:T(128)}, u32[]{:S(2)}) copy-start(s32[2]{0:T(128)} %constant.68) | copy-start | bytes 28
  28.5 19.7 %copy-start.57 = (s32[2]{0:T(128)S(1)}, s32[2]{0:T(128)}, u32[]{:S(2)}) copy-start(s32[2]{0:T(128)} %constant.71) | copy-start | bytes 28
  29.1 46.8 %copy-start.39 = (f32[768]{0:T(1024)}, f32[768]{0:T(1024)S(1)}, u32[]{:S(2)}) copy-start(f32[768]{0:T(1024)S(1)} %convert_element_type.172) | copy-start | bytes 9220
  50.2 36.9 %copy-start.8 = (f32[512,768]{1,0:T(8,128)}, f32[512,768]{1,0:T(8,128)S(1)}, u32[]{:S(2)}) copy-start(f32[512,768]{1,0:T(8,128)S(1)} %convert_element_type.184) | copy-start | bytes 4718596
  50.2 27.3 %copy-start.26 = (bf16[768,64]{0,1:T(8,128)(2,1)S(1)}, bf16[768,64]{0,1:T(8,128)(2,1)}, u32[]{:S(2)}) copy-start(bf16[768,64]{0,1:T(8,128)(2,1)} %param.26) | copy-start | bytes 294916
  87.1 7.5 %copy-start.15 = (f32[512,2]{1,0:T(8,128)}, f32[512,2]{1,0:T(8,128)S(1)}, u32[]{:S(2)}) copy-start(f32[512,2]{1,0:T(8,128)S(1)} %copy.176) | copy-start | bytes 12292
  102.2 74.9 %all-to-all-start.2 = ((bf16[64,32,768]{2,1,0:T(8,128)(2,1)}), bf16[64,32,768]{2,1,0:T(8,128)(2,1)S(1)}, u32[]{:S(2)}, u32[]{:S(2)}) async-start(bf16[64,32,768]{2,1,0:T(8,128)(2,1)} %bitcast.123), calls=%async_computation.2 | async-start | bytes 6291456 | tf_op jit(solution)/shard_map/all_to_all | solution.py:182
  178.8 84.2 %all-to-all-start = ((bf16[64,32,768]{2,1,0:T(8,128)(2,1)}), bf16[64,32,768]{2,1,0:T(8,128)(2,1)}, u32[]{:S(2)}, u32[]{:S(2)}) async-start(bf16[64,32,768]{2,1,0:T(8,128)(2,1)} %bitcast.122), calls=%async_computation | async-start | bytes 6291456 | tf_op jit(solution)/shard_map/all_to_all | solution.py:156
  195.7 69.5 %copy-start.3 = (bf16[8,8,32,768]{3,2,1,0:T(8,128)(2,1)}, bf16[8,8,32,768]{3,2,1,0:T(8,128)(2,1)S(1)}, u32[]{:S(2)}) copy-start(bf16[8,8,32,768]{3,2,1,0:T(8,128)(2,1)S(1)} %copy.191) | copy-start | bytes 9437188
  265.2 12.7 %copy-start.7 = (bf16[8,8,32,768]{3,2,1,0:T(8,128)(2,1)}, bf16[8,8,32,768]{3,2,1,0:T(8,128)(2,1)S(1)}, u32[]{:S(2)}) copy-start(bf16[8,8,32,768]{3,2,1,0:T(8,128)(2,1)S(1)} %copy.187) | copy-start | bytes 9437188
  289.9 11.2 %copy-start.13 = (bf16[8,256,768]{2,1,0:T(8,128)(2,1)}, bf16[8,256,768]{2,1,0:T(8,128)(2,1)S(1)}, u32[]{:S(2)}) copy-start(bf16[8,256,768]{2,1,0:T(8,128)(2,1)S(1)} %get-tuple-element.45) | copy-start | bytes 9437188
  304.4 75.1 %all-to-all-start.3 = ((bf16[8,256,768]{2,0,1:T(8,128)(2,1)}), bf16[8,256,768]{2,0,1:T(8,128)(2,1)S(1)}, u32[]{:S(2)}, u32[]{:S(2)}) async-start(bf16[8,256,768]{2,0,1:T(8,128)(2,1)} %copy.192), calls=%async_computation.3 | async-start | bytes 6291456 | tf_op jit(solution)/shard_map/all_to_all | solution.py:202
  379.5 74.0 %all-to-all-start.1 = ((bf16[8,256,768]{2,0,1:T(8,128)(2,1)}), bf16[8,256,768]{2,0,1:T(8,128)(2,1)}, u32[]{:S(2)}, u32[]{:S(2)}) async-start(bf16[8,256,768]{2,0,1:T(8,128)(2,1)} %copy.188), calls=%async_computation.1 | async-start | bytes 6291456 | tf_op jit(solution)/shard_map/all_to_all | solution.py:160
  384.1 153.3 %all-reduce.14.cloned.1.call-start = ((), (), s32[]{:S(2)}) async-start(), calls=%async_computation.7 | async-start | bytes 4718592 | tf_op jit(solution)/shard_map/psum | solution.py:163
  474.6 7.2 copy-start.38
  474.6 7.2 copy-start.46
  474.6 7.3 copy-start.4
  481.4 113.4 %all-reduce.10.cloned.1.call-start = ((), (), s32[]{:S(2)}) async-start(), calls=%async_computation.5 | async-start | bytes 1572864 | tf_op jit(solution)/shard_map/psum | solution.py:268
  494.6 52.6 %copy-start.6 = (f32[512,768]{1,0:T(8,128)S(1)}, f32[512,768]{1,0:T(8,128)}, u32[]{:S(2)}) copy-start(f32[512,768]{1,0:T(8,128)} %copy-done.5) | copy-start | bytes 4718596
  494.6 52.7 %copy-start.27 = (bf16[768,64]{0,1:T(8,128)(2,1)S(1)}, bf16[768,64]{0,1:T(8,128)(2,1)}, u32[]{:S(2)}) copy-start(bf16[768,64]{0,1:T(8,128)(2,1)} %param.26) | copy-start | bytes 294916
  494.6 52.7 %copy-start.40 = (f32[768]{0:T(1024)S(1)}, f32[768]{0:T(1024)}, u32[]{:S(2)}) copy-start(f32[768]{0:T(1024)} %copy-done.39) | copy-start | bytes 9220
  494.6 52.7 %copy-start.44 = (f32[512]{0:T(512)S(1)}, f32[512]{0:T(512)}, u32[]{:S(2)}) copy-start(f32[512]{0:T(512)} %copy-done.43) | copy-start | bytes 6148
  537.4 9.9 %copy-start.19 = (bf16[512,768]{1,0:T(8,128)(2,1)S(1)}, bf16[512,768]{1,0:T(8,128)(2,1)}, u32[]{:S(2)}) copy-start(bf16[512,768]{1,0:T(8,128)(2,1)} %get-tuple-element.29) | copy-start | bytes 2359300
  548.6 3.1 copy-start.2
  555.0 3.1 copy-start.32
  556.8 3.0 copy-start.29
  561.1 155.8 %all-reduce.12.cloned.1.call-start = ((), (), s32[]{:S(2)}) async-start(), calls=%async_computation.6 | async-start | bytes 5111808 | tf_op jit(solution)/shard_map/psum | solution.py:273
  565.7 12.6 %copy-start.18 = (s32[512,512]{0,1:T(8,128)S(1)}, s32[512,512]{0,1:T(8,128)}, u32[]{:S(2)}) copy-start(s32[512,512]{0,1:T(8,128)} %copy-done.17) | copy-start | bytes 3145732
  565.7 12.6 %copy-start.54 = (s32[32]{0:T(128)S(1)}, s32[32]{0:T(128)}, u32[]{:S(2)}) copy-start(s32[32]{0:T(128)} %copy-done.53) | copy-start | bytes 388
  565.7 12.6 %copy-start.56 = (s32[32]{0:T(128)S(1)}, s32[32]{0:T(128)}, u32[]{:S(2)}) copy-start(s32[32]{0:T(128)} %copy-done.55) | copy-start | bytes 388
  578.3 50.5 %copy-start.49 = (f32[512]{0:T(512)S(1)}, f32[512]{0:T(512)}, u32[]{:S(2)}) copy-start(f32[512]{0:T(512)} %get-tuple-element.39) | copy-start | bytes 6148
  716.9 5.8 copy-start.25
  716.9 6.6 copy-start.35
  (19 other events, 25.4 us)
Sparse Core Ops, SparseCore 0:
  28.7 44.8 all-reduce.7
  481.5 55.8 all-reduce.13
  561.2 33.5 all-reduce.9
  599.9 116.9 all-reduce.11

commit v2 on v0

v2 whole, which is shorter than its diff:
```python
import functools

import jax
import jax.numpy as jnp
from jax import lax
from jax.experimental import pallas as pl
from jax.experimental.pallas import tpu as pltpu
from jax.sharding import PartitionSpec as P

epsilon = 1e-06
masked_value = -1e30
bf16 = jnp.bfloat16
f32 = jnp.float32
VMEM = pl.BlockSpec(memory_space=pltpu.VMEM)
SMEM = pl.BlockSpec(memory_space=pltpu.SMEM)
vmem_bytes = 56 * 1024 * 1024
expert_vmem_bytes = vmem_bytes
gelu_root = 0.7978845608028654
gelu_cubic = 0.044715


def mm(left, right, left_dim=1, right_dim=0, precision=None):
    return lax.dot_general(
        left,
        right,
        (((left_dim,), (right_dim,)), ((), ())),
        preferred_element_type=f32,
        precision=precision,
    )


def gain_row(ref):
    return ref[...].astype(f32).reshape(1, ref.shape[0])


def iota(shape, dim):
    return lax.broadcasted_iota(jnp.int32, shape, dim)


def call(kernel, out_shape, operands, specs, flops, nbytes, **options):
    return pl.pallas_call(
        kernel,
        out_shape=out_shape,
        in_specs=specs,
        compiler_params=pltpu.CompilerParams(vmem_limit_bytes=vmem_bytes),
        cost_estimate=pl.CostEstimate(flops=flops, bytes_accessed=nbytes, transcendentals=0),
        **options,
    )(*operands)


def half(ref_or_width, which, width):
    return pl.ds(pl.multiple_of(which * width, 128), width)


def route_kernel(place_ref, routes_ref, cotangent_ref, placing_ref, payload_ref, *, experts, capacity):
    tokens = routes_ref.shape[1]
    groups, padded_rows, width = payload_ref.shape
    rows = experts * capacity // groups
    sent = padded_rows - 16
    core = place_ref[0]
    ids = iota((experts, tokens), 0)
    hit = ((routes_ref[0:1, :] == ids) | (routes_ref[1:2, :] == ids)).astype(f32)
    earlier = (iota((tokens, tokens), 0) < iota((tokens, tokens), 1)).astype(bf16)
    rank = mm(hit.astype(bf16), earlier)
    slot = jnp.where(hit > 0.5, rank, -1.0)
    id_sum = jnp.sum(hit * ids.astype(f32), axis=0, keepdims=True)
    id_sum = jnp.broadcast_to(id_sum, (16, tokens)).astype(bf16)
    slot_iota = iota((capacity, tokens), 0).astype(f32)
    for e in range(experts):
        placing_ref[e * capacity : (e + 1) * capacity, :] = (slot[e : e + 1, :] == slot_iota).astype(bf16)
    grad_half = cotangent_ref[:, half(None, core, width)]
    start = 0 if sent == rows else place_ref[2] * sent
    for d in range(groups):
        placed = placing_ref[pl.ds(pl.multiple_of(d * rows + start, 16), sent), :]
        payload_ref[d, 0:sent, :] = mm(placed, grad_half).astype(bf16)
        slot_ids = mm(id_sum, placed, 1, 1).astype(bf16)
        payload_ref[d, sent : sent + 16, :] = jnp.concatenate(
            [slot_ids, jnp.zeros((16, width - sent), bf16)], axis=1
        )


def bucket_rows(rel_bucket_ref, span, buckets):
    offsets = rel_bucket_ref.shape[1]
    backwards = (iota((offsets, span), 0) == span - 1 - iota((offsets, span), 1)).astype(bf16)
    table = jnp.broadcast_to(rel_bucket_ref[...].astype(f32), (16, offsets)).astype(bf16)
    reversed_bucket = mm(table, backwards)[0:1, :]
    return reversed_bucket == iota((buckets, span), 0).astype(f32)


def attention_kernel(
    lengths_ref,
    tokens_ref,
    rel_bucket_ref,
    norm1_ref,
    wq_ref,
    wk_ref,
    wv_ref,
    table_ref,
    attended_ref,
    q_ref,
    k_ref,
    v_ref,
    probs_ref,
):
    span = tokens_ref.shape[0]
    heads, buckets = table_ref.shape
    size = wq_ref.shape[0] // heads
    x = tokens_ref[...].astype(f32)
    r1 = lax.rsqrt(jnp.mean(x * x, axis=1, keepdims=True) + epsilon)
    normed = (x * r1 * gain_row(norm1_ref)).astype(bf16)
    q = mm(normed, wq_ref[...], 1, 1).astype(bf16)
    k = mm(normed, wk_ref[...], 1, 1).astype(bf16)
    v = mm(normed, wv_ref[...], 1, 1).astype(bf16)
    q_ref[...] = q
    k_ref[...] = k
    v_ref[...] = v
    query_index = iota((span, 1), 0)
    key_index = iota((1, span), 1)
    query_segment = jnp.zeros((span, 1), jnp.int32)
    key_segment = jnp.zeros((1, span), jnp.int32)
    end = jnp.int32(0)
    for j in range(lengths_ref.shape[1]):
        end = end + lengths_ref[0, j]
        query_segment = query_segment + (query_index >= end).astype(jnp.int32)
        key_segment = key_segment + (key_index >= end).astype(jnp.int32)
    allowed = (query_segment == key_segment) & (query_index >= key_index)
    indicator = bucket_rows(rel_bucket_ref, span, buckets).astype(bf16)
    bias_rows = mm(table_ref[...], indicator)
    outs = []
    for h in range(heads):
        cut = slice(h * size, (h + 1) * size)
        bias = jnp.broadcast_to(bias_rows[h : h + 1, :], (span, span))
        bias = pltpu.roll(bias, 1, 1, stride=1, stride_axis=0)
        scores = mm(q[:, cut], k[:, cut], 1, 1) * (size**-0.5) + bias
        scores = jnp.where(allowed, scores, masked_value)
        lifted = jnp.exp(scores - jnp.max(scores, axis=1, keepdims=True))
        probs = lifted / jnp.sum(lifted, axis=1, keepdims=True)
        probs_ref[h] = probs
        outs.append(mm(probs.astype(bf16), v[:, cut]))
    attended_ref[...] = jnp.concatenate(outs, axis=1).astype(bf16)


def hidden_kernel(
    core_ref,
    tokens_ref,
    a0_ref,
    a1_ref,
    a2_ref,
    a3_ref,
    w0_ref,
    w1_ref,
    w2_ref,
    w3_ref,
    norm2_ref,
    placing_ref,
    hidden_ref,
    payload_ref,
    normed_ref,
    heads_ref,
    weights_ref,
):
    groups, rows, width = payload_ref.shape
    core, far = core_ref[0], core_ref[2]
    parts = ((a0_ref, w0_ref), (a1_ref, w1_ref), (a2_ref, w2_ref), (a3_ref, w3_ref))
    for bits, (a, w) in enumerate(parts):
        index = (far ^ (bits // 2)) * 2 + (core ^ (bits % 2))
        heads_ref[index] = a[...]
        weights_ref[index] = w[...]
    hidden = tokens_ref[...].astype(f32)
    for index in range(4):
        hidden = hidden + mm(heads_ref[index], weights_ref[index])
    hidden_ref[...] = hidden
    r2 = lax.rsqrt(jnp.mean(hidden * hidden, axis=1, keepdims=True) + epsilon)
    normed_ref[...] = (hidden * r2 * gain_row(norm2_ref)).astype(bf16)
    normed_half = normed_ref[:, half(None, core_ref[0], width)]
    for d in range(groups):
        payload_ref[d] = mm(placing_ref[d * rows : (d + 1) * rows, :], normed_half).astype(bf16)


def merge_rows(ref):
    a, b, c = ref.shape
    return ref[...].reshape(a * b, c)


def cotangent_kernel(place_ref, *refs, halves, share):
    ids_refs, own_refs, oth_refs = refs[:halves], refs[halves : 2 * halves], refs[2 * halves : 3 * halves]
    w_out_ref, back_ref, rows_ref, other_ref = refs[3 * halves :]
    e = pl.program_id(0)
    blocks, capacity, width = own_refs[0].shape
    rows = blocks * capacity
    experts = other_ref.shape[2]
    core = place_ref[0]
    own = half(None, core, width)
    oth = half(None, 1 - core, width)
    ids = [r[:, 0:1, :].astype(f32) for r in ids_refs]
    g_own, g_oth = [merge_rows(r) for r in own_refs], [merge_rows(r) for r in oth_refs]
    if halves == 2:
        mine = e // share == place_ref[2]
        ids, g_own, g_oth = (jnp.where(mine, pair[0], pair[1]) for pair in (ids, g_own, g_oth))
    else:
        ids, g_own, g_oth = ids[0], g_own[0], g_oth[0]
    ids = jnp.broadcast_to(ids, (blocks, capacity, width)).reshape(rows, width)
    lane = iota((rows, width), 1)
    slot = lax.rem(iota((rows, width), 0), capacity)
    id_sum = jnp.sum(
        jnp.where(lane == lax.rem(e, share) * capacity + slot, ids, 0.0), axis=1, keepdims=True
    )
    other = id_sum.astype(jnp.int32) - (place_ref[1] + e)
    other_ref[0] = (iota((rows, experts), 1) == other).astype(bf16)
    rows_ref[0, :, own] = g_own
    rows_ref[0, :, oth] = g_oth
    back = mm(g_own, w_out_ref[0, :, own], 1, 1) + mm(g_oth, w_out_ref[0, :, oth], 1, 1)
    back_ref[0] = back.astype(bf16)


def expert_grad_kernel(
    place_ref,
    n_own_ref,
    n_oth_ref,
    back_ref,
    other_ref,
    router_ref,
    w_in_ref,
    w_out_ref,
    keep_ref,
    send_ref,
    act_ref,
    pre_ref,
    y_keep_ref,
    y_send_ref,
    grad_router_ref,
):
    blocks, capacity, width = n_own_ref.shape
    rows = blocks * capacity
    experts = router_ref.shape[0]
    units = pre_ref.shape[2]
    core = place_ref[0]
    own = half(None, core, width)
    oth = half(None, 1 - core, width)
    n_own, n_oth = merge_rows(n_own_ref), merge_rows(n_oth_ref)
    is_own = iota((rows, experts), 1) == place_ref[1] + pl.program_id(0)
    is_other = other_ref[0].astype(f32)
    logits = mm(n_own, router_ref[:, own], 1, 1) + mm(n_oth, router_ref[:, oth], 1, 1)
    logit_own = jnp.sum(jnp.where(is_own, logits, 0.0), axis=1, keepdims=True)
    logit_other = jnp.sum(is_other * logits, axis=1, keepdims=True)
    peak = jnp.maximum(logit_own, logit_other)
    up_own, up_other = jnp.exp(logit_own - peak), jnp.exp(logit_other - peak)
    gate = up_own / (up_own + up_other)
    grad_gate = jnp.zeros((rows, 1), f32)
    step = 256 if units % 256 == 0 else units
    for start in range(0, units, step):
        cut = slice(start, start + step)
        pre = mm(n_own, w_in_ref[0, own, cut]) + mm(n_oth, w_in_ref[0, oth, cut])
        square = pre * pre
        bend = jnp.tanh(pre * (gelu_root + gelu_root * gelu_cubic * square))
        rise = 0.5 + 0.5 * bend
        act = pre * rise
        slope = rise + act * (1.0 - bend) * (gelu_root + 3.0 * gelu_root * gelu_cubic * square)
        back = gate * back_ref[0, :, cut].astype(f32)
        grad_gate = grad_gate + jnp.sum(act * back, axis=1, keepdims=True)
        act_ref[0, :, cut] = (gate * act).astype(bf16)
        pre_ref[0, :, cut] = (back * slope).astype(bf16)
    grad_logit = grad_gate * (up_other / (up_own + up_other))
    coefficient = (jnp.where(is_own, grad_logit, 0.0) - is_other * grad_logit).astype(bf16)

    @pl.when((pl.program_id(0) == 0) & (pl.program_id(1) == 0))
    def _():
        grad_router_ref[...] = jnp.zeros_like(grad_router_ref)

    grad_router_ref[:, own] += mm(coefficient, n_own, 0, 0)
    grad_router_ref[:, oth] += mm(coefficient, n_oth, 0, 0)
    y_send_ref[...] = mm(act_ref[0], w_out_ref[0, :, oth]).astype(bf16).reshape(y_send_ref.shape)
    y_keep_ref[...] = mm(act_ref[0], w_out_ref[0, :, own]).astype(bf16).reshape(y_keep_ref.shape)

    def grad_in(cut):
        rows_back = mm(pre_ref[0], w_in_ref[0, cut, :], 1, 1)
        rows_back = rows_back + mm(coefficient, router_ref[:, cut])
        return rows_back.astype(bf16).reshape(blocks, capacity, width)

    send_ref[...] = grad_in(oth)
    keep_ref[...] = grad_in(own)


def expert_weight_kernel(
    place_ref, n_own_ref, n_oth_ref, g_ref, act_ref, pre_ref, grad_in_ref, grad_out_ref
):
    width = n_own_ref.shape[2]
    core = place_ref[0]
    act, grad_pre = act_ref[0], pre_ref[0]
    parts = (
        (half(None, core, width), merge_rows(n_own_ref)),
        (half(None, 1 - core, width), merge_rows(n_oth_ref)),
    )

    @pl.when(pl.program_id(1) == 0)
    def _():
        grad_out_ref[0] = mm(act, g_ref[0], 0, 0)
        for cut, n in parts:
            grad_in_ref[0, cut, :] = mm(n, grad_pre, 0, 0)

    @pl.when(pl.program_id(1) > 0)
    def _():
        grad_out_ref[0] += mm(act, g_ref[0], 0, 0)
        for cut, n in parts:
            grad_in_ref[0, cut, :] += mm(n, grad_pre, 0, 0)


def combine_kernel(place_ref, placing_ref, rows_ref, out_ref):
    groups, rows, width = rows_ref.shape
    placing = placing_ref[...].reshape(groups * rows, placing_ref.shape[3])
    out_ref[...] = mm(placing, rows_ref[...].reshape(groups * rows, width), 0, 0).astype(bf16)


def attention_back_kernel(
    core_ref,
    z0_ref,
    z1_ref,
    z2_ref,
    z3_ref,
    hidden_ref,
    cotangent_ref,
    tokens_ref,
    norm1_ref,
    norm2_ref,
    wo_ref,
    attended_ref,
    q_ref,
    k_ref,
    v_ref,
    probs_ref,
    rel_bucket_ref,
    grad_router_ref,
    grad_hidden_ref,
    weights_ref,
    low_ref,
    gn_ref,
):
    span, model = hidden_ref.shape
    heads = probs_ref.shape[0]
    size = q_ref.shape[1] // heads
    inner = q_ref.shape[1]
    width = z0_ref.shape[1]
    core = core_ref[0]
    own = half(None, core, width)
    oth = half(None, 1 - core, width)
    gn_ref[:, own] = z0_ref[...].astype(f32) + z2_ref[...].astype(f32)
    gn_ref[:, oth] = z1_ref[...].astype(f32) + z3_ref[...].astype(f32)
    grad_normed = gn_ref[...]
    hidden = hidden_ref[...]
    r2 = lax.rsqrt(jnp.mean(hidden * hidden, axis=1, keepdims=True) + epsilon)
    weighted = grad_normed * gain_row(norm2_ref)
    inner_mean = jnp.mean(hidden * weighted, axis=1, keepdims=True)
    grad_hidden = cotangent_ref[...].astype(f32) + (r2 * weighted - hidden * (r2 * r2 * r2) * inner_mean)
    grad_hidden_ref[...] = grad_hidden
    grad_norm2 = jnp.sum(grad_normed * hidden * r2, axis=0, keepdims=True)
    branch = grad_hidden.astype(bf16)
    weights_ref[3 * inner : 4 * inner, :] = mm(attended_ref[...], branch, 0, 0).astype(bf16)
    grad_attended = mm(branch, wo_ref[...], 1, 1).astype(bf16)
    indicator = bucket_rows(rel_bucket_ref, span, 128).astype(f32)
    flip = (iota((span, span), 0) + iota((span, span), 1) == span - 1).astype(bf16)
    q, k, v = q_ref[...], k_ref[...], v_ref[...]
    dq, dk, dv, diagonals = [], [], [], []
    for h in range(heads):
        cut = slice(h * size, (h + 1) * size)
        probs = probs_ref[h]
        ga = grad_attended[:, cut]
        dv.append(mm(probs.astype(bf16), ga, 0, 0))
        grad_probs = mm(ga, v[:, cut], 1, 1)
        delta = jnp.sum(probs * grad_probs, axis=1, keepdims=True)
        ds = (probs * (grad_probs - delta)).astype(bf16)
        dq.append(mm(ds, k[:, cut]) * (size**-0.5))
        dk.append(mm(ds, q[:, cut], 0, 0) * (size**-0.5))
        rolled = pltpu.roll(mm(flip, ds), 0, 1, stride=1, stride_axis=0)
        diagonals.append(jnp.sum(rolled, axis=0, keepdims=True))
    diagonals = jnp.concatenate(diagonals + [jnp.zeros((8 - heads, span), f32)], axis=0)
    bias = mm(diagonals, indicator, 1, 1, lax.Precision.HIGHEST)
    small = jnp.concatenate(
        [
            jnp.concatenate([bias, jnp.zeros((8, model - 128), f32)], axis=1),
            jnp.broadcast_to(grad_norm2, (8, model)),
        ],
        axis=0,
    )
    x = tokens_ref[...].astype(f32)
    r1 = lax.rsqrt(jnp.mean(x * x, axis=1, keepdims=True) + epsilon)
    normed = (x * r1 * gain_row(norm1_ref)).astype(bf16)
    for j, parts in enumerate((dq, dk, dv)):
        low = jnp.concatenate(parts, axis=1).astype(bf16)
        low_ref[j] = low
        weights_ref[j * inner : (j + 1) * inner, :] = mm(low, normed, 0, 0).astype(bf16)
    end = 4 * inner
    experts = grad_router_ref.shape[0]
    weights_ref[end : end + experts, :] = grad_router_ref[...].astype(bf16)
    end = end + experts
    weights_ref[end : end + 16, :] = small.astype(bf16)
    weights_ref[end + 16 :, :] = jnp.zeros((weights_ref.shape[0] - end - 16, model), bf16)


def input_back_kernel(core_ref, low_ref, wq_ref, wk_ref, wv_ref, keep_ref, send_ref, piece_ref):
    width = keep_ref.shape[1]
    core = core_ref[0]
    piece_ref[...] = (
        mm(low_ref[0], wq_ref[...])
        + mm(low_ref[1], wk_ref[...])
        + mm(low_ref[2], wv_ref[...])
    )
    keep_ref[...] = piece_ref[:, half(None, core, width)]
    send_ref[...] = piece_ref[:, half(None, 1 - core, width)].astype(bf16)


def finish_kernel(
    core_ref,
    u0_ref,
    u1_ref,
    u2_ref,
    u3_ref,
    grad_hidden_ref,
    tokens_ref,
    norm1_ref,
    out_ref,
    norm_row_ref,
    gn_ref,
):
    width = u0_ref.shape[1]
    core = core_ref[0]
    gn_ref[:, half(None, core, width)] = u0_ref[...].astype(f32) + u2_ref[...].astype(f32)
    gn_ref[:, half(None, 1 - core, width)] = u1_ref[...].astype(f32) + u3_ref[...].astype(f32)
    x = tokens_ref[...].astype(f32)
    r1 = lax.rsqrt(jnp.mean(x * x, axis=1, keepdims=True) + epsilon)
    grad_normed = gn_ref[...]
    weighted = grad_normed * gain_row(norm1_ref)
    inner_mean = jnp.mean(x * weighted, axis=1, keepdims=True)
    out_ref[...] = grad_hidden_ref[...] + (r1 * weighted - x * (r1 * r1 * r1) * inner_mean)
    row = jnp.sum(grad_normed * x * r1, axis=0, keepdims=True)
    norm_row_ref[...] = jnp.broadcast_to(row, norm_row_ref.shape).astype(bf16)


def chunk_kernel(rows_ref, norm_row_ref, out_ref):
    groups, chunk, _ = rows_ref.shape
    total = rows_ref[0].astype(f32)
    for d in range(1, groups):
        total = total + rows_ref[d].astype(f32)
    total = total.astype(bf16)
    for d in range(groups):
        out_ref[d, 0:chunk, :] = total
        out_ref[d, chunk : chunk + 16, :] = norm_row_ref[...]


def unpack_kernel(
    rows_ref, norm1_ref, wq_ref, wk_ref, wv_ref, wo_ref, bias_ref, norm2_ref, router_ref, all_ref
):
    groups, padded, _ = rows_ref.shape
    chunk = padded - 16
    inner = wo_ref.shape[0]
    experts = router_ref.shape[0]
    heads, buckets = bias_ref.shape
    norm1 = rows_ref[0, chunk : chunk + 1, :].astype(f32)
    for d in range(groups):
        all_ref[d * chunk : (d + 1) * chunk, :] = rows_ref[d, 0:chunk, :]
        if d:
            norm1 = norm1 + rows_ref[d, chunk : chunk + 1, :].astype(f32)
    norm1_ref[...] = norm1.reshape(norm1_ref.shape)
    for j, out in enumerate((wq_ref, wk_ref, wv_ref)):
        out[...] = all_ref[j * inner : (j + 1) * inner, :].astype(f32)
    wo_ref[...] = all_ref[3 * inner : 4 * inner, :].astype(f32)
    end = 4 * inner
    router_ref[...] = all_ref[end : end + experts, :].astype(f32)
    small = all_ref[end + experts : end + experts + 16, :].astype(f32)
    bias_ref[...] = small[0:heads, 0:buckets]
    norm2_ref[...] = small[8:9, :].reshape(norm2_ref.shape)


def layer_out_kernel(core_ref, y0_ref, y1_ref, y2_ref, y3_ref, hidden_ref, out_ref):
    width = y0_ref.shape[1]
    core = core_ref[0]
    own = half(None, core, width)
    oth = half(None, 1 - core, width)
    out_ref[:, own] = (
        hidden_ref[:, own] + (y0_ref[...].astype(f32) + y2_ref[...].astype(f32))
    ).astype(bf16)
    out_ref[:, oth] = (
        hidden_ref[:, oth] + (y1_ref[...].astype(f32) + y3_ref[...].astype(f32))
    ).astype(bf16)


def struct(shape, dtype):
    return jax.ShapeDtypeStruct(shape, dtype)


def body(
    groups,
    lanes,
    tokens,
    lengths,
    routes,
    rel_bucket,
    norm1,
    w_query,
    w_key,
    w_value,
    output_weight,
    position_bias_table,
    norm2,
    router,
    expert_in,
    expert_out,
    cotangent,
):
    span, model = tokens.shape
    heads, buckets = position_bias_table.shape
    inner = w_query.shape[1]
    experts = router.shape[1]
    local_experts, _, hidden_units = expert_in.shape
    capacity = 2 * routes.shape[1] * span // experts
    rows = local_experts * capacity
    width = model // 2
    rel_bucket = rel_bucket.reshape(1, -1)
    member = lax.axis_index("tensor")
    group = lax.axis_index("dp")
    place = jnp.stack([lax.rem(member, 2), group * local_experts, member // 2]).astype(jnp.int32)
    halves = 2 if local_experts % 2 == 0 else 1
    share = local_experts // halves
    sent = rows // halves

    def swap(value, bits):
        return lax.ppermute(value, "tensor", [(i, i ^ bits) for i in range(lanes)])

    def spread(value):
        far = swap(value, 2)
        return value, swap(value, 1), far, swap(far, 1)

    def exchange(value):
        return lax.all_to_all(value, "dp", split_axis=0, concat_axis=0, tiled=True)

    def add_low(left, right):
        return (left.astype(f32) + right.astype(f32)).astype(bf16)

    placing, grad_payload = call(
        functools.partial(route_kernel, experts=experts, capacity=capacity),
        (
            struct((experts * capacity, span), bf16),
            struct((groups, sent + 16, width), bf16),
        ),
        (place, routes.T, cotangent),
        [SMEM, VMEM, VMEM],
        3 * 10**9,
        6 * 10**6,
    )
    g_rows = [exchange(grad_payload)]
    if halves == 2:
        g_rows.append(swap(g_rows[0], 2))
    g_others = [swap(value, 1) for value in g_rows]
    output_weights = spread(output_weight)
    attended, q, k, v, probs = call(
        attention_kernel,
        (
            struct((span, inner), bf16),
            struct((span, inner), bf16),
            struct((span, inner), bf16),
            struct((span, inner), bf16),
            struct((heads, span, span), f32),
        ),
        (lengths, tokens, rel_bucket, norm1, w_query.T, w_key.T, w_value.T, position_bias_table),
        [SMEM] + [VMEM] * 7,
        6 * 10**9,
        8 * 10**6,
    )
    attended_all = spread(attended)
    hidden, payload = call(
        hidden_kernel,
        (struct((span, model), f32), struct((groups, rows, width), bf16)),
        (place, tokens) + attended_all + output_weights + (norm2, placing),
        [SMEM] + [VMEM] * 11,
        2 * 10**9,
        8 * 10**6,
        scratch_shapes=[
            pltpu.VMEM((span, model), bf16),
            pltpu.VMEM((4, span, inner), bf16),
            pltpu.VMEM((4, inner, model), bf16),
        ],
    )
    n_own = exchange(payload)

    blocks = min(groups, 8)
    steps = groups // blocks
    block_rows = blocks * capacity
    row_spec = pl.BlockSpec((blocks, capacity, width), lambda e, j, p: (j, e, 0))

    def half_spec(which):
        def index(e, j, p):
            first = (p[2] ^ which) * share if halves == 2 else 0
            return (j, jnp.clip(e - first, 0, share - 1), 0)

        return pl.BlockSpec((blocks, capacity, width), index)

    ids_spec = pl.BlockSpec((blocks, 16, width), lambda e, j, p: (j, sent // 16, 0))

    def kept_spec(columns):
        return pl.BlockSpec((1, block_rows, columns), lambda e, j, p: (e, j, 0))

    in_spec = pl.BlockSpec((1, model, hidden_units), lambda e, j, p: (e, 0, 0))
    out_spec = pl.BlockSpec((1, hidden_units, model), lambda e, j, p: (e, 0, 0))
    router_spec = pl.BlockSpec((experts, model), lambda e, j, p: (0, 0))
    row_struct = struct((groups, rows, width), bf16)
    unit = 2 * groups * rows * model * hidden_units

    def kept_struct(columns):
        return struct((local_experts, groups * capacity, columns), bf16)

    def expert_call(kernel, out_shape, operands, in_specs, out_specs, flops, nbytes):
        return pl.pallas_call(
            kernel,
            out_shape=out_shape,
            grid_spec=pltpu.PrefetchScalarGridSpec(
                num_scalar_prefetch=1,
                grid=(local_experts, steps),
                in_specs=in_specs,
                out_specs=out_specs,
            ),
            compiler_params=pltpu.CompilerParams(vmem_limit_bytes=expert_vmem_bytes),
            cost_estimate=pl.CostEstimate(flops=flops, bytes_accessed=nbytes, transcendentals=0),
        )(place, *operands)

    which = range(halves)
    back, g_full, other = expert_call(
        functools.partial(cotangent_kernel, halves=halves, share=share),
        (kept_struct(hidden_units), kept_struct(model), kept_struct(experts)),
        (*g_rows, *g_rows, *g_others, expert_out),
        [ids_spec] * halves + [half_spec(w) for w in which] * 2 + [out_spec],
        (kept_spec(hidden_units), kept_spec(model), kept_spec(experts)),
        unit,
        20 * 10**6,
    )
    n_own, back, g_full, other = lax.optimization_barrier((n_own, back, g_full, other))
    n_oth = swap(n_own, 1)
    if halves == 2:
        y_struct = struct((2, groups, sent, width), bf16)
        y_spec = pl.BlockSpec(
            (1, blocks, capacity, width),
            lambda e, j, p: ((e // share) ^ p[2], j, lax.rem(e, share), 0),
        )
    else:
        y_struct, y_spec = row_struct, row_spec
    keep, send, act, grad_pre, y_keep, y_send, grad_router = expert_call(
        expert_grad_kernel,
        (
            row_struct,
            row_struct,
            kept_struct(hidden_units),
            kept_struct(hidden_units),
            y_struct,
            y_struct,
            struct((experts, model), f32),
        ),
        (n_own, n_oth, back, other, router.T, expert_in, expert_out),
        [row_spec, row_spec, kept_spec(hidden_units), kept_spec(experts)]
        + [router_spec, in_spec, out_spec],
        (row_spec, row_spec, kept_spec(hidden_units), kept_spec(hidden_units))
        + (y_spec, y_spec, router_spec),
        3 * unit,
        35 * 10**6,
    )
    back_rows = add_low(keep, swap(send, 1))
    back_rows, y_send = lax.optimization_barrier((back_rows, y_send))
    back_rows = exchange(back_rows)
    y_rows = add_low(y_keep, swap(y_send, 1))
    y_far = swap(y_rows[1], 2) if halves == 2 else None
    grad_router = grad_router + swap(grad_router, 1)
    grad_router = grad_router + swap(grad_router, 2)


    def combine(value):
        count = value.shape[1]
        parted = placing.reshape(groups, rows // count, count, span)
        return pl.pallas_call(
            combine_kernel,
            out_shape=struct((span, width), bf16),
            grid_spec=pltpu.PrefetchScalarGridSpec(
                num_scalar_prefetch=1,
                grid=(1,),
                in_specs=[
                    pl.BlockSpec(
                        (groups, 1, count, span),
                        lambda i, p: (0, p[2] if count < rows else 0, 0, 0),
                    ),
                    pl.BlockSpec((groups, count, width), lambda i, p: (0, 0, 0)),
                ],
                out_specs=pl.BlockSpec((span, width), lambda i, p: (0, 0)),
            ),
            compiler_params=pltpu.CompilerParams(vmem_limit_bytes=vmem_bytes),
            cost_estimate=pl.CostEstimate(flops=10**9, bytes_accessed=4 * 10**6, transcendentals=0),
        )(place, parted, value)

    back_rows, grad_router = lax.optimization_barrier((back_rows, grad_router))
    z = combine(back_rows)
    if halves == 2:
        z, y_far = lax.optimization_barrier((z, y_far))
        y_rows = add_low(y_rows[0], y_far)
    y_rows = exchange(y_rows)
    z = spread(z)
    chunk = -(-(4 * inner + experts + 16) // (16 * groups)) * 16
    grad_hidden, weights, low = call(
        attention_back_kernel,
        (
            struct((span, model), f32),
            struct((groups * chunk, model), bf16),
            struct((3, span, inner), bf16),
        ),
        (place,)
        + z
        + (hidden, cotangent, tokens, norm1, norm2, output_weight)
        + (attended, q, k, v, probs, rel_bucket, grad_router),
        [SMEM] + [VMEM] * 17,
        10 * 10**9,
        14 * 10**6,
        scratch_shapes=[pltpu.VMEM((span, model), f32)],
    )
    weights, y_rows = lax.optimization_barrier((weights, y_rows))
    weight_rows = exchange(weights.reshape(groups, chunk, model))
    piece_keep, piece_send = call(
        input_back_kernel,
        (struct((span, width), f32), struct((span, width), bf16)),
        (place, low, w_query.T, w_key.T, w_value.T),
        [SMEM] + [VMEM] * 4,
        10**9,
        4 * 10**6,
        scratch_shapes=[pltpu.VMEM((span, model), f32)],
    )
    piece = add_low(piece_keep, swap(piece_send, 1))
    grad_tokens, norm_row = call(
        finish_kernel,
        (struct((span, model), f32), struct((16, model), bf16)),
        (place,) + spread(piece) + (grad_hidden, tokens, norm1),
        [SMEM] + [VMEM] * 7,
        10**7,
        6 * 10**6,
        scratch_shapes=[pltpu.VMEM((span, model), f32)],
    )
    grad_pre, norm_row = lax.optimization_barrier((grad_pre, norm_row))
    grad_expert_in, grad_expert_out = expert_call(
        expert_weight_kernel,
        (struct(expert_in.shape, f32), struct(expert_out.shape, f32)),
        (n_own, n_oth, g_full, act, grad_pre),
        [row_spec, row_spec, kept_spec(model), kept_spec(hidden_units), kept_spec(hidden_units)],
        (in_spec, out_spec),
        2 * unit,
        55 * 10**6,
    )
    weight_rows = exchange(
        call(
            chunk_kernel,
            struct((groups, chunk + 16, model), bf16),
            (weight_rows, norm_row),
            [VMEM] * 2,
            10**7,
            3 * 10**6,
        )
    )
    grad_norm1, grad_query, grad_key, grad_value, grad_output, grad_bias, grad_norm2, grad_router = call(
        unpack_kernel,
        (
            struct((model,), f32),
            struct((inner, model), f32),
            struct((inner, model), f32),
            struct((inner, model), f32),
            struct((inner, model), f32),
            struct((heads, buckets), f32),
            struct((model,), f32),
            struct((experts, model), f32),
        ),
        (weight_rows,),
        [VMEM],
        10**7,
        5 * 10**6,
        scratch_shapes=[pltpu.VMEM((groups * chunk, model), bf16)],
    )
    layer_out = call(
        layer_out_kernel,
        struct((span, model), bf16),
        (place,) + spread(combine(y_rows)) + (hidden,),
        [SMEM] + [VMEM] * 5,
        10**7,
        4 * 10**6,
    )
    return (
        layer_out,
        grad_tokens,
        grad_norm1,
        grad_query.T,
        grad_key.T,
        grad_value.T,
        grad_output,
        grad_bias,
        grad_norm2,
        grad_router.T,
        grad_expert_in,
        grad_expert_out,
    )


def solution(mesh):
    in_specs = (
        P("dp", None),
        P("dp", None),
        P("dp", None),
        P(),
        P(),
        P(None, "tensor"),
        P(None, "tensor"),
        P(None, "tensor"),
        P("tensor", None),
        P("tensor", None),
        P(),
        P(),
        P("dp", None, "tensor"),
        P("dp", "tensor", None),
        P("dp", None),
    )
    out_specs = (
        P("dp", None),
        P("dp", None),
        P(),
        P(None, "tensor"),
        P(None, "tensor"),
        P(None, "tensor"),
        P("tensor", None),
        P("tensor", None),
        P(),
        P(),
        P("dp", None, "tensor"),
        P("dp", "tensor", None),
    )
    return jax.shard_map(
        functools.partial(body, mesh.shape["dp"], mesh.shape["tensor"]),
        mesh=mesh,
        in_specs=in_specs,
        out_specs=out_specs,
        check_vma=False,
    )
```

time: 2370 us -> 277 us (0.12)
  local copies, waits for them, and re-layouts: 1740 us -> 11.9 us
  waiting for transfers between devices: 388 us -> 92.8 us
  matrix products: 106 us -> 0 us
  Pallas kernels: 0 us -> 106 us
  other arithmetic: 57.6 us -> 9.98 us
  blocking collectives: 31.7 us -> 0 us
  starting transfers between devices: 29.9 us -> 54.2 us
    gather x10 -> x0, local copies, waits for them, and re-layouts: 1670 us -> none  [the longest x2 1630 us: block_context(): bucket = jnp.take(rel_bucket, offset)]
    all_to_all x4 -> x6, waiting for transfers between devices: 226 us -> 16.4 us  [exchange(): return lax.all_to_all(value, 'dp', split_axis=0, concat_axis=0, tiled=True)]
    psum x4 -> x0, waiting for transfers between devices: 161 us -> none  [the longest x1 81.8 us: body(): lax.psum((grad_w_query, grad_w_key, grad_w_value, grad_w_output, gradient...]
    pallas_call x0 -> x14, Pallas kernels: none -> 106 us  [the longest x3 53.6 us: expert_call(): pl.pallas_call(kernel, out_shape=out_shape, grid_spec=pltpu.PrefetchScala...]
    dot_general x29 -> x0, matrix products: 106 us -> none  [the longest x1 12.8 us: body(): jnp.einsum('erf,erd->efd', activated, grad_arrived, preferred_element_typ...]
    ppermute x0 -> x25, waiting for transfers between devices: none -> 76.5 us  [swap(): return lax.ppermute(value, 'tensor', [(i, i ^ bits) for i in range(lanes)])]
    psum x1 -> x0, blocking collectives: 31.7 us -> none  [body(): lax.psum((grad_w_query, grad_w_key, grad_w_value, grad_w_output, gradient...]
    ppermute x0 -> x25, starting transfers between devices: none -> 24.4 us  [swap(): return lax.ppermute(value, 'tensor', [(i, i ^ bits) for i in range(lanes)])]
  transfers between devices with their start and end apart: 8 -> 31, of which waited for: 7 -> 17; matrix products, arithmetic and copies ran while one was open for 5% -> 3% of each run, Pallas kernels for 0% -> 26%
where the time goes in v2:
time: 277 us; the launch traced here: 276 us
  Pallas kernels  106 us (38%)
  waiting for transfers between devices  92.8 us (34%)
  starting transfers between devices  54.2 us (20%)
  local copies, waits for them, and re-layouts  11.9 us (4%)
  other arithmetic  9.98 us (4%)
    ppermute x25, waiting for transfers between devices, swap(): return lax.ppermute(value, 'tensor', [(i, i ^ bits) for i in range(lanes)])  76.5 us
    pallas_call x3, Pallas kernels, expert_call(): pl.pallas_call(kernel, out_shape=out_shape, grid_spec=pltpu.PrefetchScala...  53.6 us
    pallas_call x9, Pallas kernels, call(): pl.pallas_call(kernel, out_shape=out_shape, in_specs=specs, compiler_para...  44.4 us
    all_to_all x6, starting transfers between devices, exchange(): return lax.all_to_all(value, 'dp', split_axis=0, concat_axis=0, tiled=True)  29.8 us
    ppermute x25, starting transfers between devices, swap(): return lax.ppermute(value, 'tensor', [(i, i ^ bits) for i in range(lanes)])  24.4 us
    all_to_all x6, waiting for transfers between devices, exchange(): return lax.all_to_all(value, 'dp', split_axis=0, concat_axis=0, tiled=True)  16.4 us
    unnamed x62, local copies, waits for them, and re-layouts  10.3 us
    convert_element_type x4, other arithmetic, add_low(): return (left.astype(f32) + right.astype(f32)).astype(bf16)  8.69 us
  transfers between devices with their start and end apart: 31, of which 17 were waited for; matrix products, arithmetic and copies ran while one was open for 3% of the time, Pallas kernels for 26%

profile of v2, /device:TPU:1, one launch (start us, length us, event | category | flops | bytes accessed | tf_op | source)
XLA Modules:
  0.0 276.1 jit_solution(2705025399928122796)
XLA Ops:
  1.2 4.1 %shard_map.238 = (bf16[2048,512]{1,0:T(8,128)(2,1)}, bf16[8,144,384]{2,1,0:T(8,128)(2,1)}) custom-call(s32[3]{0:T(128)} %pad_add_fusion.place_ref.core_ref, s32[2,512]{1,0:T(2,128)} %bitcast.36, bf16[512,768]{1,0:T(8,128)(2,1)} %cotangent_ref.3), custom_call_target="tpu_custom_call" | custom-call | flops 3000000000 | bytes 6000000 | tf_op jit(solution)/shard_map/pallas_call | solution.py:41
  5.3 6.5 %all-to-all-start.1 = ((bf16[8,144,384]{2,1,0:T(8,128)(2,1)}), bf16[8,144,384]{2,1,0:T(8,128)(2,1)S(1)}, u32[]{:S(2)}, u32[]{:S(2)}) async-start(bf16[8,144,384]{2,1,0:T(8,128)(2,1)} %get-tuple-element.65), calls=%async_computation.1 | async-start | bytes 1769472 | tf_op jit(solution)/shard_map/all_to_all | solution.py:533
  11.8 1.3 collective-permute-start.4
  13.6 6.1 %shard_map.239 = (bf16[512,192]{1,0:T(8,128)(2,1)}, bf16[512,192]{1,0:T(8,128)(2,1)}, bf16[512,192]{1,0:T(8,128)(2,1)}, bf16[512,192]{1,0:T(8,128)(2,1)}, f32[3,512,512]{2,1,0:T(8,128)}) custom-call(s32[1,3]{1,0:T(1,128)} %lengths_ref.1, bf16[512,768]{1,0:T(8,128)(2,1)} %tokens_ref.7, s32[1,384]{1,0:T(1,128)} %reshape.40.rel_bucket_ref, ...), custom_call_target="tpu_custom_call" | custom-call | flops 6000000000 | bytes 8000000 | tf_op jit(solution)/shard_map/pallas_call | solution.py:41
  20.0 1.5 collective-permute-start.3
  22.0 4.5 %collective-permute-done.1.a2_ref = bf16[512,192]{1,0:T(8,128)(2,1)S(1)} collective-permute-done((bf16[512,192]{1,0:T(8,128)(2,1)}, bf16[512,192]{1,0:T(8,128)(2,1)S(1)}, u32[]{:S(2)}, u32[]{:S(2)}) %collective-permute-start.1) | collective-permute-done | bytes 196640 | tf_op jit(solution)/shard_map/ppermute | solution.py:526
  26.6 2.1 collective-permute-start.2
  30.7 6.8 %shard_map.240 = (f32[512,768]{1,0:T(8,128)}, bf16[8,256,384]{2,1,0:T(8,128)(2,1)}) custom-call(s32[3]{0:T(128)} %pad_add_fusion.place_ref.core_ref, bf16[512,768]{1,0:T(8,128)(2,1)} %tokens_ref.7, bf16[512,192]{1,0:T(8,128)(2,1)} %get-tuple-element.63.a0_ref.attended_ref, bf16[512,192]{1,0:T(8,128)(2,1)} %copy-done.29, bf16[512,192]{1,0:T(8,128)(2,1)} %copy-done.28, ...), custom_call_target="tpu_custom_call" | custom-call | flops 2000000000 | bytes 8000000 | tf_op jit(solution)/shard_map/pallas_call | solution.py:41
  37.5 5.4 %all-to-all-start = ((bf16[8,256,384]{2,1,0:T(8,128)(2,1)}), bf16[8,256,384]{2,1,0:T(8,128)(2,1)S(1)}, u32[]{:S(2)}, u32[]{:S(2)}) async-start(bf16[8,256,384]{2,1,0:T(8,128)(2,1)} %get-tuple-element.64), calls=%async_computation | async-start | bytes 3145728 | tf_op jit(solution)/shard_map/all_to_all | solution.py:533
  44.1 19.4 %collective-permute-done.6.refs_1_.refs_3_ = bf16[8,144,384]{2,1,0:T(8,128)(2,1)S(1)} collective-permute-done((bf16[8,144,384]{2,1,0:T(8,128)(2,1)S(1)}, bf16[8,144,384]{2,1,0:T(8,128)(2,1)S(1)}, u32[]{:S(2)}, u32[]{:S(2)}) %collective-permute-start.6) | collective-permute-done | bytes 884768 | tf_op jit(solution)/shard_map/ppermute | solution.py:526
  63.5 1.5 collective-permute-start.8
  65.0 2.0 collective-permute-done.8.refs_5_
  67.9 11.4 %shard_map.241 = (bf16[8,256,768]{2,1,0:T(8,128)(2,1)}, bf16[8,256,768]{2,1,0:T(8,128)(2,1)}, bf16[8,256,64]{2,1,0:T(8,128)(2,1)}) custom-call(s32[3]{0:T(128)} %pad_add_fusion.place_ref.core_ref, bf16[8,144,384]{2,1,0:T(8,128)(2,1)} %copy-done, bf16[8,144,384]{2,1,0:T(8,128)(2,1)} %copy-done.4, bf16[8,144,384]{2,1,0:T(8,128)(2,1)} %copy-done, ...), custom_call_target="tpu_custom_call" | custom-call | flops 2415919104 | bytes 20000000 | tf_op jit(solution)/shard_map/pallas_call | solution.py:611
  79.4 1.4 collective-permute-start.9
  80.9 3.0 %collective-permute-done.9.n_oth_ref = bf16[8,256,384]{2,1,0:T(8,128)(2,1)S(1)} collective-permute-done((bf16[8,256,384]{2,1,0:T(8,128)(2,1)S(1)}, bf16[8,256,384]{2,1,0:T(8,128)(2,1)S(1)}, u32[]{:S(2)}, u32[]{:S(2)}) %collective-permute-start.9) | collective-permute-done | bytes 1572896 | tf_op jit(solution)/shard_map/ppermute | solution.py:526
  85.0 24.0 %shard_map.242 = (bf16[8,256,384]{2,1,0:T(8,128)(2,1)}, bf16[8,256,384]{2,1,0:T(8,128)(2,1)}, bf16[8,256,768]{2,1,0:T(8,128)(2,1)}, bf16[8,256,768]{2,1,0:T(8,12...) custom-call(s32[3]{0:T(128)} %pad_add_fusion.place_ref.core_ref, ...), custom_call_target="tpu_custom_call" | custom-call | flops 7247757312 | bytes 35000000 | tf_op jit(solution)/shard_map/pallas_call | solution.py:611
  109.5 3.2 %collective-permute-done.10 = bf16[8,256,384]{2,1,0:T(8,128)(2,1)S(1)} collective-permute-done((bf16[8,256,384]{2,1,0:T(8,128)(2,1)}, bf16[8,256,384]{2,1,0:T(8,128)(2,1)S(1)}, u32[]{:S(2)}, u32[]{:S(2)}) %collective-permute-start.10) | collective-permute-done | bytes 1572896 | tf_op jit(solution)/shard_map/ppermute | solution.py:526
  112.8 2.9 %add_convert_fusion.1 = bf16[8,256,384]{2,1,0:T(8,128)(2,1)} fusion(bf16[8,256,384]{2,1,0:T(8,128)(2,1)S(1)} %collective-permute-done.10, bf16[8,256,384]{2,1,0:T(8,128)(2,1)} %get-tuple-element.72), kind=kLoop, calls=%fused_computation.1 | loop fusion | flops 3145728 | bytes 4718592 | tf_op jit(solution)/shard_map/convert_element_type | solution.py:536
  116.1 4.4 %all-to-all-start.2 = ((bf16[8,256,384]{2,1,0:T(8,128)(2,1)}), bf16[8,256,384]{2,1,0:T(8,128)(2,1)S(1)}, u32[]{:S(2)}, u32[]{:S(2)}) async-start(bf16[8,256,384]{2,1,0:T(8,128)(2,1)} %add_convert_fusion.1), calls=%async_computation.2 | async-start | bytes 3145728 | tf_op jit(solution)/shard_map/all_to_all | solution.py:533
  121.6 2.3 add_convert_fusion
  127.0 1.3 collective-permute-start.12
  128.3 19.7 %collective-permute-done.12 = f32[64,768]{1,0:T(8,128)S(1)} collective-permute-done((f32[64,768]{1,0:T(8,128)S(1)}, f32[64,768]{1,0:T(8,128)S(1)}, u32[]{:S(2)}, u32[]{:S(2)}) %collective-permute-start.12) | collective-permute-done | bytes 196640 | tf_op jit(solution)/shard_map/ppermute | solution.py:526
  148.7 8.4 %all-to-all-done.2.rows_ref = bf16[8,256,384]{2,1,0:T(8,128)(2,1)S(1)} async-done(((bf16[8,256,384]{2,1,0:T(8,128)(2,1)}), bf16[8,256,384]{2,1,0:T(8,128)(2,1)S(1)}, u32[]{:S(2)}, u32[]{:S(2)}) %all-to-all-start.2) | async-done | bytes 1572896 | tf_op jit(solution)/shard_map/all_to_all | solution.py:533
  158.2 4.7 %shard_map.243.z0_ref = bf16[512,384]{1,0:T(8,128)(2,1)} custom-call(s32[3]{0:T(128)} %pad_add_fusion.place_ref.core_ref, bf16[8,1,256,512]{3,2,1,0:T(8,128)(2,1)} %bitcast.22, bf16[8,256,384]{2,1,0:T(8,128)(2,1)} %copy-done.2), custom_call_target="tpu_custom_call" | custom-call | flops 1000000000 | bytes 4000000 | tf_op jit(solution)/shard_map/pallas_call | solution.py:675
  163.2 2.2 fusion
  165.4 4.2 %all-to-all-start.3 = ((bf16[8,128,384]{2,1,0:T(8,128)(2,1)}), bf16[8,128,384]{2,1,0:T(8,128)(2,1)S(1)}, u32[]{:S(2)}, u32[]{:S(2)}) async-start(bf16[8,128,384]{2,1,0:T(8,128)(2,1)} %fusion), calls=%async_computation.3 | async-start | bytes 1572864 | tf_op jit(solution)/shard_map/all_to_all | solution.py:533
  170.7 1.7 collective-permute-done.16.z2_ref
  172.5 2.2 collective-permute-start.17
  174.7 1.3 collective-permute-done.17.z3_ref
  176.8 11.3 %shard_map.244 = (f32[512,768]{1,0:T(8,128)}, bf16[896,768]{1,0:T(8,128)(2,1)}, bf16[3,512,192]{2,1,0:T(8,128)(2,1)}) custom-call(s32[3]{0:T(128)} %pad_add_fusion.place_ref.core_ref, bf16[512,384]{1,0:T(8,128)(2,1)} %shard_map.243.z0_ref, bf16[512,384]{1,0:T(8,128)(2,1)} %copy-done.22, bf16[512,384]{1,0:T(8,128)(2,1)} %copy-done.21, ...), custom_call_target="tpu_custom_call" | custom-call | flops 10000000000 | bytes 14000000 | tf_op jit(solution)/shard_map/pallas_call | solution.py:41
  188.7 4.9 %all-to-all-start.4 = ((bf16[8,112,768]{2,1,0:T(8,128)(2,1)}), bf16[8,112,768]{2,1,0:T(8,128)(2,1)S(1)}, u32[]{:S(2)}, u32[]{:S(2)}) async-start(bf16[8,112,768]{2,1,0:T(8,128)(2,1)} %bitcast.24), calls=%async_computation.4 | async-start | bytes 2752512 | tf_op jit(solution)/shard_map/all_to_all | solution.py:533
  193.5 3.2 %shard_map.247 = (f32[512,384]{1,0:T(8,128)}, bf16[512,384]{1,0:T(8,128)(2,1)}) custom-call(s32[3]{0:T(128)} %pad_add_fusion.place_ref.core_ref, bf16[3,512,192]{2,1,0:T(8,128)(2,1)} %get-tuple-element.90.low_ref, bf16[192,768]{1,0:T(8,128)(2,1)} %bitcast.29, bf16[192,768]{1,0:T(8,128)(2,1)} %bitcast.31, bf16[192,768]{1,0:T(8,128)(2,1)} %bitcast.33), custom_call_target="tpu_custom_call" | custom-call | flops 1000000000 | bytes 4000000 | tf_op jit(solution)/shard_map/pallas_call | solution.py:41
  197.6 1.6 collective-permute-done.21
  199.2 1.2 add_convert_fusion.2.u0_ref
  200.4 1.3 collective-permute-start.23
  202.3 8.5 %collective-permute-done.23.u2_ref = bf16[512,384]{1,0:T(8,128)(2,1)S(1)} collective-permute-done((bf16[512,384]{1,0:T(8,128)(2,1)S(1)}, bf16[512,384]{1,0:T(8,128)(2,1)S(1)}, u32[]{:S(2)}, u32[]{:S(2)}) %collective-permute-start.23) | collective-permute-done | bytes 393248 | tf_op jit(solution)/shard_map/ppermute | solution.py:526
  212.0 1.3 collective-permute-done.24.u3_ref
  214.1 4.2 %shard_map.248 = (f32[512,768]{1,0:T(8,128)}, bf16[16,768]{1,0:T(8,128)(2,1)}) custom-call(s32[3]{0:T(128)} %pad_add_fusion.place_ref.core_ref, bf16[512,384]{1,0:T(8,128)(2,1)} %copy-done.7, bf16[512,384]{1,0:T(8,128)(2,1)} %copy-done.16, bf16[512,384]{1,0:T(8,128)(2,1)} %copy-done.15, bf16[512,384]{1,0:T(8,128)(2,1)} %copy-done.17, ...), custom_call_target="tpu_custom_call" | custom-call | flops 10000000 | bytes 6000000 | tf_op jit(solution)/shard_map/pallas_call | solution.py:41
  218.3 7.4 %all-to-all-done.4.rows_ref = bf16[8,112,768]{2,1,0:T(8,128)(2,1)S(1)} async-done(((bf16[8,112,768]{2,1,0:T(8,128)(2,1)}), bf16[8,112,768]{2,1,0:T(8,128)(2,1)S(1)}, u32[]{:S(2)}, u32[]{:S(2)}) %all-to-all-start.4) | async-done | bytes 1376288 | tf_op jit(solution)/shard_map/all_to_all | solution.py:533
  226.8 2.7 shard_map.249
  229.4 4.5 %all-to-all-start.5 = ((bf16[8,128,768]{2,1,0:T(8,128)(2,1)}), bf16[8,128,768]{2,1,0:T(8,128)(2,1)S(1)}, u32[]{:S(2)}, u32[]{:S(2)}) async-start(bf16[8,128,768]{2,1,0:T(8,128)(2,1)} %shard_map.249), calls=%async_computation.5 | async-start | bytes 3145728 | tf_op jit(solution)/shard_map/all_to_all | solution.py:533
  233.9 3.6 %shard_map.245.y0_ref = bf16[512,384]{1,0:T(8,128)(2,1)} custom-call(s32[3]{0:T(128)} %pad_add_fusion.place_ref.core_ref, bf16[8,2,128,512]{3,2,1,0:T(8,128)(2,1)} %bitcast.23, bf16[8,128,384]{2,1,0:T(8,128)(2,1)} %copy-done.10), custom_call_target="tpu_custom_call" | custom-call | flops 1000000000 | bytes 4000000 | tf_op jit(solution)/shard_map/pallas_call | solution.py:675
  237.5 1.2 collective-permute-start.19
  239.8 7.8 %collective-permute-done.19.y2_ref = bf16[512,384]{1,0:T(8,128)(2,1)S(1)} collective-permute-done((bf16[512,384]{1,0:T(8,128)(2,1)}, bf16[512,384]{1,0:T(8,128)(2,1)S(1)}, u32[]{:S(2)}, u32[]{:S(2)}) %collective-permute-start.19) | collective-permute-done | bytes 393248 | tf_op jit(solution)/shard_map/ppermute | solution.py:526
  247.6 1.7 collective-permute-start.20
  249.3 18.2 %shard_map.251 = (f32[8,768,768]{2,1,0:T(8,128)}, f32[8,768,768]{2,1,0:T(8,128)}) custom-call(s32[3]{0:T(128)} %pad_add_fusion.place_ref.core_ref, bf16[8,256,384]{2,1,0:T(8,128)(2,1)} %copy-done.5, bf16[8,256,384]{2,1,0:T(8,128)(2,1)} %copy-done.20, bf16[8,256,768]{2,1,0:T(8,128)(2,1)} %get-tuple-element.107.g_ref, ...), custom_call_target="tpu_custom_call" | custom-call | flops 4831838208 | bytes 55000000 | tf_op jit(solution)/shard_map/pallas_call | solution.py:611
  268.9 3.0 %shard_map.246 = bf16[512,768]{1,0:T(8,128)(2,1)} custom-call(s32[3]{0:T(128)} %pad_add_fusion.place_ref.core_ref, bf16[512,384]{1,0:T(8,128)(2,1)} %shard_map.245.y0_ref, bf16[512,384]{1,0:T(8,128)(2,1)} %copy-done.13, bf16[512,384]{1,0:T(8,128)(2,1)} %copy-done.12, bf16[512,384]{1,0:T(8,128)(2,1)} %copy-done.14, f32[512,768]{1,0:T(8,128)} %get-tuple-element.81.hidden_ref), custom_call_target="tpu_custom_call" | custom-call | flops 10000000 | bytes 4000000 | tf_op jit(solution)/shard_map/pallas_call | solution.py:41
  273.2 2.9 %shard_map.250 = (f32[768]{0:T(1024)}, f32[192,768]{1,0:T(8,128)}, f32[192,768]{1,0:T(8,128)}, f32[192,768]{1,0:T(8,128)}, f32[192,768]{1,0:T(8,128)}, /*index=5...) custom-call(bf16[8,128,768]{2,1,0:T(8,128)(2,1)} %copy-done.1), custom_call_target="tpu_custom_call" | custom-call | flops 10000000 | bytes 5000000 | tf_op jit(solution)/shard_map/pallas_call | solution.py:41
  (99 shorter events, 24.8 us)
Async XLA Ops:
  5.3 6.5 %copy-start.24 = (bf16[192,768]{1,0:T(8,128)(2,1)S(1)}, bf16[192,768]{1,0:T(8,128)(2,1)}, u32[]{:S(2)}) copy-start(bf16[192,768]{1,0:T(8,128)(2,1)} %wo_ref.1) | copy-start | bytes 884740
  5.3 7.8 %copy-start.19 = (s32[384]{0:T(512)S(1)}, s32[384]{0:T(512)}, u32[]{:S(2)}) copy-start(s32[384]{0:T(512)} %param.18) | copy-start | bytes 4612
  5.3 32.2 %all-to-all-start.1 = ((bf16[8,144,384]{2,1,0:T(8,128)(2,1)}), bf16[8,144,384]{2,1,0:T(8,128)(2,1)S(1)}, u32[]{:S(2)}, u32[]{:S(2)}) async-start(bf16[8,144,384]{2,1,0:T(8,128)(2,1)} %get-tuple-element.65), calls=%async_computation.1 | async-start | bytes 1769472 | tf_op jit(solution)/shard_map/all_to_all | solution.py:533
  11.8 9.7 %collective-permute-start.4 = (bf16[192,768]{1,0:T(8,128)(2,1)S(1)}, bf16[192,768]{1,0:T(8,128)(2,1)S(1)}, u32[]{:S(2)}, u32[]{:S(2)}) collective-permute-start(bf16[192,768]{1,0:T(8,128)(2,1)S(1)} %copy-done.24), channel_id=1, source_target_pairs={{0,2},{1,3},{2,0},{3,1},{4,6},{5,7},{6,4},{7,5},{8,10},{9,11},{10,... | collective-permute-start | bytes 884744 | tf_op jit(solution)/shard_map/ppermute | solution.py:526
  19.8 6.8 %collective-permute-start.1 = (bf16[512,192]{1,0:T(8,128)(2,1)}, bf16[512,192]{1,0:T(8,128)(2,1)S(1)}, u32[]{:S(2)}, u32[]{:S(2)}) collective-permute-start(bf16[512,192]{1,0:T(8,128)(2,1)} %get-tuple-element.63.a0_ref.attended_ref), channel_id=1, source_target_pairs={{0,2},{1,3},{2,0},{3,1},{4,6},{5,7},{6,4},{7,5},{8,10},{9,11},{10,... | collective-permute-start | bytes 589832 | tf_op jit(solution)/shard_map/ppermute | solution.py:526
  20.0 8.7 %collective-permute-start.3 = (bf16[192,768]{1,0:T(8,128)(2,1)S(1)}, bf16[192,768]{1,0:T(8,128)(2,1)S(1)}, u32[]{:S(2)}, u32[]{:S(2)}) collective-permute-start(bf16[192,768]{1,0:T(8,128)(2,1)S(1)} %copy-done.24), channel_id=1, source_target_pairs={{0,1},{1,0},{2,3},{3,2},{4,5},{5,4},{6,7},{7,6},{8,9},{9,8},{10,11... | collective-permute-start | bytes 884744 | tf_op jit(solution)/shard_map/ppermute | solution.py:526
  21.5 8.4 %copy-start.25 = (bf16[192,768]{1,0:T(8,128)(2,1)}, bf16[192,768]{1,0:T(8,128)(2,1)S(1)}, u32[]{:S(2)}) copy-start(bf16[192,768]{1,0:T(8,128)(2,1)S(1)} %collective-permute-done.4.w2_ref) | copy-start | bytes 884740
  21.5 8.4 %collective-permute-start.5 = (bf16[192,768]{1,0:T(8,128)(2,1)S(1)}, bf16[192,768]{1,0:T(8,128)(2,1)S(1)}, u32[]{:S(2)}, u32[]{:S(2)}) collective-permute-start(bf16[192,768]{1,0:T(8,128)(2,1)S(1)} %collective-permute-done.4.w2_ref), channel_id=1, source_target_pairs={{0,1},{1,0},{2,3},{3,2},{4,5},{5,4},{6,7},{7,6},{8,9},{9,8},{10,11... | collective-permute-start | bytes 884744 | tf_op jit(solution)/shard_map/ppermute | solution.py:526
  21.6 7.1 %collective-permute-start = (bf16[512,192]{1,0:T(8,128)(2,1)}, bf16[512,192]{1,0:T(8,128)(2,1)S(1)}, u32[]{:S(2)}, u32[]{:S(2)}) collective-permute-start(bf16[512,192]{1,0:T(8,128)(2,1)} %get-tuple-element.63.a0_ref.attended_ref), channel_id=1, source_target_pairs={{0,1},{1,0},{2,3},{3,2},{4,5},{5,4},{6,7},{7,6},{8,9},{9,8},{10,11... | collective-permute-start | bytes 589832 | tf_op jit(solution)/shard_map/ppermute | solution.py:526
  26.6 3.3 %copy-start.28 = (bf16[512,192]{1,0:T(8,128)(2,1)}, bf16[512,192]{1,0:T(8,128)(2,1)S(1)}, u32[]{:S(2)}) copy-start(bf16[512,192]{1,0:T(8,128)(2,1)S(1)} %collective-permute-done.1.a2_ref) | copy-start | bytes 589828
  26.6 3.3 %collective-permute-start.2 = (bf16[512,192]{1,0:T(8,128)(2,1)S(1)}, bf16[512,192]{1,0:T(8,128)(2,1)S(1)}, u32[]{:S(2)}, u32[]{:S(2)}) collective-permute-start(bf16[512,192]{1,0:T(8,128)(2,1)S(1)} %collective-permute-done.1.a2_ref), channel_id=1, source_target_pairs={{0,1},{1,0},{2,3},{3,2},{4,5},{5,4},{6,7},{7,6},{8,9},{9,8},{10,11... | collective-permute-start | bytes 589832 | tf_op jit(solution)/shard_map/ppermute | solution.py:526
  37.5 5.6 %copy-start = (bf16[8,144,384]{2,1,0:T(8,128)(2,1)}, bf16[8,144,384]{2,1,0:T(8,128)(2,1)S(1)}, u32[]{:S(2)}) copy-start(bf16[8,144,384]{2,1,0:T(8,128)(2,1)S(1)} %all-to-all-done.1.refs_0_.refs_2_) | copy-start | bytes 2654212
  37.5 41.9 %all-to-all-start = ((bf16[8,256,384]{2,1,0:T(8,128)(2,1)}), bf16[8,256,384]{2,1,0:T(8,128)(2,1)S(1)}, u32[]{:S(2)}, u32[]{:S(2)}) async-start(bf16[8,256,384]{2,1,0:T(8,128)(2,1)} %get-tuple-element.64), calls=%async_computation | async-start | bytes 3145728 | tf_op jit(solution)/shard_map/all_to_all | solution.py:533
  42.9 20.6 %collective-permute-start.6 = (bf16[8,144,384]{2,1,0:T(8,128)(2,1)S(1)}, bf16[8,144,384]{2,1,0:T(8,128)(2,1)S(1)}, u32[]{:S(2)}, u32[]{:S(2)}) collective-permute-start(bf16[8,144,384]{2,1,0:T(8,128)(2,1)S(1)} %all-to-all-done.1.refs_0_.refs_2_), channel_id=1, source_target_pairs={{0,2},{1,3},{2,0},{3,1},{4,6},{5,7},{6,4},{7,5},{8,10},{9,11},{10,... | collective-permute-start | bytes 2654216 | tf_op jit(solution)/shard_map/ppermute | solution.py:526
  43.2 21.8 %collective-permute-start.7 = (bf16[8,144,384]{2,1,0:T(8,128)(2,1)S(1)}, bf16[8,144,384]{2,1,0:T(8,128)(2,1)S(1)}, u32[]{:S(2)}, u32[]{:S(2)}) collective-permute-start(bf16[8,144,384]{2,1,0:T(8,128)(2,1)S(1)} %all-to-all-done.1.refs_0_.refs_2_), channel_id=1, source_target_pairs={{0,1},{1,0},{2,3},{3,2},{4,5},{5,4},{6,7},{7,6},{8,9},{9,8},{10,11... | collective-permute-start | bytes 2654216 | tf_op jit(solution)/shard_map/ppermute | solution.py:526
  63.5 3.6 %copy-start.4 = (bf16[8,144,384]{2,1,0:T(8,128)(2,1)}, bf16[8,144,384]{2,1,0:T(8,128)(2,1)S(1)}, u32[]{:S(2)}) copy-start(bf16[8,144,384]{2,1,0:T(8,128)(2,1)S(1)} %collective-permute-done.6.refs_1_.refs_3_) | copy-start | bytes 2654212
  63.5 3.6 %collective-permute-start.8 = (bf16[8,144,384]{2,1,0:T(8,128)(2,1)S(1)}, bf16[8,144,384]{2,1,0:T(8,128)(2,1)S(1)}, u32[]{:S(2)}, u32[]{:S(2)}) collective-permute-start(bf16[8,144,384]{2,1,0:T(8,128)(2,1)S(1)} %collective-permute-done.6.refs_1_.refs_3_), channel_id=1, source_target_pairs={{0,1},{1,0},{2,3},{3,2},{4,5},{5,4},{6,7},{7,6},{8,9},{9,8},{10,11... | collective-permute-start | bytes 2654216 | tf_op jit(solution)/shard_map/ppermute | solution.py:526
  65.0 2.1 copy-start.8
  79.4 4.5 %copy-start.5 = (bf16[8,256,384]{2,1,0:T(8,128)(2,1)}, bf16[8,256,384]{2,1,0:T(8,128)(2,1)S(1)}, u32[]{:S(2)}) copy-start(bf16[8,256,384]{2,1,0:T(8,128)(2,1)S(1)} %all-to-all-done.n_own_ref) | copy-start | bytes 4718596
  79.4 4.5 %collective-permute-start.9 = (bf16[8,256,384]{2,1,0:T(8,128)(2,1)S(1)}, bf16[8,256,384]{2,1,0:T(8,128)(2,1)S(1)}, u32[]{:S(2)}, u32[]{:S(2)}) collective-permute-start(bf16[8,256,384]{2,1,0:T(8,128)(2,1)S(1)} %all-to-all-done.n_own_ref), channel_id=1, source_target_pairs={{0,1},{1,0},{2,3},{3,2},{4,5},{5,4},{6,7},{7,6},{8,9},{9,8},{10,11... | collective-permute-start | bytes 4718600 | tf_op jit(solution)/shard_map/ppermute | solution.py:526
  109.1 3.7 %collective-permute-start.10 = (bf16[8,256,384]{2,1,0:T(8,128)(2,1)}, bf16[8,256,384]{2,1,0:T(8,128)(2,1)S(1)}, u32[]{:S(2)}, u32[]{:S(2)}) collective-permute-start(bf16[8,256,384]{2,1,0:T(8,128)(2,1)} %get-tuple-element.73), channel_id=1, source_target_pairs={{0,1},{1,0},{2,3},{3,2},{4,5},{5,4},{6,7},{7,6},{8,9},{9,8},{10,11... | collective-permute-start | bytes 4718600 | tf_op jit(solution)/shard_map/ppermute | solution.py:526
  115.7 4.8 %collective-permute-start.13 = (bf16[2,8,128,384]{3,2,1,0:T(8,128)(2,1)}, bf16[2,8,128,384]{3,2,1,0:T(8,128)(2,1)S(1)}, u32[]{:S(2)}, u32[]{:S(2)}) collective-permute-start(bf16[2,8,128,384]{3,2,1,0:T(8,128)(2,1)} %get-tuple-element.79), channel_id=1, source_target_pairs={{0,1},{1,0},{2,3},{3,2},{4,5},{5,4},{6,7},{7,6},{8,9},{9,8},{10,11... | collective-permute-start | bytes 4718600 | tf_op jit(solution)/shard_map/ppermute | solution.py:526
  116.1 41.0 %all-to-all-start.2 = ((bf16[8,256,384]{2,1,0:T(8,128)(2,1)}), bf16[8,256,384]{2,1,0:T(8,128)(2,1)S(1)}, u32[]{:S(2)}, u32[]{:S(2)}) async-start(bf16[8,256,384]{2,1,0:T(8,128)(2,1)} %add_convert_fusion.1), calls=%async_computation.2 | async-start | bytes 3145728 | tf_op jit(solution)/shard_map/all_to_all | solution.py:533
  124.0 1.2 copy-start.18
  124.9 38.0 %collective-permute-start.14 = (bf16[8,128,384]{2,1,0:T(8,128)(2,1)}, bf16[8,128,384]{2,1,0:T(8,128)(2,1)}, u32[]{:S(2)}, u32[]{:S(2)}) collective-permute-start(bf16[8,128,384]{2,1,0:T(8,128)(2,1)} %slice_bitcast_fusion.1), channel_id=1, source_target_pairs={{0,2},{1,3},{2,0},{3,1},{4,6},{5,7},{6,4},{7,5},{8,10},{9,11},{10,... | collective-permute-start | bytes 2359304 | tf_op jit(solution)/shard_map/ppermute | solution.py:526
  125.2 1.8 collective-permute-start.11
  127.0 21.0 %collective-permute-start.12 = (f32[64,768]{1,0:T(8,128)S(1)}, f32[64,768]{1,0:T(8,128)S(1)}, u32[]{:S(2)}, u32[]{:S(2)}) collective-permute-start(f32[64,768]{1,0:T(8,128)S(1)} %add.20), channel_id=1, source_target_pairs={{0,2},{1,3},{2,0},{3,1},{4,6},{5,7},{6,4},{7,5},{8,10},{9,11},{10,... | collective-permute-start | bytes 589832 | tf_op jit(solution)/shard_map/ppermute | solution.py:526
  163.0 6.7 %copy-start.11 = (bf16[512,384]{1,0:T(8,128)(2,1)S(1)}, bf16[512,384]{1,0:T(8,128)(2,1)}, u32[]{:S(2)}) copy-start(bf16[512,384]{1,0:T(8,128)(2,1)} %shard_map.243.z0_ref) | copy-start | bytes 1179652
  163.0 9.5 %collective-permute-start.16 = (bf16[512,384]{1,0:T(8,128)(2,1)}, bf16[512,384]{1,0:T(8,128)(2,1)S(1)}, u32[]{:S(2)}, u32[]{:S(2)}) collective-permute-start(bf16[512,384]{1,0:T(8,128)(2,1)} %shard_map.243.z0_ref), channel_id=1, source_target_pairs={{0,2},{1,3},{2,0},{3,1},{4,6},{5,7},{6,4},{7,5},{8,10},{9,11},{10,... | collective-permute-start | bytes 1179656 | tf_op jit(solution)/shard_map/ppermute | solution.py:526
  165.4 23.2 %all-to-all-start.3 = ((bf16[8,128,384]{2,1,0:T(8,128)(2,1)}), bf16[8,128,384]{2,1,0:T(8,128)(2,1)S(1)}, u32[]{:S(2)}, u32[]{:S(2)}) async-start(bf16[8,128,384]{2,1,0:T(8,128)(2,1)} %fusion), calls=%async_computation.3 | async-start | bytes 1572864 | tf_op jit(solution)/shard_map/all_to_all | solution.py:533
  169.6 5.1 %collective-permute-start.15 = (bf16[512,384]{1,0:T(8,128)(2,1)S(1)}, bf16[512,384]{1,0:T(8,128)(2,1)S(1)}, u32[]{:S(2)}, u32[]{:S(2)}) collective-permute-start(bf16[512,384]{1,0:T(8,128)(2,1)S(1)} %copy-done.11), channel_id=1, source_target_pairs={{0,1},{1,0},{2,3},{3,2},{4,5},{5,4},{6,7},{7,6},{8,9},{9,8},{10,11... | collective-permute-start | bytes 1179656 | tf_op jit(solution)/shard_map/ppermute | solution.py:526
  172.5 3.6 %copy-start.21 = (bf16[512,384]{1,0:T(8,128)(2,1)}, bf16[512,384]{1,0:T(8,128)(2,1)S(1)}, u32[]{:S(2)}) copy-start(bf16[512,384]{1,0:T(8,128)(2,1)S(1)} %collective-permute-done.16.z2_ref) | copy-start | bytes 1179652
  172.5 3.6 %collective-permute-start.17 = (bf16[512,384]{1,0:T(8,128)(2,1)S(1)}, bf16[512,384]{1,0:T(8,128)(2,1)S(1)}, u32[]{:S(2)}, u32[]{:S(2)}) collective-permute-start(bf16[512,384]{1,0:T(8,128)(2,1)S(1)} %collective-permute-done.16.z2_ref), channel_id=1, source_target_pairs={{0,1},{1,0},{2,3},{3,2},{4,5},{5,4},{6,7},{7,6},{8,9},{9,8},{10,11... | collective-permute-start | bytes 1179656 | tf_op jit(solution)/shard_map/ppermute | solution.py:526
  174.7 1.4 copy-start.22
  188.7 8.1 %copy-start.10 = (bf16[8,128,384]{2,1,0:T(8,128)(2,1)}, bf16[8,128,384]{2,1,0:T(8,128)(2,1)S(1)}, u32[]{:S(2)}) copy-start(bf16[8,128,384]{2,1,0:T(8,128)(2,1)S(1)} %all-to-all-done.3.rows_ref) | copy-start | bytes 2359300
  188.7 37.0 %all-to-all-start.4 = ((bf16[8,112,768]{2,1,0:T(8,128)(2,1)}), bf16[8,112,768]{2,1,0:T(8,128)(2,1)S(1)}, u32[]{:S(2)}, u32[]{:S(2)}) async-start(bf16[8,112,768]{2,1,0:T(8,128)(2,1)} %bitcast.24), calls=%async_computation.4 | async-start | bytes 2752512 | tf_op jit(solution)/shard_map/all_to_all | solution.py:533
  196.8 2.4 collective-permute-start.21
  200.4 13.0 %copy-start.7 = (bf16[512,384]{1,0:T(8,128)(2,1)}, bf16[512,384]{1,0:T(8,128)(2,1)S(1)}, u32[]{:S(2)}) copy-start(bf16[512,384]{1,0:T(8,128)(2,1)S(1)} %add_convert_fusion.2.u0_ref) | copy-start | bytes 1179652
  200.4 10.4 %collective-permute-start.23 = (bf16[512,384]{1,0:T(8,128)(2,1)S(1)}, bf16[512,384]{1,0:T(8,128)(2,1)S(1)}, u32[]{:S(2)}, u32[]{:S(2)}) collective-permute-start(bf16[512,384]{1,0:T(8,128)(2,1)S(1)} %add_convert_fusion.2.u0_ref), channel_id=1, source_target_pairs={{0,2},{1,3},{2,0},{3,1},{4,6},{5,7},{6,4},{7,5},{8,10},{9,11},{10,... | collective-permute-start | bytes 1179656 | tf_op jit(solution)/shard_map/ppermute | solution.py:526
  201.7 10.3 %collective-permute-start.22 = (bf16[512,384]{1,0:T(8,128)(2,1)S(1)}, bf16[512,384]{1,0:T(8,128)(2,1)S(1)}, u32[]{:S(2)}, u32[]{:S(2)}) collective-permute-start(bf16[512,384]{1,0:T(8,128)(2,1)S(1)} %add_convert_fusion.2.u0_ref), channel_id=1, source_target_pairs={{0,1},{1,0},{2,3},{3,2},{4,5},{5,4},{6,7},{7,6},{8,9},{9,8},{10,11... | collective-permute-start | bytes 1179656 | tf_op jit(solution)/shard_map/ppermute | solution.py:526
  210.8 2.6 copy-start.15
  210.8 2.6 collective-permute-start.24
  212.0 1.4 copy-start.16
  229.4 42.5 %all-to-all-start.5 = ((bf16[8,128,768]{2,1,0:T(8,128)(2,1)}), bf16[8,128,768]{2,1,0:T(8,128)(2,1)S(1)}, u32[]{:S(2)}, u32[]{:S(2)}) async-start(bf16[8,128,768]{2,1,0:T(8,128)(2,1)} %shard_map.249), calls=%async_computation.5 | async-start | bytes 3145728 | tf_op jit(solution)/shard_map/all_to_all | solution.py:533
  237.5 10.1 %collective-permute-start.19 = (bf16[512,384]{1,0:T(8,128)(2,1)}, bf16[512,384]{1,0:T(8,128)(2,1)S(1)}, u32[]{:S(2)}, u32[]{:S(2)}) collective-permute-start(bf16[512,384]{1,0:T(8,128)(2,1)} %shard_map.245.y0_ref), channel_id=1, source_target_pairs={{0,2},{1,3},{2,0},{3,1},{4,6},{5,7},{6,4},{7,5},{8,10},{9,11},{10,... | collective-permute-start | bytes 1179656 | tf_op jit(solution)/shard_map/ppermute | solution.py:526
  238.7 28.7 %collective-permute-start.18 = (bf16[512,384]{1,0:T(8,128)(2,1)}, bf16[512,384]{1,0:T(8,128)(2,1)S(1)}, u32[]{:S(2)}, u32[]{:S(2)}) collective-permute-start(bf16[512,384]{1,0:T(8,128)(2,1)} %shard_map.245.y0_ref), channel_id=1, source_target_pairs={{0,1},{1,0},{2,3},{3,2},{4,5},{5,4},{6,7},{7,6},{8,9},{9,8},{10,11... | collective-permute-start | bytes 1179656 | tf_op jit(solution)/shard_map/ppermute | solution.py:526
  247.6 19.8 %copy-start.12 = (bf16[512,384]{1,0:T(8,128)(2,1)}, bf16[512,384]{1,0:T(8,128)(2,1)S(1)}, u32[]{:S(2)}) copy-start(bf16[512,384]{1,0:T(8,128)(2,1)S(1)} %collective-permute-done.19.y2_ref) | copy-start | bytes 1179652
  247.6 19.9 %collective-permute-start.20 = (bf16[512,384]{1,0:T(8,128)(2,1)S(1)}, bf16[512,384]{1,0:T(8,128)(2,1)S(1)}, u32[]{:S(2)}, u32[]{:S(2)}) collective-permute-start(bf16[512,384]{1,0:T(8,128)(2,1)S(1)} %collective-permute-done.19.y2_ref), channel_id=1, source_target_pairs={{0,1},{1,0},{2,3},{3,2},{4,5},{5,4},{6,7},{7,6},{8,9},{9,8},{10,11... | collective-permute-start | bytes 1179656 | tf_op jit(solution)/shard_map/ppermute | solution.py:526
  (14 other events, 13.4 us)

commit v3 on v2

--- a/solution.py
+++ b/solution.py
@@ -135,8 +135,9 @@
         scores = jnp.where(allowed, scores, masked_value)
         lifted = jnp.exp(scores - jnp.max(scores, axis=1, keepdims=True))
         probs = lifted / jnp.sum(lifted, axis=1, keepdims=True)
+        probs = probs.astype(bf16)
         probs_ref[h] = probs
-        outs.append(mm(probs.astype(bf16), v[:, cut]))
+        outs.append(mm(probs, v[:, cut]))
     attended_ref[...] = jnp.concatenate(outs, axis=1).astype(bf16)
 
 
@@ -154,12 +155,11 @@
     norm2_ref,
     placing_ref,
     hidden_ref,
-    payload_ref,
-    normed_ref,
-    heads_ref,
-    weights_ref,
+    *refs,
 ):
-    groups, rows, width = payload_ref.shape
+    normed_ref, heads_ref, weights_ref = refs[-3:]
+    payload_refs = refs[:-3]
+    groups, rows, width = payload_refs[0].shape
     core, far = core_ref[0], core_ref[2]
     parts = ((a0_ref, w0_ref), (a1_ref, w1_ref), (a2_ref, w2_ref), (a3_ref, w3_ref))
     for bits, (a, w) in enumerate(parts):
@@ -173,8 +173,11 @@
     r2 = lax.rsqrt(jnp.mean(hidden * hidden, axis=1, keepdims=True) + epsilon)
     normed_ref[...] = (hidden * r2 * gain_row(norm2_ref)).astype(bf16)
     normed_half = normed_ref[:, half(None, core_ref[0], width)]
+    parts = len(payload_refs)
     for d in range(groups):
-        payload_ref[d] = mm(placing_ref[d * rows : (d + 1) * rows, :], normed_half).astype(bf16)
+        for part, payload_ref in enumerate(payload_refs):
+            start = pl.multiple_of((d * parts + (core_ref[3] ^ part)) * rows, 16)
+            payload_ref[d] = mm(placing_ref[pl.ds(start, rows), :], normed_half).astype(bf16)
 
 
 def merge_rows(ref):
@@ -182,35 +185,36 @@
     return ref[...].reshape(a * b, c)
 
 
-def cotangent_kernel(place_ref, *refs, halves, share):
-    ids_refs, own_refs, oth_refs = refs[:halves], refs[halves : 2 * halves], refs[2 * halves : 3 * halves]
-    w_out_ref, back_ref, rows_ref, other_ref = refs[3 * halves :]
+def whole_rows(even, own, oth):
+    return jnp.concatenate([jnp.where(even, own, oth), jnp.where(even, oth, own)], axis=1)
+
+
+def part_rows(low, rows):
+    width = rows.shape[1] // 2
+    return jnp.where(low, rows[:, :width], rows[:, width:])
+
+
+def first_expert(place_ref, part, share):
+    return place_ref[1] + (place_ref[3] ^ part) * share
+
+
+def cotangent_kernel(
+    place_ref, ids_ref, own_ref, oth_ref, w_out_ref, back_ref, rows_ref, other_ref, *, part, share
+):
     e = pl.program_id(0)
-    blocks, capacity, width = own_refs[0].shape
+    blocks, capacity, width = own_ref.shape
     rows = blocks * capacity
     experts = other_ref.shape[2]
-    core = place_ref[0]
-    own = half(None, core, width)
-    oth = half(None, 1 - core, width)
-    ids = [r[:, 0:1, :].astype(f32) for r in ids_refs]
-    g_own, g_oth = [merge_rows(r) for r in own_refs], [merge_rows(r) for r in oth_refs]
-    if halves == 2:
-        mine = e // share == place_ref[2]
-        ids, g_own, g_oth = (jnp.where(mine, pair[0], pair[1]) for pair in (ids, g_own, g_oth))
-    else:
-        ids, g_own, g_oth = ids[0], g_own[0], g_oth[0]
+    ids = ids_ref[:, 0:1, :].astype(f32)
     ids = jnp.broadcast_to(ids, (blocks, capacity, width)).reshape(rows, width)
     lane = iota((rows, width), 1)
     slot = lax.rem(iota((rows, width), 0), capacity)
-    id_sum = jnp.sum(
-        jnp.where(lane == lax.rem(e, share) * capacity + slot, ids, 0.0), axis=1, keepdims=True
-    )
-    other = id_sum.astype(jnp.int32) - (place_ref[1] + e)
+    id_sum = jnp.sum(jnp.where(lane == e * capacity + slot, ids, 0.0), axis=1, keepdims=True)
+    other = id_sum.astype(jnp.int32) - (first_expert(place_ref, part, share) + e)
     other_ref[0] = (iota((rows, experts), 1) == other).astype(bf16)
-    rows_ref[0, :, own] = g_own
-    rows_ref[0, :, oth] = g_oth
-    back = mm(g_own, w_out_ref[0, :, own], 1, 1) + mm(g_oth, w_out_ref[0, :, oth], 1, 1)
-    back_ref[0] = back.astype(bf16)
+    g = whole_rows(place_ref[0] == 0, merge_rows(own_ref), merge_rows(oth_ref))
+    rows_ref[0] = g
+    back_ref[0] = mm(g, w_out_ref[0], 1, 1).astype(bf16)
 
 
 def expert_grad_kernel(
@@ -228,87 +232,103 @@
     pre_ref,
     y_keep_ref,
     y_send_ref,
-    grad_router_ref,
+    coefficient_ref,
+    *,
+    part,
+    share,
 ):
-    blocks, capacity, width = n_own_ref.shape
-    rows = blocks * capacity
+    per, rows, units = pre_ref.shape
+    blocks, _, width = n_own_ref.shape
+    capacity = rows // blocks
     experts = router_ref.shape[0]
-    units = pre_ref.shape[2]
     core = place_ref[0]
-    own = half(None, core, width)
-    oth = half(None, 1 - core, width)
-    n_own, n_oth = merge_rows(n_own_ref), merge_rows(n_oth_ref)
-    is_own = iota((rows, experts), 1) == place_ref[1] + pl.program_id(0)
-    is_other = other_ref[0].astype(f32)
-    logits = mm(n_own, router_ref[:, own], 1, 1) + mm(n_oth, router_ref[:, oth], 1, 1)
-    logit_own = jnp.sum(jnp.where(is_own, logits, 0.0), axis=1, keepdims=True)
-    logit_other = jnp.sum(is_other * logits, axis=1, keepdims=True)
-    peak = jnp.maximum(logit_own, logit_other)
-    up_own, up_other = jnp.exp(logit_own - peak), jnp.exp(logit_other - peak)
-    gate = up_own / (up_own + up_other)
-    grad_gate = jnp.zeros((rows, 1), f32)
-    step = 256 if units % 256 == 0 else units
-    for start in range(0, units, step):
-        cut = slice(start, start + step)
-        pre = mm(n_own, w_in_ref[0, own, cut]) + mm(n_oth, w_in_ref[0, oth, cut])
-        square = pre * pre
-        bend = jnp.tanh(pre * (gelu_root + gelu_root * gelu_cubic * square))
-        rise = 0.5 + 0.5 * bend
-        act = pre * rise
-        slope = rise + act * (1.0 - bend) * (gelu_root + 3.0 * gelu_root * gelu_cubic * square)
-        back = gate * back_ref[0, :, cut].astype(f32)
-        grad_gate = grad_gate + jnp.sum(act * back, axis=1, keepdims=True)
-        act_ref[0, :, cut] = (gate * act).astype(bf16)
-        pre_ref[0, :, cut] = (back * slope).astype(bf16)
-    grad_logit = grad_gate * (up_other / (up_own + up_other))
-    coefficient = (jnp.where(is_own, grad_logit, 0.0) - is_other * grad_logit).astype(bf16)
-
-    @pl.when((pl.program_id(0) == 0) & (pl.program_id(1) == 0))
-    def _():
-        grad_router_ref[...] = jnp.zeros_like(grad_router_ref)
-
-    grad_router_ref[:, own] += mm(coefficient, n_own, 0, 0)
-    grad_router_ref[:, oth] += mm(coefficient, n_oth, 0, 0)
-    y_send_ref[...] = mm(act_ref[0], w_out_ref[0, :, oth]).astype(bf16).reshape(y_send_ref.shape)
-    y_keep_ref[...] = mm(act_ref[0], w_out_ref[0, :, own]).astype(bf16).reshape(y_keep_ref.shape)
-
-    def grad_in(cut):
-        rows_back = mm(pre_ref[0], w_in_ref[0, cut, :], 1, 1)
-        rows_back = rows_back + mm(coefficient, router_ref[:, cut])
-        return rows_back.astype(bf16).reshape(blocks, capacity, width)
-
-    send_ref[...] = grad_in(oth)
-    keep_ref[...] = grad_in(own)
-
-
-def expert_weight_kernel(
-    place_ref, n_own_ref, n_oth_ref, g_ref, act_ref, pre_ref, grad_in_ref, grad_out_ref
-):
-    width = n_own_ref.shape[2]
+    even = core == 0
+    first = first_expert(place_ref, part, share) + pl.program_id(0) * per
+    for i in range(per):
+        slots = slice(i * capacity, (i + 1) * capacity)
+        n = whole_rows(
+            even, n_own_ref[:, slots, :].reshape(rows, width), n_oth_ref[:, slots, :].reshape(rows, width)
+        )
+        is_own = iota((rows, experts), 1) == first + i
+        is_other = other_ref[i].astype(f32)
+        logits = mm(n, router_ref[...], 1, 1)
+        logit_own = jnp.sum(jnp.where(is_own, logits, 0.0), axis=1, keepdims=True)
+        logit_other = jnp.sum(is_other * logits, axis=1, keepdims=True)
+        peak = jnp.maximum(logit_own, logit_other)
+        up_own, up_other = jnp.exp(logit_own - peak), jnp.exp(logit_other - peak)
+        gate = up_own / (up_own + up_other)
+        grad_gate = jnp.zeros((rows, 1), f32)
+        step = 256 if units % 256 == 0 else units
+        for start in range(0, units, step):
+            cut = slice(start, start + step)
+            pre = mm(n, w_in_ref[i, :, cut])
+            square = pre * pre
+            bend = jnp.tanh(pre * (gelu_root + gelu_root * gelu_cubic * square))
+            rise = 0.5 + 0.5 * bend
+            act = pre * rise
+            slope = rise + act * (1.0 - bend) * (gelu_root + 3.0 * gelu_root * gelu_cubic * square)
+            back = gate * back_ref[i, :, cut].astype(f32)
+            grad_gate = grad_gate + jnp.sum(act * back, axis=1, keepdims=True)
+            act_ref[i, :, cut] = (gate * act).astype(bf16)
+            pre_ref[i, :, cut] = (back * slope).astype(bf16)
+        grad_logit = grad_gate * (up_other / (up_own + up_other))
+        coefficient = (jnp.where(is_own, grad_logit, 0.0) - is_other * grad_logit).astype(bf16)
+        coefficient_ref[i] = coefficient
+        rows_back = (mm(pre_ref[i], w_in_ref[i], 1, 1) + mm(coefficient, router_ref[...])).astype(bf16)
+        y = mm(act_ref[i], w_out_ref[i]).astype(bf16)
+        for take, grad_ref, y_ref in ((core == 1, send_ref, y_send_ref), (even, keep_ref, y_keep_ref)):
+            grad_ref[:, slots, :] = part_rows(take, rows_back).reshape(blocks, capacity, width)
+            y_ref[:, slots, :] = part_rows(take, y).reshape(blocks, capacity, width)
+
+
+def router_kernel(place_ref, *refs):
+    out_ref = refs[-1]
+    parts = (len(refs) - 1) // 3
     core = place_ref[0]
-    act, grad_pre = act_ref[0], pre_ref[0]
-    parts = (
-        (half(None, core, width), merge_rows(n_own_ref)),
-        (half(None, 1 - core, width), merge_rows(n_oth_ref)),
-    )
-
-    @pl.when(pl.program_id(1) == 0)
-    def _():
-        grad_out_ref[0] = mm(act, g_ref[0], 0, 0)
-        for cut, n in parts:
-            grad_in_ref[0, cut, :] = mm(n, grad_pre, 0, 0)
-
-    @pl.when(pl.program_id(1) > 0)
-    def _():
-        grad_out_ref[0] += mm(act, g_ref[0], 0, 0)
-        for cut, n in parts:
-            grad_in_ref[0, cut, :] += mm(n, grad_pre, 0, 0)
-
-
-def combine_kernel(place_ref, placing_ref, rows_ref, out_ref):
+    totals = [None, None]
+    for part in range(parts):
+        n_refs, coefficient_ref = refs[3 * part : 3 * part + 2], refs[3 * part + 2]
+        local_experts, rows, _ = coefficient_ref.shape
+        groups, _, width = n_refs[0].shape
+        capacity = rows // groups
+        for which in range(2):
+            for i in range(local_experts):
+                n = n_refs[which][:, i * capacity : (i + 1) * capacity, :].reshape(rows, width)
+                term = mm(coefficient_ref[i], n, 0, 0)
+                totals[which] = term if totals[which] is None else totals[which] + term
+    out_ref[:, half(None, core, width)] = totals[0]
+    out_ref[:, half(None, 1 - core, width)] = totals[1]
+
+
+def expert_weight_kernel(place_ref, *refs, share):
+    grad_in_ref, grad_out_ref = refs[-2:]
+    e, j = pl.program_id(0), pl.program_id(1)
+
+    def add(n_own_ref, n_oth_ref, act_ref, pre_ref, g_ref):
+        n = whole_rows(place_ref[0] == 0, merge_rows(n_own_ref), merge_rows(n_oth_ref))
+
+        @pl.when(j == 0)
+        def _():
+            grad_out_ref[0] = mm(act_ref[0], g_ref[0], 0, 0)
+            grad_in_ref[0] = mm(n, pre_ref[0], 0, 0)
+
+        @pl.when(j > 0)
+        def _():
+            grad_out_ref[0] += mm(act_ref[0], g_ref[0], 0, 0)
+            grad_in_ref[0] += mm(n, pre_ref[0], 0, 0)
+
+    for part in range((len(refs) - 2) // 5):
+        pl.when(e // share == part)(functools.partial(add, *refs[5 * part : 5 * part + 5]))
+
+
+def combine_kernel(place_ref, placing_ref, rows_ref, *refs):
+    out_ref = refs[-1]
     groups, rows, width = rows_ref.shape
     placing = placing_ref[...].reshape(groups * rows, placing_ref.shape[3])
-    out_ref[...] = mm(placing, rows_ref[...].reshape(groups * rows, width), 0, 0).astype(bf16)
+    total = mm(placing, rows_ref[...].reshape(groups * rows, width), 0, 0)
+    if len(refs) == 2:
+        total = total + refs[0][...]
+    out_ref[...] = total.astype(out_ref.dtype)
 
 
 def attention_back_kernel(
@@ -334,6 +354,7 @@
     weights_ref,
     low_ref,
     gn_ref,
+    all_ref,
 ):
     span, model = hidden_ref.shape
     heads = probs_ref.shape[0]
@@ -354,7 +375,7 @@
     grad_hidden_ref[...] = grad_hidden
     grad_norm2 = jnp.sum(grad_normed * hidden * r2, axis=0, keepdims=True)
     branch = grad_hidden.astype(bf16)
-    weights_ref[3 * inner : 4 * inner, :] = mm(attended_ref[...], branch, 0, 0).astype(bf16)
+    all_ref[3 * inner : 4 * inner, :] = mm(attended_ref[...], branch, 0, 0)
     grad_attended = mm(branch, wo_ref[...], 1, 1).astype(bf16)
     indicator = bucket_rows(rel_bucket_ref, span, 128).astype(f32)
     flip = (iota((span, span), 0) + iota((span, span), 1) == span - 1).astype(bf16)
@@ -362,9 +383,9 @@
     dq, dk, dv, diagonals = [], [], [], []
     for h in range(heads):
         cut = slice(h * size, (h + 1) * size)
-        probs = probs_ref[h]
         ga = grad_attended[:, cut]
-        dv.append(mm(probs.astype(bf16), ga, 0, 0))
+        dv.append(mm(probs_ref[h], ga, 0, 0))
+        probs = probs_ref[h].astype(f32)
         grad_probs = mm(ga, v[:, cut], 1, 1)
         delta = jnp.sum(probs * grad_probs, axis=1, keepdims=True)
         ds = (probs * (grad_probs - delta)).astype(bf16)
@@ -374,26 +395,25 @@
         diagonals.append(jnp.sum(rolled, axis=0, keepdims=True))
     diagonals = jnp.concatenate(diagonals + [jnp.zeros((8 - heads, span), f32)], axis=0)
     bias = mm(diagonals, indicator, 1, 1, lax.Precision.HIGHEST)
-    small = jnp.concatenate(
-        [
-            jnp.concatenate([bias, jnp.zeros((8, model - 128), f32)], axis=1),
-            jnp.broadcast_to(grad_norm2, (8, model)),
-        ],
-        axis=0,
-    )
+    bias = jnp.concatenate([bias, jnp.zeros((8, model - 128), f32)], axis=1)
+    small = jnp.where(iota((8, model), 0) == 7, grad_norm2, bias).astype(bf16)
     x = tokens_ref[...].astype(f32)
     r1 = lax.rsqrt(jnp.mean(x * x, axis=1, keepdims=True) + epsilon)
     normed = (x * r1 * gain_row(norm1_ref)).astype(bf16)
     for j, parts in enumerate((dq, dk, dv)):
         low = jnp.concatenate(parts, axis=1).astype(bf16)
         low_ref[j] = low
-        weights_ref[j * inner : (j + 1) * inner, :] = mm(low, normed, 0, 0).astype(bf16)
-    end = 4 * inner
-    experts = grad_router_ref.shape[0]
-    weights_ref[end : end + experts, :] = grad_router_ref[...].astype(bf16)
-    end = end + experts
-    weights_ref[end : end + 16, :] = small.astype(bf16)
-    weights_ref[end + 16 :, :] = jnp.zeros((weights_ref.shape[0] - end - 16, model), bf16)
+        all_ref[j * inner : (j + 1) * inner, :] = mm(low, normed, 0, 0)
+    groups, chunk, _ = weights_ref.shape
+    count = 4 * inner // groups
+    share = grad_router_ref.shape[0] // groups
+    weights_ref[:, chunk - 16 :, :] = jnp.zeros((groups, 16, model), bf16)
+    for d in range(groups):
+        weights_ref[d, 0:count, :] = all_ref[d * count : (d + 1) * count, :].astype(bf16)
+        tail = grad_router_ref[d * share : (d + 1) * share, :].astype(bf16)
+        weights_ref[d, chunk - 16 : chunk - 16 + share, :] = tail
+        if d < 8:
+            weights_ref[d, chunk - 8 : chunk - 7, :] = small[d : d + 1, :]
 
 
 def input_back_kernel(core_ref, low_ref, wq_ref, wk_ref, wv_ref, keep_ref, send_ref, piece_ref):
@@ -436,38 +456,38 @@
 
 
 def chunk_kernel(rows_ref, norm_row_ref, out_ref):
-    groups, chunk, _ = rows_ref.shape
+    groups, chunk, model = rows_ref.shape
     total = rows_ref[0].astype(f32)
     for d in range(1, groups):
         total = total + rows_ref[d].astype(f32)
-    total = total.astype(bf16)
+    norm_row = norm_row_ref[...].astype(f32)[0:1, :]
+    total = jnp.where(iota((chunk, model), 0) == chunk - 1, norm_row, total).astype(bf16)
     for d in range(groups):
-        out_ref[d, 0:chunk, :] = total
-        out_ref[d, chunk : chunk + 16, :] = norm_row_ref[...]
+        out_ref[d] = total
 
 
 def unpack_kernel(
     rows_ref, norm1_ref, wq_ref, wk_ref, wv_ref, wo_ref, bias_ref, norm2_ref, router_ref, all_ref
 ):
-    groups, padded, _ = rows_ref.shape
-    chunk = padded - 16
+    groups, chunk, _ = rows_ref.shape
     inner = wo_ref.shape[0]
     experts = router_ref.shape[0]
     heads, buckets = bias_ref.shape
-    norm1 = rows_ref[0, chunk : chunk + 1, :].astype(f32)
+    count = 4 * inner // groups
+    share = experts // groups
+    norm1 = None
     for d in range(groups):
-        all_ref[d * chunk : (d + 1) * chunk, :] = rows_ref[d, 0:chunk, :]
-        if d:
-            norm1 = norm1 + rows_ref[d, chunk : chunk + 1, :].astype(f32)
+        all_ref[d * count : (d + 1) * count, :] = rows_ref[d, 0:count, :].astype(f32)
+        tail = rows_ref[d, chunk - 16 : chunk, :].astype(f32)
+        router_ref[d * share : (d + 1) * share, :] = tail[0:share, :]
+        if d < heads:
+            bias_ref[d : d + 1, :] = tail[8:9, 0:buckets]
+        if d == 7:
+            norm2_ref[...] = tail[8:9, :].reshape(norm2_ref.shape)
+        norm1 = tail[15:16, :] if norm1 is None else norm1 + tail[15:16, :]
     norm1_ref[...] = norm1.reshape(norm1_ref.shape)
-    for j, out in enumerate((wq_ref, wk_ref, wv_ref)):
-        out[...] = all_ref[j * inner : (j + 1) * inner, :].astype(f32)
-    wo_ref[...] = all_ref[3 * inner : 4 * inner, :].astype(f32)
-    end = 4 * inner
-    router_ref[...] = all_ref[end : end + experts, :].astype(f32)
-    small = all_ref[end + experts : end + experts + 16, :].astype(f32)
-    bias_ref[...] = small[0:heads, 0:buckets]
-    norm2_ref[...] = small[8:9, :].reshape(norm2_ref.shape)
+    for j, out in enumerate((wq_ref, wk_ref, wv_ref, wo_ref)):
+        out[...] = all_ref[j * inner : (j + 1) * inner, :]
 
 
 def layer_out_kernel(core_ref, y0_ref, y1_ref, y2_ref, y3_ref, hidden_ref, out_ref):
@@ -517,8 +537,10 @@
     rel_bucket = rel_bucket.reshape(1, -1)
     member = lax.axis_index("tensor")
     group = lax.axis_index("dp")
-    place = jnp.stack([lax.rem(member, 2), group * local_experts, member // 2]).astype(jnp.int32)
     halves = 2 if local_experts % 2 == 0 else 1
+    far = member // 2
+    place = jnp.stack([lax.rem(member, 2), group * local_experts, far, far * (halves - 1)])
+    place = place.astype(jnp.int32)
     share = local_experts // halves
     sent = rows // halves
 
@@ -547,9 +569,6 @@
         6 * 10**6,
     )
     g_rows = [exchange(grad_payload)]
-    if halves == 2:
-        g_rows.append(swap(g_rows[0], 2))
-    g_others = [swap(value, 1) for value in g_rows]
     output_weights = spread(output_weight)
     attended, q, k, v, probs = call(
         attention_kernel,
@@ -558,7 +577,7 @@
             struct((span, inner), bf16),
             struct((span, inner), bf16),
             struct((span, inner), bf16),
-            struct((heads, span, span), f32),
+            struct((heads, span, span), bf16),
         ),
         (lengths, tokens, rel_bucket, norm1, w_query.T, w_key.T, w_value.T, position_bias_table),
         [SMEM] + [VMEM] * 7,
@@ -566,9 +585,9 @@
         8 * 10**6,
     )
     attended_all = spread(attended)
-    hidden, payload = call(
+    hidden, *payloads = call(
         hidden_kernel,
-        (struct((span, model), f32), struct((groups, rows, width), bf16)),
+        (struct((span, model), f32),) + (struct((groups, sent, width), bf16),) * halves,
         (place, tokens) + attended_all + output_weights + (norm2, placing),
         [SMEM] + [VMEM] * 11,
         2 * 10**9,
@@ -579,41 +598,36 @@
             pltpu.VMEM((4, inner, model), bf16),
         ],
     )
-    n_own = exchange(payload)
+    payloads[0], g_rows[0] = lax.optimization_barrier((payloads[0], g_rows[0]))
+    if halves == 2:
+        g_rows.append(swap(g_rows[0], 2))
+    n_owns = [exchange(payloads[0])]
 
     blocks = min(groups, 8)
     steps = groups // blocks
     block_rows = blocks * capacity
     row_spec = pl.BlockSpec((blocks, capacity, width), lambda e, j, p: (j, e, 0))
 
-    def half_spec(which):
-        def index(e, j, p):
-            first = (p[2] ^ which) * share if halves == 2 else 0
-            return (j, jnp.clip(e - first, 0, share - 1), 0)
-
-        return pl.BlockSpec((blocks, capacity, width), index)
-
     ids_spec = pl.BlockSpec((blocks, 16, width), lambda e, j, p: (j, sent // 16, 0))
 
     def kept_spec(columns):
         return pl.BlockSpec((1, block_rows, columns), lambda e, j, p: (e, j, 0))
 
-    in_spec = pl.BlockSpec((1, model, hidden_units), lambda e, j, p: (e, 0, 0))
-    out_spec = pl.BlockSpec((1, hidden_units, model), lambda e, j, p: (e, 0, 0))
+    def ordered(e, p):
+        return (p[3] ^ (e // share)) * share + lax.rem(e, share)
+
+    in_spec = pl.BlockSpec((1, model, hidden_units), lambda e, j, p: (ordered(e, p), 0, 0))
+    out_spec = pl.BlockSpec((1, hidden_units, model), lambda e, j, p: (ordered(e, p), 0, 0))
     router_spec = pl.BlockSpec((experts, model), lambda e, j, p: (0, 0))
-    row_struct = struct((groups, rows, width), bf16)
     unit = 2 * groups * rows * model * hidden_units
 
-    def kept_struct(columns):
-        return struct((local_experts, groups * capacity, columns), bf16)
-
-    def expert_call(kernel, out_shape, operands, in_specs, out_specs, flops, nbytes):
+    def expert_call(kernel, out_shape, operands, in_specs, out_specs, flops, nbytes, grid=None):
         return pl.pallas_call(
             kernel,
             out_shape=out_shape,
             grid_spec=pltpu.PrefetchScalarGridSpec(
                 num_scalar_prefetch=1,
-                grid=(local_experts, steps),
+                grid=grid or (local_experts, steps),
                 in_specs=in_specs,
                 out_specs=out_specs,
             ),
@@ -622,88 +636,121 @@
         )(place, *operands)
 
     which = range(halves)
-    back, g_full, other = expert_call(
-        functools.partial(cotangent_kernel, halves=halves, share=share),
-        (kept_struct(hidden_units), kept_struct(model), kept_struct(experts)),
-        (*g_rows, *g_rows, *g_others, expert_out),
-        [ids_spec] * halves + [half_spec(w) for w in which] * 2 + [out_spec],
-        (kept_spec(hidden_units), kept_spec(model), kept_spec(experts)),
-        unit,
-        20 * 10**6,
-    )
-    n_own, back, g_full, other = lax.optimization_barrier((n_own, back, g_full, other))
-    n_oth = swap(n_own, 1)
+    n_oths = [None] * halves
+    back_rows, y_rows, kept = [None] * halves, [None] * halves, [None] * halves
+    part_struct = struct((groups, sent, width), bf16)
+
+    def weight_spec(weight, part):
+        return pl.BlockSpec((1,) + weight.shape[1:], lambda e, j, p: ((p[3] ^ part) * share + e, 0, 0))
+
+    def part_kept(columns):
+        return struct((share, groups * capacity, columns), bf16)
+
+    def multiply_cotangent(part):
+        g_own = g_rows[part]
+        return expert_call(
+            functools.partial(cotangent_kernel, part=part, share=share),
+            (part_kept(hidden_units), part_kept(model), part_kept(experts)),
+            (g_own, g_own, swap(g_own, 1), expert_out),
+            [ids_spec, row_spec, row_spec, weight_spec(expert_out, part)],
+            (kept_spec(hidden_units), kept_spec(model), kept_spec(experts)),
+            unit // halves,
+            20 * 10**6 // halves,
+            grid=(share, steps),
+        )
+
+    backs = [multiply_cotangent(0)] + [None] * (halves - 1)
     if halves == 2:
-        y_struct = struct((2, groups, sent, width), bf16)
-        y_spec = pl.BlockSpec(
-            (1, blocks, capacity, width),
-            lambda e, j, p: ((e // share) ^ p[2], j, lax.rem(e, share), 0),
+        later, n_owns[0], back = lax.optimization_barrier((payloads[1], n_owns[0], backs[0][0]))
+        backs[0] = (back,) + tuple(backs[0][1:])
+        n_owns.append(exchange(later))
+    for part in which:
+        back, g_full, other = backs[part]
+        n_oths[part] = swap(n_owns[part], 1)
+        if part + 1 < halves:
+            n_oths[part], g_rows[1] = lax.optimization_barrier((n_oths[part], g_rows[1]))
+            backs[1] = multiply_cotangent(1)
+        keep, send, act, grad_pre, y_keep, y_send, coefficient = expert_call(
+            functools.partial(expert_grad_kernel, part=part, share=share),
+            (part_struct, part_struct, part_kept(hidden_units), part_kept(hidden_units))
+            + (part_struct, part_struct, part_kept(experts)),
+            (n_owns[part], n_oths[part], back, other, router.T, expert_in, expert_out),
+            [row_spec, row_spec, kept_spec(hidden_units), kept_spec(experts), router_spec]
+            + [weight_spec(expert_in, part), weight_spec(expert_out, part)],
+            (row_spec, row_spec, kept_spec(hidden_units), kept_spec(hidden_units))
+            + (row_spec, row_spec, kept_spec(experts)),
+            3 * unit // halves,
+            35 * 10**6 // halves,
+            grid=(share, steps),
         )
-    else:
-        y_struct, y_spec = row_struct, row_spec
-    keep, send, act, grad_pre, y_keep, y_send, grad_router = expert_call(
-        expert_grad_kernel,
-        (
-            row_struct,
-            row_struct,
-            kept_struct(hidden_units),
-            kept_struct(hidden_units),
-            y_struct,
-            y_struct,
-            struct((experts, model), f32),
-        ),
-        (n_own, n_oth, back, other, router.T, expert_in, expert_out),
-        [row_spec, row_spec, kept_spec(hidden_units), kept_spec(experts)]
-        + [router_spec, in_spec, out_spec],
-        (row_spec, row_spec, kept_spec(hidden_units), kept_spec(hidden_units))
-        + (y_spec, y_spec, router_spec),
-        3 * unit,
-        35 * 10**6,
-    )
-    back_rows = add_low(keep, swap(send, 1))
-    back_rows, y_send = lax.optimization_barrier((back_rows, y_send))
-    back_rows = exchange(back_rows)
-    y_rows = add_low(y_keep, swap(y_send, 1))
-    y_far = swap(y_rows[1], 2) if halves == 2 else None
-    grad_router = grad_router + swap(grad_router, 1)
-    grad_router = grad_router + swap(grad_router, 2)
-
-
-    def combine(value):
-        count = value.shape[1]
-        parted = placing.reshape(groups, rows // count, count, span)
+        kept[part] = (n_owns[part], n_oths[part], act, grad_pre, g_full, coefficient)
+        total = add_low(keep, swap(send, 1))
+        if part + 1 < halves:
+            total, n_owns[1], other = lax.optimization_barrier((total, n_owns[1], backs[1][2]))
+            backs[1] = tuple(backs[1][:2]) + (other,)
+        elif part > 0:
+            total, back_rows[0] = lax.optimization_barrier((total, back_rows[0]))
+        total, y_send = lax.optimization_barrier((total, y_send))
+        back_rows[part] = exchange(total)
+        y_rows[part] = (y_keep, y_send)
+    y_rows = [add_low(y_keep, swap(y_send, 1)) for y_keep, y_send in y_rows]
+    last, y_rows[-1] = lax.optimization_barrier((kept[-1][5], y_rows[-1]))
+    kept[-1] = kept[-1][:5] + (last,)
+    if halves == 2:
+        y_near, y_far = y_rows[0], swap(y_rows[1], 2)
+    def combine(value, part, before=None, dtype=bf16):
+        parted = placing.reshape(groups, halves, sent, span)
+        out_spec = pl.BlockSpec((span, width), lambda i, p: (0, 0))
+        placing_spec = pl.BlockSpec(
+            (groups, 1, sent, span), lambda i, p: (0, p[3] ^ part, 0, 0)
+        )
+        rows_spec = pl.BlockSpec((groups, sent, width), lambda i, p: (0, 0, 0))
         return pl.pallas_call(
             combine_kernel,
-            out_shape=struct((span, width), bf16),
+            out_shape=struct((span, width), dtype),
             grid_spec=pltpu.PrefetchScalarGridSpec(
                 num_scalar_prefetch=1,
                 grid=(1,),
-                in_specs=[
-                    pl.BlockSpec(
-                        (groups, 1, count, span),
-                        lambda i, p: (0, p[2] if count < rows else 0, 0, 0),
-                    ),
-                    pl.BlockSpec((groups, count, width), lambda i, p: (0, 0, 0)),
-                ],
-                out_specs=pl.BlockSpec((span, width), lambda i, p: (0, 0)),
+                in_specs=[placing_spec, rows_spec] + [out_spec] * (before is not None),
+                out_specs=out_spec,
             ),
             compiler_params=pltpu.CompilerParams(vmem_limit_bytes=vmem_bytes),
             cost_estimate=pl.CostEstimate(flops=10**9, bytes_accessed=4 * 10**6, transcendentals=0),
-        )(place, parted, value)
-
-    back_rows, grad_router = lax.optimization_barrier((back_rows, grad_router))
-    z = combine(back_rows)
+        )(place, parted, value, *([] if before is None else [before]))
+
+    grad_router = call(
+        router_kernel,
+        struct((experts, model), f32),
+        (place,) + sum([(a, b, c) for a, b, _, _, _, c in kept], ()),
+        [SMEM] + [VMEM] * (3 * halves),
+        10**9,
+        4 * 10**6,
+    )
+    before = None
     if halves == 2:
+        before = combine(back_rows[0], 0, None, f32)
+        grad_router, before = lax.optimization_barrier((grad_router, before))
+    grad_router = grad_router + swap(grad_router, 1)
+    grad_router = grad_router.astype(bf16)
+    grad_router = grad_router.astype(f32) + swap(grad_router, 2).astype(f32)
+
+
+    if halves == 2:
+        back_rows[1], before = lax.optimization_barrier((back_rows[1], before))
+        z = combine(back_rows[1], 1, before)
         z, y_far = lax.optimization_barrier((z, y_far))
-        y_rows = add_low(y_rows[0], y_far)
+        y_rows = add_low(y_near, y_far)
+    else:
+        z = combine(back_rows[0], 0)
+        y_rows = y_rows[0]
     y_rows = exchange(y_rows)
     z = spread(z)
-    chunk = -(-(4 * inner + experts + 16) // (16 * groups)) * 16
+    chunk = -(-4 * inner // (16 * groups)) * 16 + 16
     grad_hidden, weights, low = call(
         attention_back_kernel,
         (
             struct((span, model), f32),
-            struct((groups * chunk, model), bf16),
+            struct((groups, chunk, model), bf16),
             struct((3, span, inner), bf16),
         ),
         (place,)
@@ -713,10 +760,10 @@
         [SMEM] + [VMEM] * 17,
         10 * 10**9,
         14 * 10**6,
-        scratch_shapes=[pltpu.VMEM((span, model), f32)],
+        scratch_shapes=[pltpu.VMEM((span, model), f32), pltpu.VMEM((4 * inner, model), f32)],
     )
     weights, y_rows = lax.optimization_barrier((weights, y_rows))
-    weight_rows = exchange(weights.reshape(groups, chunk, model))
+    weight_rows = exchange(weights)
     piece_keep, piece_send = call(
         input_back_kernel,
         (struct((span, width), f32), struct((span, width), bf16)),
@@ -737,19 +784,39 @@
         scratch_shapes=[pltpu.VMEM((span, model), f32)],
     )
     grad_pre, norm_row = lax.optimization_barrier((grad_pre, norm_row))
+    operands, specs = (), []
+    for part in which:
+        if part == halves - 1:
+            kept[part] = kept[part][:3] + (grad_pre,) + kept[part][4:]
+
+        def near_index(e, first=part * share):
+            return jnp.clip(e - first, 0, share - 1)
+
+        operands = operands + kept[part][:5]
+        for _ in range(2):
+            specs.append(
+                pl.BlockSpec((blocks, capacity, width), lambda e, j, p, f=near_index: (j, f(e), 0))
+            )
+        for columns in (hidden_units, hidden_units, model):
+            specs.append(
+                pl.BlockSpec((1, block_rows, columns), lambda e, j, p, f=near_index: (f(e), j, 0))
+            )
     grad_expert_in, grad_expert_out = expert_call(
-        expert_weight_kernel,
+        functools.partial(expert_weight_kernel, share=share),
         (struct(expert_in.shape, f32), struct(expert_out.shape, f32)),
-        (n_own, n_oth, g_full, act, grad_pre),
-        [row_spec, row_spec, kept_spec(model), kept_spec(hidden_units), kept_spec(hidden_units)],
+        operands,
+        specs,
         (in_spec, out_spec),
         2 * unit,
         55 * 10**6,
     )
+    norm_row, y_rows = lax.optimization_barrier((norm_row, y_rows))
+    y_part = combine(y_rows, 0)
+    weight_rows, y_part = lax.optimization_barrier((weight_rows, y_part))
     weight_rows = exchange(
         call(
             chunk_kernel,
-            struct((groups, chunk + 16, model), bf16),
+            struct((groups, chunk, model), bf16),
             (weight_rows, norm_row),
             [VMEM] * 2,
             10**7,
@@ -772,12 +839,12 @@
         [VMEM],
         10**7,
         5 * 10**6,
-        scratch_shapes=[pltpu.VMEM((groups * chunk, model), bf16)],
+        scratch_shapes=[pltpu.VMEM((4 * inner, model), f32)],
     )
     layer_out = call(
         layer_out_kernel,
         struct((span, model), bf16),
-        (place,) + spread(combine(y_rows)) + (hidden,),
+        (place,) + spread(y_part) + (hidden,),
         [SMEM] + [VMEM] * 5,
         10**7,
         4 * 10**6,

time: 277 us -> 260 us (0.939)
  waiting for transfers between devices: 92.8 us -> 66.1 us
  Pallas kernels: 106 us -> 114 us
  starting transfers between devices: 54.2 us -> 58.4 us
    ppermute x25 -> x28, waiting for transfers between devices: 76.5 us -> 40.5 us  [swap(): return lax.ppermute(value, 'tensor', [(i, i ^ bits) for i in range(lanes)])]
    all_to_all x6 -> x8, waiting for transfers between devices: 16.4 us -> 25.5 us  [exchange(): return lax.all_to_all(value, 'dp', split_axis=0, concat_axis=0, tiled=True)]
    all_to_all x6 -> x8, starting transfers between devices: 29.8 us -> 36.7 us  [exchange(): return lax.all_to_all(value, 'dp', split_axis=0, concat_axis=0, tiled=True)]
    pallas_call x2 -> x3, Pallas kernels: 8.32 us -> 11.2 us  [combine(): pl.pallas_call(combine_kernel, out_shape=struct((span, width), dtype), gr...]
    ppermute x25 -> x28, starting transfers between devices: 24.4 us -> 21.7 us  [swap(): return lax.ppermute(value, 'tensor', [(i, i ^ bits) for i in range(lanes)])]
    pallas_call x9 -> x10, Pallas kernels: 44.4 us -> 46.7 us  [call(): pl.pallas_call(kernel, out_shape=out_shape, in_specs=specs, compiler_para...]
    pallas_call x3 -> x5, Pallas kernels: 53.6 us -> 55.7 us  [expert_call(): pl.pallas_call(kernel, out_shape=out_shape, grid_spec=pltpu.PrefetchScala...]
    unnamed x62 -> x64, local copies, waits for them, and re-layouts: 10.3 us -> 9.55 us
  transfers between devices with their start and end apart: 31 -> 36, of which waited for: 17 -> 15; matrix products, arithmetic and copies ran while one was open for 3% -> 4% of each run, Pallas kernels for 26% -> 40%
where the time goes in v3:
time: 260 us; the launch traced here: 259 us
  Pallas kernels  114 us (44%)
  waiting for transfers between devices  66.1 us (25%)
  starting transfers between devices  58.4 us (22%)
  local copies, waits for them, and re-layouts  10.1 us (4%)
  other arithmetic  9.33 us (4%)
    pallas_call x5, Pallas kernels, expert_call(): pl.pallas_call(kernel, out_shape=out_shape, grid_spec=pltpu.PrefetchScala...  55.7 us
    pallas_call x10, Pallas kernels, call(): pl.pallas_call(kernel, out_shape=out_shape, in_specs=specs, compiler_para...  46.7 us
    ppermute x28, waiting for transfers between devices, swap(): return lax.ppermute(value, 'tensor', [(i, i ^ bits) for i in range(lanes)])  40.5 us
    all_to_all x8, starting transfers between devices, exchange(): return lax.all_to_all(value, 'dp', split_axis=0, concat_axis=0, tiled=True)  36.7 us
    all_to_all x8, waiting for transfers between devices, exchange(): return lax.all_to_all(value, 'dp', split_axis=0, concat_axis=0, tiled=True)  25.5 us
    ppermute x28, starting transfers between devices, swap(): return lax.ppermute(value, 'tensor', [(i, i ^ bits) for i in range(lanes)])  21.7 us
    pallas_call x3, Pallas kernels, combine(): pl.pallas_call(combine_kernel, out_shape=struct((span, width), dtype), gr...  11.2 us
    unnamed x64, local copies, waits for them, and re-layouts  9.55 us
  transfers between devices with their start and end apart: 36, of which 15 were waited for; matrix products, arithmetic and copies ran while one was open for 4% of the time, Pallas kernels for 40%

profile of v3, /device:TPU:1, one launch (start us, length us, event | category | flops | bytes accessed | tf_op | source)
XLA Modules:
  0.0 258.5 jit_solution(8784354787839218543)
XLA Ops:
  1.3 4.1 %shard_map.238 = (bf16[2048,512]{1,0:T(8,128)(2,1)}, bf16[8,144,384]{2,1,0:T(8,128)(2,1)}) custom-call(s32[4]{0:T(128)} %pad_add_fusion.place_ref.core_ref, s32[2,512]{1,0:T(2,128)} %bitcast.28, bf16[512,768]{1,0:T(8,128)(2,1)} %cotangent_ref.3), custom_call_target="tpu_custom_call" | custom-call | flops 3000000000 | bytes 6000000 | tf_op jit(solution)/shard_map/pallas_call | solution.py:41
  5.3 6.5 %all-to-all-start = ((bf16[8,144,384]{2,1,0:T(8,128)(2,1)}), bf16[8,144,384]{2,1,0:T(8,128)(2,1)S(1)}, u32[]{:S(2)}, u32[]{:S(2)}) async-start(bf16[8,144,384]{2,1,0:T(8,128)(2,1)} %get-tuple-element.95), calls=%async_computation | async-start | bytes 1769472 | tf_op jit(solution)/shard_map/all_to_all | solution.py:555
  13.7 5.6 %shard_map.239 = (bf16[512,192]{1,0:T(8,128)(2,1)}, bf16[512,192]{1,0:T(8,128)(2,1)}, bf16[512,192]{1,0:T(8,128)(2,1)}, bf16[512,192]{1,0:T(8,128)(2,1)}, bf16[3,512,512]{2,1,0:T(8,128)(2,1)}) custom-call(s32[1,3]{1,0:T(1,128)} %lengths_ref.1, bf16[512,768]{1,0:T(8,128)(2,1)} %tokens_ref.7, s32[1,384]{1,0:T(1,128)} %reshape.33.rel_bucket_ref, ...), custom_call_target="tpu_custom_call" | custom-call | flops 6000000000 | bytes 8000000 | tf_op jit(solution)/shard_map/pallas_call | solution.py:41
  19.5 1.5 collective-permute-start.3
  21.6 4.5 %collective-permute-done.1.a2_ref = bf16[512,192]{1,0:T(8,128)(2,1)S(1)} collective-permute-done((bf16[512,192]{1,0:T(8,128)(2,1)}, bf16[512,192]{1,0:T(8,128)(2,1)S(1)}, u32[]{:S(2)}, u32[]{:S(2)}) %collective-permute-start.1) | collective-permute-done | bytes 196640 | tf_op jit(solution)/shard_map/ppermute | solution.py:548
  26.1 2.1 collective-permute-start.2
  30.2 6.9 %shard_map.240 = (f32[512,768]{1,0:T(8,128)}, bf16[8,128,384]{2,1,0:T(8,128)(2,1)}, bf16[8,128,384]{2,1,0:T(8,128)(2,1)}) custom-call(s32[4]{0:T(128)} %pad_add_fusion.place_ref.core_ref, bf16[512,768]{1,0:T(8,128)(2,1)} %tokens_ref.7, bf16[512,192]{1,0:T(8,128)(2,1)} %get-tuple-element.92.a0_ref.attended_ref, bf16[512,192]{1,0:T(8,128)(2,1)} %copy-done.30, ...), custom_call_target="tpu_custom_call" | custom-call | flops 2000000000 | bytes 8000000 | tf_op jit(solution)/shard_map/pallas_call | solution.py:41
  37.1 5.4 %all-to-all-start.1 = ((bf16[8,128,384]{2,1,0:T(8,128)(2,1)}), bf16[8,128,384]{2,1,0:T(8,128)(2,1)S(1)}, u32[]{:S(2)}, u32[]{:S(2)}) async-start(bf16[8,128,384]{2,1,0:T(8,128)(2,1)} %get-tuple-element.96), calls=%async_computation.1 | async-start | bytes 1572864 | tf_op jit(solution)/shard_map/all_to_all | solution.py:555
  43.5 1.8 collective-permute-done.6.oth_ref
  46.2 6.4 %shard_map.241 = (bf16[4,256,768]{2,1,0:T(8,128)(2,1)}, bf16[4,256,768]{2,1,0:T(8,128)(2,1)}, bf16[4,256,64]{2,1,0:T(8,128)(2,1)}) custom-call(s32[4]{0:T(128)} %pad_add_fusion.place_ref.core_ref, bf16[8,144,384]{2,1,0:T(8,128)(2,1)} %copy-done, bf16[8,144,384]{2,1,0:T(8,128)(2,1)} %copy-done, bf16[8,144,384]{2,1,0:T(8,128)(2,1)} %copy-done.10, ...), custom_call_target="tpu_custom_call" | custom-call | flops 1207959552 | bytes 10000000 | tf_op jit(solution)/shard_map/pallas_call | solution.py:625
  52.6 9.2 %all-to-all-done.1.n_own_ref.refs_0_ = bf16[8,128,384]{2,1,0:T(8,128)(2,1)S(1)} async-done(((bf16[8,128,384]{2,1,0:T(8,128)(2,1)}), bf16[8,128,384]{2,1,0:T(8,128)(2,1)S(1)}, u32[]{:S(2)}, u32[]{:S(2)}) %all-to-all-start.1) | async-done | bytes 786464 | tf_op jit(solution)/shard_map/all_to_all | solution.py:555
  61.8 1.8 collective-permute-start.7
  63.7 3.5 %all-to-all-start.2 = ((bf16[8,128,384]{2,1,0:T(8,128)(2,1)}), bf16[8,128,384]{2,1,0:T(8,128)(2,1)S(1)}, u32[]{:S(2)}, u32[]{:S(2)}) async-start(bf16[8,128,384]{2,1,0:T(8,128)(2,1)} %get-tuple-element.105), calls=%async_computation.2 | async-start | bytes 1572864 | tf_op jit(solution)/shard_map/all_to_all | solution.py:555
  67.2 12.1 %shard_map.242 = (bf16[8,128,384]{2,1,0:T(8,128)(2,1)}, bf16[8,128,384]{2,1,0:T(8,128)(2,1)}, bf16[4,256,768]{2,1,0:T(8,128)(2,1)}, bf16[4,256,768]{2,1,0:T(8,12...) custom-call(s32[4]{0:T(128)} %pad_add_fusion.place_ref.core_ref, ...), custom_call_target="tpu_custom_call" | custom-call | flops 3623878656 | bytes 17500000 | tf_op jit(solution)/shard_map/pallas_call | solution.py:625
  79.9 2.2 collective-permute-done.9
  82.1 2.2 add_convert_fusion.4
  85.3 6.4 %shard_map.243 = (bf16[4,256,768]{2,1,0:T(8,128)(2,1)}, bf16[4,256,768]{2,1,0:T(8,128)(2,1)}, bf16[4,256,64]{2,1,0:T(8,128)(2,1)}) custom-call(s32[4]{0:T(128)} %pad_add_fusion.place_ref.core_ref, bf16[8,144,384]{2,1,0:T(8,128)(2,1)} %copy-done.5, bf16[8,144,384]{2,1,0:T(8,128)(2,1)} %copy-done.5, bf16[8,144,384]{2,1,0:T(8,128)(2,1)} %copy-done.9, ...), custom_call_target="tpu_custom_call" | custom-call | flops 1207959552 | bytes 10000000 | tf_op jit(solution)/shard_map/pallas_call | solution.py:625
  91.9 5.4 %all-to-all-start.3 = ((bf16[8,128,384]{2,1,0:T(8,128)(2,1)}), bf16[8,128,384]{2,1,0:T(8,128)(2,1)S(1)}, u32[]{:S(2)}, u32[]{:S(2)}) async-start(bf16[8,128,384]{2,1,0:T(8,128)(2,1)} %add_convert_fusion.4), calls=%async_computation.3 | async-start | bytes 1572864 | tf_op jit(solution)/shard_map/all_to_all | solution.py:555
  98.2 12.1 %shard_map.244 = (bf16[8,128,384]{2,1,0:T(8,128)(2,1)}, bf16[8,128,384]{2,1,0:T(8,128)(2,1)}, bf16[4,256,768]{2,1,0:T(8,128)(2,1)}, bf16[4,256,768]{2,1,0:T(8,12...) custom-call(s32[4]{0:T(128)} %pad_add_fusion.place_ref.core_ref, ...), custom_call_target="tpu_custom_call" | custom-call | flops 3623878656 | bytes 17500000 | tf_op jit(solution)/shard_map/pallas_call | solution.py:625
  110.8 2.1 collective-permute-done.12
  112.9 2.3 add_convert_fusion.3
  115.2 1.9 all-to-all-done.3.rows_ref
  118.4 3.5 %all-to-all-start.4 = ((bf16[8,128,384]{2,1,0:T(8,128)(2,1)}), bf16[8,128,384]{2,1,0:T(8,128)(2,1)S(1)}, u32[]{:S(2)}, u32[]{:S(2)}) async-start(bf16[8,128,384]{2,1,0:T(8,128)(2,1)} %add_convert_fusion.3), calls=%async_computation.4 | async-start | bytes 1572864 | tf_op jit(solution)/shard_map/all_to_all | solution.py:555
  123.7 3.8 %shard_map.246.refs_0_ = f32[512,384]{1,0:T(8,128)} custom-call(s32[4]{0:T(128)} %pad_add_fusion.place_ref.core_ref, bf16[8,2,128,512]{3,2,1,0:T(8,128)(2,1)} %bitcast.13, bf16[8,128,384]{2,1,0:T(8,128)(2,1)} %copy-done.13), custom_call_target="tpu_custom_call" | custom-call | flops 1000000000 | bytes 4000000 | tf_op jit(solution)/shard_map/pallas_call | solution.py:708
  127.4 3.3 %shard_map.245 = f32[64,768]{1,0:T(8,128)} custom-call(s32[4]{0:T(128)} %pad_add_fusion.place_ref.core_ref, bf16[8,128,384]{2,1,0:T(8,128)(2,1)} %copy-done.1, bf16[8,128,384]{2,1,0:T(8,128)(2,1)} %collective-permute-done.7.n_oth_ref.refs_1_, bf16[4,256,64]{2,1,0:T(8,128)(2,1)} %get-tuple-element.119.refs_2_, bf16[8,128,384]{2,1,0:T(8,128)(2,1)} %copy-done.2, ...), custom_call_target="tpu_custom_call" | custom-call | flops 1000000000 | bytes 4000000 | tf_op jit(solution)/shard_map/pallas_call | solution.py:41
  130.8 11.2 %all-to-all-done.4.rows_ref = bf16[8,128,384]{2,1,0:T(8,128)(2,1)S(1)} async-done(((bf16[8,128,384]{2,1,0:T(8,128)(2,1)}), bf16[8,128,384]{2,1,0:T(8,128)(2,1)S(1)}, u32[]{:S(2)}, u32[]{:S(2)}) %all-to-all-start.4) | async-done | bytes 786464 | tf_op jit(solution)/shard_map/all_to_all | solution.py:555
  142.9 3.8 %shard_map.247.z0_ref = bf16[512,384]{1,0:T(8,128)(2,1)} custom-call(s32[4]{0:T(128)} %pad_add_fusion.place_ref.core_ref, bf16[8,2,128,512]{3,2,1,0:T(8,128)(2,1)} %bitcast.14, bf16[8,128,384]{2,1,0:T(8,128)(2,1)} %copy-done.7, f32[512,384]{1,0:T(8,128)} %shard_map.246.refs_0_), custom_call_target="tpu_custom_call" | custom-call | flops 1000000000 | bytes 4000000 | tf_op jit(solution)/shard_map/pallas_call | solution.py:708
  146.9 1.3 collective-permute-start.18
  149.4 3.5 %all-to-all-start.5 = ((bf16[8,128,384]{2,1,0:T(8,128)(2,1)}), bf16[8,128,384]{2,1,0:T(8,128)(2,1)S(1)}, u32[]{:S(2)}, u32[]{:S(2)}) async-start(bf16[8,128,384]{2,1,0:T(8,128)(2,1)} %add_convert_fusion), calls=%async_computation.5 | async-start | bytes 1572864 | tf_op jit(solution)/shard_map/all_to_all | solution.py:555
  153.0 3.6 %collective-permute-done.16.z2_ref = bf16[512,384]{1,0:T(8,128)(2,1)} collective-permute-done((bf16[512,384]{1,0:T(8,128)(2,1)}, bf16[512,384]{1,0:T(8,128)(2,1)}, u32[]{:S(2)}, u32[]{:S(2)}) %collective-permute-start.16) | collective-permute-done | bytes 393248 | tf_op jit(solution)/shard_map/ppermute | solution.py:548
  156.6 1.9 collective-permute-start.17
  158.9 4.2 %collective-permute-done.19 = bf16[64,768]{1,0:T(8,128)(2,1)S(1)} collective-permute-done((bf16[64,768]{1,0:T(8,128)(2,1)S(1)}, bf16[64,768]{1,0:T(8,128)(2,1)S(1)}, u32[]{:S(2)}, u32[]{:S(2)}) %collective-permute-start.19) | collective-permute-done | bytes 98336 | tf_op jit(solution)/shard_map/ppermute | solution.py:548
  164.5 10.9 %shard_map.248 = (f32[512,768]{1,0:T(8,128)}, bf16[8,112,768]{2,1,0:T(8,128)(2,1)}, bf16[3,512,192]{2,1,0:T(8,128)(2,1)}) custom-call(s32[4]{0:T(128)} %pad_add_fusion.place_ref.core_ref, bf16[512,384]{1,0:T(8,128)(2,1)} %shard_map.247.z0_ref, bf16[512,384]{1,0:T(8,128)(2,1)} %collective-permute-done.15.z1_ref, ...), custom_call_target="tpu_custom_call" | custom-call | flops 10000000000 | bytes 14000000 | tf_op jit(solution)/shard_map/pallas_call | solution.py:41
  175.4 3.9 %all-to-all-start.6 = ((bf16[8,112,768]{2,1,0:T(8,128)(2,1)}), bf16[8,112,768]{2,1,0:T(8,128)(2,1)S(1)}, u32[]{:S(2)}, u32[]{:S(2)}) async-start(bf16[8,112,768]{2,1,0:T(8,128)(2,1)} %get-tuple-element.140), calls=%async_computation.6 | async-start | bytes 2752512 | tf_op jit(solution)/shard_map/all_to_all | solution.py:555
  179.3 3.2 %shard_map.249 = (f32[512,384]{1,0:T(8,128)}, bf16[512,384]{1,0:T(8,128)(2,1)}) custom-call(s32[4]{0:T(128)} %pad_add_fusion.place_ref.core_ref, bf16[3,512,192]{2,1,0:T(8,128)(2,1)} %get-tuple-element.142.low_ref, bf16[192,768]{1,0:T(8,128)(2,1)} %bitcast.22, bf16[192,768]{1,0:T(8,128)(2,1)} %bitcast.24, bf16[192,768]{1,0:T(8,128)(2,1)} %bitcast.26), custom_call_target="tpu_custom_call" | custom-call | flops 1000000000 | bytes 4000000 | tf_op jit(solution)/shard_map/pallas_call | solution.py:41
  183.6 1.6 collective-permute-done.21
  187.3 9.4 %collective-permute-done.23.u2_ref = bf16[512,384]{1,0:T(8,128)(2,1)S(1)} collective-permute-done((bf16[512,384]{1,0:T(8,128)(2,1)S(1)}, bf16[512,384]{1,0:T(8,128)(2,1)S(1)}, u32[]{:S(2)}, u32[]{:S(2)}) %collective-permute-start.23) | collective-permute-done | bytes 393248 | tf_op jit(solution)/shard_map/ppermute | solution.py:548
  198.0 1.3 collective-permute-done.24.u3_ref
  200.1 4.2 %shard_map.250 = (f32[512,768]{1,0:T(8,128)}, bf16[16,768]{1,0:T(8,128)(2,1)}) custom-call(s32[4]{0:T(128)} %pad_add_fusion.place_ref.core_ref, bf16[512,384]{1,0:T(8,128)(2,1)} %copy-done.8, bf16[512,384]{1,0:T(8,128)(2,1)} %copy-done.21, bf16[512,384]{1,0:T(8,128)(2,1)} %copy-done.20, bf16[512,384]{1,0:T(8,128)(2,1)} %copy-done.22, ...), custom_call_target="tpu_custom_call" | custom-call | flops 10000000 | bytes 6000000 | tf_op jit(solution)/shard_map/pallas_call | solution.py:41
  204.3 3.6 %shard_map.251.y0_ref = bf16[512,384]{1,0:T(8,128)(2,1)} custom-call(s32[4]{0:T(128)} %pad_add_fusion.place_ref.core_ref, bf16[8,2,128,512]{3,2,1,0:T(8,128)(2,1)} %bitcast.15, bf16[8,128,384]{2,1,0:T(8,128)(2,1)} %copy-done.12), custom_call_target="tpu_custom_call" | custom-call | flops 1000000000 | bytes 4000000 | tf_op jit(solution)/shard_map/pallas_call | solution.py:708
  207.9 3.2 %all-to-all-done.6.rows_ref = bf16[8,112,768]{2,1,0:T(8,128)(2,1)S(1)} async-done(((bf16[8,112,768]{2,1,0:T(8,128)(2,1)}), bf16[8,112,768]{2,1,0:T(8,128)(2,1)S(1)}, u32[]{:S(2)}, u32[]{:S(2)}) %all-to-all-start.6) | async-done | bytes 1376288 | tf_op jit(solution)/shard_map/all_to_all | solution.py:555
  212.2 2.6 %shard_map.253 = bf16[8,112,768]{2,1,0:T(8,128)(2,1)} custom-call(bf16[8,112,768]{2,1,0:T(8,128)(2,1)} %copy-done.4, bf16[16,768]{1,0:T(8,128)(2,1)} %get-tuple-element.153.norm_row_ref), custom_call_target="tpu_custom_call" | custom-call | flops 10000000 | bytes 3000000 | tf_op jit(solution)/shard_map/pallas_call | solution.py:41
  214.8 4.9 %all-to-all-start.7 = ((bf16[8,112,768]{2,1,0:T(8,128)(2,1)}), bf16[8,112,768]{2,1,0:T(8,128)(2,1)S(1)}, u32[]{:S(2)}, u32[]{:S(2)}) async-start(bf16[8,112,768]{2,1,0:T(8,128)(2,1)} %shard_map.253), calls=%async_computation.7 | async-start | bytes 2752512 | tf_op jit(solution)/shard_map/all_to_all | solution.py:555
  221.1 8.6 %collective-permute-done.26.y2_ref = bf16[512,384]{1,0:T(8,128)(2,1)S(1)} collective-permute-done((bf16[512,384]{1,0:T(8,128)(2,1)S(1)}, bf16[512,384]{1,0:T(8,128)(2,1)S(1)}, u32[]{:S(2)}, u32[]{:S(2)}) %collective-permute-start.26) | collective-permute-done | bytes 393248 | tf_op jit(solution)/shard_map/ppermute | solution.py:548
  229.7 1.7 collective-permute-start.27
  231.3 18.7 %shard_map.255 = (f32[8,768,768]{2,1,0:T(8,128)}, f32[8,768,768]{2,1,0:T(8,128)}) custom-call(s32[4]{0:T(128)} %pad_add_fusion.place_ref.core_ref, bf16[8,128,384]{2,1,0:T(8,128)(2,1)} %copy-done.1, bf16[8,128,384]{2,1,0:T(8,128)(2,1)} %collective-permute-done.7.n_oth_ref.refs_1_, bf16[4,256,768]{2,1,0:T(8,128)(2,1)} %get-tuple-element.162.refs_2_, ...), custom_call_target="tpu_custom_call" | custom-call | flops 4831838208 | bytes 55000000 | tf_op jit(solution)/shard_map/pallas_call | solution.py:625
  251.5 3.0 %shard_map.252 = bf16[512,768]{1,0:T(8,128)(2,1)} custom-call(s32[4]{0:T(128)} %pad_add_fusion.place_ref.core_ref, bf16[512,384]{1,0:T(8,128)(2,1)} %shard_map.251.y0_ref, bf16[512,384]{1,0:T(8,128)(2,1)} %copy-done.18, bf16[512,384]{1,0:T(8,128)(2,1)} %copy-done.17, bf16[512,384]{1,0:T(8,128)(2,1)} %copy-done.19, f32[512,768]{1,0:T(8,128)} %get-tuple-element.130.hidden_ref), custom_call_target="tpu_custom_call" | custom-call | flops 10000000 | bytes 4000000 | tf_op jit(solution)/shard_map/pallas_call | solution.py:41
  255.7 2.9 %shard_map.254 = (f32[768]{0:T(1024)}, f32[192,768]{1,0:T(8,128)}, f32[192,768]{1,0:T(8,128)}, f32[192,768]{1,0:T(8,128)}, f32[192,768]{1,0:T(8,128)}, /*index=5...) custom-call(bf16[8,112,768]{2,1,0:T(8,128)(2,1)} %copy-done.3), custom_call_target="tpu_custom_call" | custom-call | flops 10000000 | bytes 5000000 | tf_op jit(solution)/shard_map/pallas_call | solution.py:41
  (115 shorter events, 27.5 us)
Async XLA Ops:
  5.3 6.5 %copy-start.25 = (bf16[192,768]{1,0:T(8,128)(2,1)S(1)}, bf16[192,768]{1,0:T(8,128)(2,1)}, u32[]{:S(2)}) copy-start(bf16[192,768]{1,0:T(8,128)(2,1)} %wo_ref.1) | copy-start | bytes 884740
  5.3 7.8 %copy-start.23 = (s32[384]{0:T(512)S(1)}, s32[384]{0:T(512)}, u32[]{:S(2)}) copy-start(s32[384]{0:T(512)} %param.18) | copy-start | bytes 4612
  5.3 31.8 %all-to-all-start = ((bf16[8,144,384]{2,1,0:T(8,128)(2,1)}), bf16[8,144,384]{2,1,0:T(8,128)(2,1)S(1)}, u32[]{:S(2)}, u32[]{:S(2)}) async-start(bf16[8,144,384]{2,1,0:T(8,128)(2,1)} %get-tuple-element.95), calls=%async_computation | async-start | bytes 1769472 | tf_op jit(solution)/shard_map/all_to_all | solution.py:555
  11.8 9.2 %collective-permute-start.4 = (bf16[192,768]{1,0:T(8,128)(2,1)S(1)}, bf16[192,768]{1,0:T(8,128)(2,1)S(1)}, u32[]{:S(2)}, u32[]{:S(2)}) collective-permute-start(bf16[192,768]{1,0:T(8,128)(2,1)S(1)} %copy-done.25), channel_id=1, source_target_pairs={{0,2},{1,3},{2,0},{3,1},{4,6},{5,7},{6,4},{7,5},{8,10},{9,11},{10,... | collective-permute-start | bytes 884744 | tf_op jit(solution)/shard_map/ppermute | solution.py:548
  19.3 6.8 %collective-permute-start.1 = (bf16[512,192]{1,0:T(8,128)(2,1)}, bf16[512,192]{1,0:T(8,128)(2,1)S(1)}, u32[]{:S(2)}, u32[]{:S(2)}) collective-permute-start(bf16[512,192]{1,0:T(8,128)(2,1)} %get-tuple-element.92.a0_ref.attended_ref), channel_id=1, source_target_pairs={{0,2},{1,3},{2,0},{3,1},{4,6},{5,7},{6,4},{7,5},{8,10},{9,11},{10,... | collective-permute-start | bytes 589832 | tf_op jit(solution)/shard_map/ppermute | solution.py:548
  19.5 8.7 %collective-permute-start.3 = (bf16[192,768]{1,0:T(8,128)(2,1)S(1)}, bf16[192,768]{1,0:T(8,128)(2,1)S(1)}, u32[]{:S(2)}, u32[]{:S(2)}) collective-permute-start(bf16[192,768]{1,0:T(8,128)(2,1)S(1)} %copy-done.25), channel_id=1, source_target_pairs={{0,1},{1,0},{2,3},{3,2},{4,5},{5,4},{6,7},{7,6},{8,9},{9,8},{10,11... | collective-permute-start | bytes 884744 | tf_op jit(solution)/shard_map/ppermute | solution.py:548
  21.0 8.4 %copy-start.26 = (bf16[192,768]{1,0:T(8,128)(2,1)}, bf16[192,768]{1,0:T(8,128)(2,1)S(1)}, u32[]{:S(2)}) copy-start(bf16[192,768]{1,0:T(8,128)(2,1)S(1)} %collective-permute-done.4.w2_ref) | copy-start | bytes 884740
  21.0 8.3 %collective-permute-start.5 = (bf16[192,768]{1,0:T(8,128)(2,1)S(1)}, bf16[192,768]{1,0:T(8,128)(2,1)S(1)}, u32[]{:S(2)}, u32[]{:S(2)}) collective-permute-start(bf16[192,768]{1,0:T(8,128)(2,1)S(1)} %collective-permute-done.4.w2_ref), channel_id=1, source_target_pairs={{0,1},{1,0},{2,3},{3,2},{4,5},{5,4},{6,7},{7,6},{8,9},{9,8},{10,11... | collective-permute-start | bytes 884744 | tf_op jit(solution)/shard_map/ppermute | solution.py:548
  21.3 6.9 %collective-permute-start = (bf16[512,192]{1,0:T(8,128)(2,1)}, bf16[512,192]{1,0:T(8,128)(2,1)S(1)}, u32[]{:S(2)}, u32[]{:S(2)}) collective-permute-start(bf16[512,192]{1,0:T(8,128)(2,1)} %get-tuple-element.92.a0_ref.attended_ref), channel_id=1, source_target_pairs={{0,1},{1,0},{2,3},{3,2},{4,5},{5,4},{6,7},{7,6},{8,9},{9,8},{10,11... | collective-permute-start | bytes 589832 | tf_op jit(solution)/shard_map/ppermute | solution.py:548
  26.1 3.3 %collective-permute-start.2 = (bf16[512,192]{1,0:T(8,128)(2,1)S(1)}, bf16[512,192]{1,0:T(8,128)(2,1)S(1)}, u32[]{:S(2)}, u32[]{:S(2)}) collective-permute-start(bf16[512,192]{1,0:T(8,128)(2,1)S(1)} %collective-permute-done.1.a2_ref), channel_id=1, source_target_pairs={{0,1},{1,0},{2,3},{3,2},{4,5},{5,4},{6,7},{7,6},{8,9},{9,8},{10,11... | collective-permute-start | bytes 589832 | tf_op jit(solution)/shard_map/ppermute | solution.py:548
  37.1 8.2 %copy-start = (bf16[8,144,384]{2,1,0:T(8,128)(2,1)}, bf16[8,144,384]{2,1,0:T(8,128)(2,1)S(1)}, u32[]{:S(2)}) copy-start(bf16[8,144,384]{2,1,0:T(8,128)(2,1)S(1)} %all-to-all-done.ids_ref.own_ref) | copy-start | bytes 2654212
  37.1 24.7 %all-to-all-start.1 = ((bf16[8,128,384]{2,1,0:T(8,128)(2,1)}), bf16[8,128,384]{2,1,0:T(8,128)(2,1)S(1)}, u32[]{:S(2)}, u32[]{:S(2)}) async-start(bf16[8,128,384]{2,1,0:T(8,128)(2,1)} %get-tuple-element.96), calls=%async_computation.1 | async-start | bytes 1572864 | tf_op jit(solution)/shard_map/all_to_all | solution.py:555
  42.5 2.8 %collective-permute-start.6 = (bf16[8,144,384]{2,1,0:T(8,128)(2,1)S(1)}, bf16[8,144,384]{2,1,0:T(8,128)(2,1)S(1)}, u32[]{:S(2)}, u32[]{:S(2)}) collective-permute-start(bf16[8,144,384]{2,1,0:T(8,128)(2,1)S(1)} %all-to-all-done.ids_ref.own_ref), channel_id=1, source_target_pairs={{0,1},{1,0},{2,3},{3,2},{4,5},{5,4},{6,7},{7,6},{8,9},{9,8},{10,11... | collective-permute-start | bytes 2654216 | tf_op jit(solution)/shard_map/ppermute | solution.py:548
  43.2 24.0 %collective-permute-start.8 = (bf16[8,144,384]{2,1,0:T(8,128)(2,1)S(1)}, bf16[8,144,384]{2,1,0:T(8,128)(2,1)S(1)}, u32[]{:S(2)}, u32[]{:S(2)}) collective-permute-start(bf16[8,144,384]{2,1,0:T(8,128)(2,1)S(1)} %all-to-all-done.ids_ref.own_ref), channel_id=1, source_target_pairs={{0,2},{1,3},{2,0},{3,1},{4,6},{5,7},{6,4},{7,5},{8,10},{9,11},{10,... | collective-permute-start | bytes 2654216 | tf_op jit(solution)/shard_map/ppermute | solution.py:548
  61.8 5.4 %collective-permute-start.7 = (bf16[8,128,384]{2,1,0:T(8,128)(2,1)S(1)}, bf16[8,128,384]{2,1,0:T(8,128)(2,1)}, u32[]{:S(2)}, u32[]{:S(2)}) collective-permute-start(bf16[8,128,384]{2,1,0:T(8,128)(2,1)S(1)} %all-to-all-done.1.n_own_ref.refs_0_), channel_id=1, source_target_pairs={{0,1},{1,0},{2,3},{3,2},{4,5},{5,4},{6,7},{7,6},{8,9},{9,8},{10,11... | collective-permute-start | bytes 2359304 | tf_op jit(solution)/shard_map/ppermute | solution.py:548
  63.7 28.0 %all-to-all-start.2 = ((bf16[8,128,384]{2,1,0:T(8,128)(2,1)}), bf16[8,128,384]{2,1,0:T(8,128)(2,1)S(1)}, u32[]{:S(2)}, u32[]{:S(2)}) async-start(bf16[8,128,384]{2,1,0:T(8,128)(2,1)} %get-tuple-element.105), calls=%async_computation.2 | async-start | bytes 1572864 | tf_op jit(solution)/shard_map/all_to_all | solution.py:555
  67.2 12.2 %copy-start.5 = (bf16[8,144,384]{2,1,0:T(8,128)(2,1)}, bf16[8,144,384]{2,1,0:T(8,128)(2,1)S(1)}, u32[]{:S(2)}) copy-start(bf16[8,144,384]{2,1,0:T(8,128)(2,1)S(1)} %collective-permute-done.8.ids_ref.own_ref) | copy-start | bytes 2654212
  79.3 2.8 %collective-permute-start.9 = (bf16[8,128,384]{2,1,0:T(8,128)(2,1)}, bf16[8,128,384]{2,1,0:T(8,128)(2,1)S(1)}, u32[]{:S(2)}, u32[]{:S(2)}) collective-permute-start(bf16[8,128,384]{2,1,0:T(8,128)(2,1)} %get-tuple-element.104), channel_id=1, source_target_pairs={{0,1},{1,0},{2,3},{3,2},{4,5},{5,4},{6,7},{7,6},{8,9},{9,8},{10,11... | collective-permute-start | bytes 2359304 | tf_op jit(solution)/shard_map/ppermute | solution.py:548
  79.4 4.9 %collective-permute-start.10 = (bf16[8,144,384]{2,1,0:T(8,128)(2,1)S(1)}, bf16[8,144,384]{2,1,0:T(8,128)(2,1)S(1)}, u32[]{:S(2)}, u32[]{:S(2)}) collective-permute-start(bf16[8,144,384]{2,1,0:T(8,128)(2,1)S(1)} %collective-permute-done.8.ids_ref.own_ref), channel_id=1, source_target_pairs={{0,1},{1,0},{2,3},{3,2},{4,5},{5,4},{6,7},{7,6},{8,9},{9,8},{10,11... | collective-permute-start | bytes 2654216 | tf_op jit(solution)/shard_map/ppermute | solution.py:548
  91.7 5.6 %collective-permute-start.11 = (bf16[8,128,384]{2,1,0:T(8,128)(2,1)S(1)}, bf16[8,128,384]{2,1,0:T(8,128)(2,1)S(1)}, u32[]{:S(2)}, u32[]{:S(2)}) collective-permute-start(bf16[8,128,384]{2,1,0:T(8,128)(2,1)S(1)} %all-to-all-done.2.n_own_ref.refs_3_.refs_5_), channel_id=1, source_target_pairs={{0,1},{1,0},{2,3},{3,2},{4,5},{5,4},{6,7},{7,6},{8,9},{9,8},{10,11... | collective-permute-start | bytes 2359304 | tf_op jit(solution)/shard_map/ppermute | solution.py:548
  91.9 25.2 %all-to-all-start.3 = ((bf16[8,128,384]{2,1,0:T(8,128)(2,1)}), bf16[8,128,384]{2,1,0:T(8,128)(2,1)S(1)}, u32[]{:S(2)}, u32[]{:S(2)}) async-start(bf16[8,128,384]{2,1,0:T(8,128)(2,1)} %add_convert_fusion.4), calls=%async_computation.3 | async-start | bytes 1572864 | tf_op jit(solution)/shard_map/all_to_all | solution.py:555
  110.3 2.6 %collective-permute-start.12 = (bf16[8,128,384]{2,1,0:T(8,128)(2,1)}, bf16[8,128,384]{2,1,0:T(8,128)(2,1)S(1)}, u32[]{:S(2)}, u32[]{:S(2)}) collective-permute-start(bf16[8,128,384]{2,1,0:T(8,128)(2,1)} %get-tuple-element.112), channel_id=1, source_target_pairs={{0,1},{1,0},{2,3},{3,2},{4,5},{5,4},{6,7},{7,6},{8,9},{9,8},{10,11... | collective-permute-start | bytes 2359304 | tf_op jit(solution)/shard_map/ppermute | solution.py:548
  112.9 9.0 %copy-start.15 = (bf16[8,128,384]{2,1,0:T(8,128)(2,1)S(1)}, bf16[8,128,384]{2,1,0:T(8,128)(2,1)}, u32[]{:S(2)}) copy-start(bf16[8,128,384]{2,1,0:T(8,128)(2,1)} %get-tuple-element.121) | copy-start | bytes 2359300
  117.1 5.9 %copy-start.13 = (bf16[8,128,384]{2,1,0:T(8,128)(2,1)}, bf16[8,128,384]{2,1,0:T(8,128)(2,1)S(1)}, u32[]{:S(2)}) copy-start(bf16[8,128,384]{2,1,0:T(8,128)(2,1)S(1)} %all-to-all-done.3.rows_ref) | copy-start | bytes 2359300
  117.1 4.8 %collective-permute-start.13 = (bf16[8,128,384]{2,1,0:T(8,128)(2,1)}, bf16[8,128,384]{2,1,0:T(8,128)(2,1)S(1)}, u32[]{:S(2)}, u32[]{:S(2)}) collective-permute-start(bf16[8,128,384]{2,1,0:T(8,128)(2,1)} %get-tuple-element.122), channel_id=1, source_target_pairs={{0,1},{1,0},{2,3},{3,2},{4,5},{5,4},{6,7},{7,6},{8,9},{9,8},{10,11... | collective-permute-start | bytes 2359304 | tf_op jit(solution)/shard_map/ppermute | solution.py:548
  118.4 23.6 %all-to-all-start.4 = ((bf16[8,128,384]{2,1,0:T(8,128)(2,1)}), bf16[8,128,384]{2,1,0:T(8,128)(2,1)S(1)}, u32[]{:S(2)}, u32[]{:S(2)}) async-start(bf16[8,128,384]{2,1,0:T(8,128)(2,1)} %add_convert_fusion.3), calls=%async_computation.4 | async-start | bytes 1572864 | tf_op jit(solution)/shard_map/all_to_all | solution.py:555
  123.0 23.6 %collective-permute-start.14 = (bf16[8,128,384]{2,1,0:T(8,128)(2,1)}, bf16[8,128,384]{2,1,0:T(8,128)(2,1)S(1)}, u32[]{:S(2)}, u32[]{:S(2)}) collective-permute-start(bf16[8,128,384]{2,1,0:T(8,128)(2,1)} %add_convert_fusion.2), channel_id=1, source_target_pairs={{0,2},{1,3},{2,0},{3,1},{4,6},{5,7},{6,4},{7,5},{8,10},{9,11},{10,... | collective-permute-start | bytes 2359304 | tf_op jit(solution)/shard_map/ppermute | solution.py:548
  123.3 24.9 %collective-permute-start.20 = (bf16[8,128,384]{2,1,0:T(8,128)(2,1)}, bf16[8,128,384]{2,1,0:T(8,128)(2,1)S(1)}, u32[]{:S(2)}, u32[]{:S(2)}) collective-permute-start(bf16[8,128,384]{2,1,0:T(8,128)(2,1)} %get-tuple-element.138), channel_id=1, source_target_pairs={{0,1},{1,0},{2,3},{3,2},{4,5},{5,4},{6,7},{7,6},{8,9},{9,8},{10,11... | collective-permute-start | bytes 2359304 | tf_op jit(solution)/shard_map/ppermute | solution.py:548
  130.8 16.2 %copy-start.11 = (f32[64,768]{1,0:T(8,128)S(1)}, f32[64,768]{1,0:T(8,128)}, u32[]{:S(2)}) copy-start(f32[64,768]{1,0:T(8,128)} %shard_map.245) | copy-start | bytes 589828
  130.8 17.5 %copy-start.14 = (bf16[8,128,384]{2,1,0:T(8,128)(2,1)S(1)}, bf16[8,128,384]{2,1,0:T(8,128)(2,1)}, u32[]{:S(2)}) copy-start(bf16[8,128,384]{2,1,0:T(8,128)(2,1)} %get-tuple-element.137) | copy-start | bytes 2359300
  146.7 9.9 %collective-permute-start.16 = (bf16[512,384]{1,0:T(8,128)(2,1)}, bf16[512,384]{1,0:T(8,128)(2,1)}, u32[]{:S(2)}, u32[]{:S(2)}) collective-permute-start(bf16[512,384]{1,0:T(8,128)(2,1)} %shard_map.247.z0_ref), channel_id=1, source_target_pairs={{0,2},{1,3},{2,0},{3,1},{4,6},{5,7},{6,4},{7,5},{8,10},{9,11},{10,... | collective-permute-start | bytes 1179656 | tf_op jit(solution)/shard_map/ppermute | solution.py:548
  146.9 11.6 %collective-permute-start.18 = (f32[64,768]{1,0:T(8,128)S(1)}, f32[64,768]{1,0:T(8,128)S(1)}, u32[]{:S(2)}, u32[]{:S(2)}) collective-permute-start(f32[64,768]{1,0:T(8,128)S(1)} %copy-done.11), channel_id=1, source_target_pairs={{0,1},{1,0},{2,3},{3,2},{4,5},{5,4},{6,7},{7,6},{8,9},{9,8},{10,11... | collective-permute-start | bytes 589832 | tf_op jit(solution)/shard_map/ppermute | solution.py:548
  148.2 15.5 %collective-permute-start.15 = (bf16[512,384]{1,0:T(8,128)(2,1)}, bf16[512,384]{1,0:T(8,128)(2,1)}, u32[]{:S(2)}, u32[]{:S(2)}) collective-permute-start(bf16[512,384]{1,0:T(8,128)(2,1)} %shard_map.247.z0_ref), channel_id=1, source_target_pairs={{0,1},{1,0},{2,3},{3,2},{4,5},{5,4},{6,7},{7,6},{8,9},{9,8},{10,11... | collective-permute-start | bytes 1179656 | tf_op jit(solution)/shard_map/ppermute | solution.py:548
  149.4 26.0 %all-to-all-start.5 = ((bf16[8,128,384]{2,1,0:T(8,128)(2,1)}), bf16[8,128,384]{2,1,0:T(8,128)(2,1)S(1)}, u32[]{:S(2)}, u32[]{:S(2)}) async-start(bf16[8,128,384]{2,1,0:T(8,128)(2,1)} %add_convert_fusion), calls=%async_computation.5 | async-start | bytes 1572864 | tf_op jit(solution)/shard_map/all_to_all | solution.py:555
  156.6 7.1 %collective-permute-start.17 = (bf16[512,384]{1,0:T(8,128)(2,1)}, bf16[512,384]{1,0:T(8,128)(2,1)S(1)}, u32[]{:S(2)}, u32[]{:S(2)}) collective-permute-start(bf16[512,384]{1,0:T(8,128)(2,1)} %collective-permute-done.16.z2_ref), channel_id=1, source_target_pairs={{0,1},{1,0},{2,3},{3,2},{4,5},{5,4},{6,7},{7,6},{8,9},{9,8},{10,11... | collective-permute-start | bytes 1179656 | tf_op jit(solution)/shard_map/ppermute | solution.py:548
  158.6 4.5 %collective-permute-start.19 = (bf16[64,768]{1,0:T(8,128)(2,1)S(1)}, bf16[64,768]{1,0:T(8,128)(2,1)S(1)}, u32[]{:S(2)}, u32[]{:S(2)}) collective-permute-start(bf16[64,768]{1,0:T(8,128)(2,1)S(1)} %add_convert_fusion.6), channel_id=1, source_target_pairs={{0,2},{1,3},{2,0},{3,1},{4,6},{5,7},{6,4},{7,5},{8,10},{9,11},{10,... | collective-permute-start | bytes 294920 | tf_op jit(solution)/shard_map/ppermute | solution.py:548
  175.4 7.1 %copy-start.12 = (bf16[8,128,384]{2,1,0:T(8,128)(2,1)}, bf16[8,128,384]{2,1,0:T(8,128)(2,1)S(1)}, u32[]{:S(2)}) copy-start(bf16[8,128,384]{2,1,0:T(8,128)(2,1)S(1)} %all-to-all-done.5.rows_ref) | copy-start | bytes 2359300
  175.4 35.7 %all-to-all-start.6 = ((bf16[8,112,768]{2,1,0:T(8,128)(2,1)}), bf16[8,112,768]{2,1,0:T(8,128)(2,1)S(1)}, u32[]{:S(2)}, u32[]{:S(2)}) async-start(bf16[8,112,768]{2,1,0:T(8,128)(2,1)} %get-tuple-element.140), calls=%async_computation.6 | async-start | bytes 2752512 | tf_op jit(solution)/shard_map/all_to_all | solution.py:555
  182.5 2.6 %collective-permute-start.21 = (bf16[512,384]{1,0:T(8,128)(2,1)}, bf16[512,384]{1,0:T(8,128)(2,1)S(1)}, u32[]{:S(2)}, u32[]{:S(2)}) collective-permute-start(bf16[512,384]{1,0:T(8,128)(2,1)} %get-tuple-element.144), channel_id=1, source_target_pairs={{0,1},{1,0},{2,3},{3,2},{4,5},{5,4},{6,7},{7,6},{8,9},{9,8},{10,11... | collective-permute-start | bytes 1179656 | tf_op jit(solution)/shard_map/ppermute | solution.py:548
  186.4 13.0 %copy-start.8 = (bf16[512,384]{1,0:T(8,128)(2,1)}, bf16[512,384]{1,0:T(8,128)(2,1)S(1)}, u32[]{:S(2)}) copy-start(bf16[512,384]{1,0:T(8,128)(2,1)S(1)} %add_convert_fusion.5.u0_ref) | copy-start | bytes 1179652
  186.4 10.4 %collective-permute-start.23 = (bf16[512,384]{1,0:T(8,128)(2,1)S(1)}, bf16[512,384]{1,0:T(8,128)(2,1)S(1)}, u32[]{:S(2)}, u32[]{:S(2)}) collective-permute-start(bf16[512,384]{1,0:T(8,128)(2,1)S(1)} %add_convert_fusion.5.u0_ref), channel_id=1, source_target_pairs={{0,2},{1,3},{2,0},{3,1},{4,6},{5,7},{6,4},{7,5},{8,10},{9,11},{10,... | collective-permute-start | bytes 1179656 | tf_op jit(solution)/shard_map/ppermute | solution.py:548
  186.7 11.3 %collective-permute-start.22 = (bf16[512,384]{1,0:T(8,128)(2,1)S(1)}, bf16[512,384]{1,0:T(8,128)(2,1)S(1)}, u32[]{:S(2)}, u32[]{:S(2)}) collective-permute-start(bf16[512,384]{1,0:T(8,128)(2,1)S(1)} %add_convert_fusion.5.u0_ref), channel_id=1, source_target_pairs={{0,1},{1,0},{2,3},{3,2},{4,5},{5,4},{6,7},{7,6},{8,9},{9,8},{10,11... | collective-permute-start | bytes 1179656 | tf_op jit(solution)/shard_map/ppermute | solution.py:548
  196.8 2.6 collective-permute-start.24
  214.8 39.8 %all-to-all-start.7 = ((bf16[8,112,768]{2,1,0:T(8,128)(2,1)}), bf16[8,112,768]{2,1,0:T(8,128)(2,1)S(1)}, u32[]{:S(2)}, u32[]{:S(2)}) async-start(bf16[8,112,768]{2,1,0:T(8,128)(2,1)} %shard_map.253), calls=%async_computation.7 | async-start | bytes 2752512 | tf_op jit(solution)/shard_map/all_to_all | solution.py:555
  219.7 9.9 %collective-permute-start.26 = (bf16[512,384]{1,0:T(8,128)(2,1)S(1)}, bf16[512,384]{1,0:T(8,128)(2,1)S(1)}, u32[]{:S(2)}, u32[]{:S(2)}) collective-permute-start(bf16[512,384]{1,0:T(8,128)(2,1)S(1)} %copy-done.16), channel_id=1, source_target_pairs={{0,2},{1,3},{2,0},{3,1},{4,6},{5,7},{6,4},{7,5},{8,10},{9,11},{10,... | collective-permute-start | bytes 1179656 | tf_op jit(solution)/shard_map/ppermute | solution.py:548
  220.1 30.0 %collective-permute-start.25 = (bf16[512,384]{1,0:T(8,128)(2,1)S(1)}, bf16[512,384]{1,0:T(8,128)(2,1)S(1)}, u32[]{:S(2)}, u32[]{:S(2)}) collective-permute-start(bf16[512,384]{1,0:T(8,128)(2,1)S(1)} %copy-done.16), channel_id=1, source_target_pairs={{0,1},{1,0},{2,3},{3,2},{4,5},{5,4},{6,7},{7,6},{8,9},{9,8},{10,11... | collective-permute-start | bytes 1179656 | tf_op jit(solution)/shard_map/ppermute | solution.py:548
  229.7 20.3 %copy-start.17 = (bf16[512,384]{1,0:T(8,128)(2,1)}, bf16[512,384]{1,0:T(8,128)(2,1)S(1)}, u32[]{:S(2)}) copy-start(bf16[512,384]{1,0:T(8,128)(2,1)S(1)} %collective-permute-done.26.y2_ref) | copy-start | bytes 1179652
  229.7 20.4 %collective-permute-start.27 = (bf16[512,384]{1,0:T(8,128)(2,1)S(1)}, bf16[512,384]{1,0:T(8,128)(2,1)S(1)}, u32[]{:S(2)}, u32[]{:S(2)}) collective-permute-start(bf16[512,384]{1,0:T(8,128)(2,1)S(1)} %collective-permute-done.26.y2_ref), channel_id=1, source_target_pairs={{0,1},{1,0},{2,3},{3,2},{4,5},{5,4},{6,7},{7,6},{8,9},{9,8},{10,11... | collective-permute-start | bytes 1179656 | tf_op jit(solution)/shard_map/ppermute | solution.py:548
  (20 other events, 35.8 us)

commit v4 on v3

--- a/solution.py
+++ b/solution.py
@@ -175,9 +175,14 @@
     normed_half = normed_ref[:, half(None, core_ref[0], width)]
     parts = len(payload_refs)
     for d in range(groups):
-        for part, payload_ref in enumerate(payload_refs):
-            start = pl.multiple_of((d * parts + (core_ref[3] ^ part)) * rows, 16)
-            payload_ref[d] = mm(placing_ref[pl.ds(start, rows), :], normed_half).astype(bf16)
+        start = d * parts * rows
+        placed = mm(placing_ref[start : start + parts * rows, :], normed_half).astype(bf16)
+        if parts == 1:
+            payload_refs[0][d] = placed
+        else:
+            first = core_ref[3] == 0
+            payload_refs[0][d] = jnp.where(first, placed[:rows], placed[rows:])
+            payload_refs[1][d] = jnp.where(first, placed[rows:], placed[:rows])
 
 
 def merge_rows(ref):
@@ -321,14 +326,20 @@
         pl.when(e // share == part)(functools.partial(add, *refs[5 * part : 5 * part + 5]))
 
 
-def combine_kernel(place_ref, placing_ref, rows_ref, *refs):
+def combine_kernel(place_ref, placing_ref, rows_ref, *refs, before):
     out_ref = refs[-1]
     groups, rows, width = rows_ref.shape
     placing = placing_ref[...].reshape(groups * rows, placing_ref.shape[3])
     total = mm(placing, rows_ref[...].reshape(groups * rows, width), 0, 0)
-    if len(refs) == 2:
+    if before:
         total = total + refs[0][...]
-    out_ref[...] = total.astype(out_ref.dtype)
+    span = total.shape[0]
+    out_ref[0:span, :] = total.astype(out_ref.dtype)
+    if len(refs) > 1 + before:
+        router_ref = refs[before]
+        experts = router_ref.shape[0]
+        out_ref[span : span + experts, :] = router_ref[:, :width].astype(out_ref.dtype)
+        out_ref[span + experts : span + 2 * experts, :] = router_ref[:, width:].astype(out_ref.dtype)
 
 
 def attention_back_kernel(
@@ -349,7 +360,6 @@
     v_ref,
     probs_ref,
     rel_bucket_ref,
-    grad_router_ref,
     grad_hidden_ref,
     weights_ref,
     low_ref,
@@ -364,8 +374,12 @@
     core = core_ref[0]
     own = half(None, core, width)
     oth = half(None, 1 - core, width)
-    gn_ref[:, own] = z0_ref[...].astype(f32) + z2_ref[...].astype(f32)
-    gn_ref[:, oth] = z1_ref[...].astype(f32) + z3_ref[...].astype(f32)
+    gn_ref[:, own] = z0_ref[0:span, :].astype(f32) + z2_ref[0:span, :].astype(f32)
+    gn_ref[:, oth] = z1_ref[0:span, :].astype(f32) + z3_ref[0:span, :].astype(f32)
+    below = [r[span:, :].astype(f32) for r in (z0_ref, z1_ref, z2_ref, z3_ref)]
+    router = (below[0] + below[1]) + (below[2] + below[3])
+    experts = router.shape[0] // 2
+    router = jnp.concatenate([router[:experts], router[experts:]], axis=1).astype(bf16)
     grad_normed = gn_ref[...]
     hidden = hidden_ref[...]
     r2 = lax.rsqrt(jnp.mean(hidden * hidden, axis=1, keepdims=True) + epsilon)
@@ -406,12 +420,11 @@
         all_ref[j * inner : (j + 1) * inner, :] = mm(low, normed, 0, 0)
     groups, chunk, _ = weights_ref.shape
     count = 4 * inner // groups
-    share = grad_router_ref.shape[0] // groups
+    share = experts // groups
     weights_ref[:, chunk - 16 :, :] = jnp.zeros((groups, 16, model), bf16)
     for d in range(groups):
         weights_ref[d, 0:count, :] = all_ref[d * count : (d + 1) * count, :].astype(bf16)
-        tail = grad_router_ref[d * share : (d + 1) * share, :].astype(bf16)
-        weights_ref[d, chunk - 16 : chunk - 16 + share, :] = tail
+        weights_ref[d, chunk - 16 : chunk - 16 + share, :] = router[d * share : (d + 1) * share, :]
         if d < 8:
             weights_ref[d, chunk - 8 : chunk - 7, :] = small[d : d + 1, :]
 
@@ -698,25 +711,29 @@
     kept[-1] = kept[-1][:5] + (last,)
     if halves == 2:
         y_near, y_far = y_rows[0], swap(y_rows[1], 2)
-    def combine(value, part, before=None, dtype=bf16):
+    def combine(value, part, before=None, dtype=bf16, extra=None):
         parted = placing.reshape(groups, halves, sent, span)
-        out_spec = pl.BlockSpec((span, width), lambda i, p: (0, 0))
+        below = 0 if extra is None else 2 * experts
+        before_spec = pl.BlockSpec((span, width), lambda i, p: (0, 0))
+        extra_spec = pl.BlockSpec((experts, model), lambda i, p: (0, 0))
         placing_spec = pl.BlockSpec(
             (groups, 1, sent, span), lambda i, p: (0, p[3] ^ part, 0, 0)
         )
         rows_spec = pl.BlockSpec((groups, sent, width), lambda i, p: (0, 0, 0))
         return pl.pallas_call(
-            combine_kernel,
-            out_shape=struct((span, width), dtype),
+            functools.partial(combine_kernel, before=int(before is not None)),
+            out_shape=struct((span + below, width), dtype),
             grid_spec=pltpu.PrefetchScalarGridSpec(
                 num_scalar_prefetch=1,
                 grid=(1,),
-                in_specs=[placing_spec, rows_spec] + [out_spec] * (before is not None),
-                out_specs=out_spec,
+                in_specs=[placing_spec, rows_spec]
+                + [before_spec] * (before is not None)
+                + [extra_spec] * (extra is not None),
+                out_specs=pl.BlockSpec((span + below, width), lambda i, p: (0, 0)),
             ),
             compiler_params=pltpu.CompilerParams(vmem_limit_bytes=vmem_bytes),
             cost_estimate=pl.CostEstimate(flops=10**9, bytes_accessed=4 * 10**6, transcendentals=0),
-        )(place, parted, value, *([] if before is None else [before]))
+        )(place, parted, value, *(operand for operand in (before, extra) if operand is not None))
 
     grad_router = call(
         router_kernel,
@@ -730,18 +747,15 @@
     if halves == 2:
         before = combine(back_rows[0], 0, None, f32)
         grad_router, before = lax.optimization_barrier((grad_router, before))
-    grad_router = grad_router + swap(grad_router, 1)
-    grad_router = grad_router.astype(bf16)
-    grad_router = grad_router.astype(f32) + swap(grad_router, 2).astype(f32)
 
 
     if halves == 2:
         back_rows[1], before = lax.optimization_barrier((back_rows[1], before))
-        z = combine(back_rows[1], 1, before)
+        z = combine(back_rows[1], 1, before, bf16, grad_router)
         z, y_far = lax.optimization_barrier((z, y_far))
         y_rows = add_low(y_near, y_far)
     else:
-        z = combine(back_rows[0], 0)
+        z = combine(back_rows[0], 0, None, bf16, grad_router)
         y_rows = y_rows[0]
     y_rows = exchange(y_rows)
     z = spread(z)
@@ -756,10 +770,10 @@
         (place,)
         + z
         + (hidden, cotangent, tokens, norm1, norm2, output_weight)
-        + (attended, q, k, v, probs, rel_bucket, grad_router),
-        [SMEM] + [VMEM] * 17,
-        10 * 10**9,
-        14 * 10**6,
+        + (attended, q, k, v, probs, rel_bucket),
+        [SMEM] + [VMEM] * 16,
+        4600 * 10**6,
+        12 * 10**6,
         scratch_shapes=[pltpu.VMEM((span, model), f32), pltpu.VMEM((4 * inner, model), f32)],
     )
     weights, y_rows = lax.optimization_barrier((weights, y_rows))

time: 260 us -> 259 us (level)
    ppermute x28 -> x26, starting transfers between devices: 21.7 us -> 20.6 us  [swap(): return lax.ppermute(value, 'tensor', [(i, i ^ bits) for i in range(lanes)])]
    ppermute x28 -> x26, waiting for transfers between devices: 40.5 us -> 39.9 us  [swap(): return lax.ppermute(value, 'tensor', [(i, i ^ bits) for i in range(lanes)])]
    unnamed x64 -> x66, local copies, waits for them, and re-layouts: 9.55 us -> 9.56 us
  transfers between devices with their start and end apart: 36 -> 34, of which waited for: 15 -> 15; matrix products, arithmetic and copies ran while one was open for 4% -> 3% of each run, Pallas kernels for 40% -> 40%
where the time goes in v4:
time: 259 us; the launch traced here: 257 us
  Pallas kernels  114 us (44%)
  waiting for transfers between devices  66.5 us (26%)
  starting transfers between devices  57.6 us (22%)
  local copies, waits for them, and re-layouts  10.1 us (4%)
  other arithmetic  8.62 us (3%)
    pallas_call x5, Pallas kernels, expert_call(): pl.pallas_call(kernel, out_shape=out_shape, grid_spec=pltpu.PrefetchScala...  55.7 us
    pallas_call x10, Pallas kernels, call(): pl.pallas_call(kernel, out_shape=out_shape, in_specs=specs, compiler_para...  46.7 us
    ppermute x26, waiting for transfers between devices, swap(): return lax.ppermute(value, 'tensor', [(i, i ^ bits) for i in range(lanes)])  39.9 us
    all_to_all x8, starting transfers between devices, exchange(): return lax.all_to_all(value, 'dp', split_axis=0, concat_axis=0, tiled=True)  37 us
    all_to_all x8, waiting for transfers between devices, exchange(): return lax.all_to_all(value, 'dp', split_axis=0, concat_axis=0, tiled=True)  26.6 us
    ppermute x26, starting transfers between devices, swap(): return lax.ppermute(value, 'tensor', [(i, i ^ bits) for i in range(lanes)])  20.6 us
    pallas_call x3, Pallas kernels, combine(): pl.pallas_call(functools.partial(combine_kernel, before=int(before is not...  11.3 us
    unnamed x66, local copies, waits for them, and re-layouts  9.56 us
  transfers between devices with their start and end apart: 34, of which 15 were waited for; matrix products, arithmetic and copies ran while one was open for 3% of the time, Pallas kernels for 40%

profile of v4, /device:TPU:1, one launch (start us, length us, event | category | flops | bytes accessed | tf_op | source)
XLA Modules:
  0.0 257.4 jit_solution(18419307862143282015)
XLA Ops:
  1.3 4.1 %shard_map.238 = (bf16[2048,512]{1,0:T(8,128)(2,1)}, bf16[8,144,384]{2,1,0:T(8,128)(2,1)}) custom-call(s32[4]{0:T(128)} %pad_add_fusion.place_ref.core_ref, s32[2,512]{1,0:T(2,128)} %bitcast.28, bf16[512,768]{1,0:T(8,128)(2,1)} %cotangent_ref.3), custom_call_target="tpu_custom_call" | custom-call | flops 3000000000 | bytes 6000000 | tf_op jit(solution)/shard_map/pallas_call | solution.py:41
  5.4 6.5 %all-to-all-start = ((bf16[8,144,384]{2,1,0:T(8,128)(2,1)}), bf16[8,144,384]{2,1,0:T(8,128)(2,1)S(1)}, u32[]{:S(2)}, u32[]{:S(2)}) async-start(bf16[8,144,384]{2,1,0:T(8,128)(2,1)} %get-tuple-element.95), calls=%async_computation | async-start | bytes 1769472 | tf_op jit(solution)/shard_map/all_to_all | solution.py:568
  11.9 1.3 collective-permute-start.4
  13.7 5.6 %shard_map.239 = (bf16[512,192]{1,0:T(8,128)(2,1)}, bf16[512,192]{1,0:T(8,128)(2,1)}, bf16[512,192]{1,0:T(8,128)(2,1)}, bf16[512,192]{1,0:T(8,128)(2,1)}, bf16[3,512,512]{2,1,0:T(8,128)(2,1)}) custom-call(s32[1,3]{1,0:T(1,128)} %lengths_ref.1, bf16[512,768]{1,0:T(8,128)(2,1)} %tokens_ref.7, s32[1,384]{1,0:T(1,128)} %reshape.33.rel_bucket_ref, ...), custom_call_target="tpu_custom_call" | custom-call | flops 6000000000 | bytes 8000000 | tf_op jit(solution)/shard_map/pallas_call | solution.py:41
  19.6 1.5 collective-permute-start.3
  21.6 4.5 %collective-permute-done.1.a2_ref = bf16[512,192]{1,0:T(8,128)(2,1)S(1)} collective-permute-done((bf16[512,192]{1,0:T(8,128)(2,1)}, bf16[512,192]{1,0:T(8,128)(2,1)S(1)}, u32[]{:S(2)}, u32[]{:S(2)}) %collective-permute-start.1) | collective-permute-done | bytes 196640 | tf_op jit(solution)/shard_map/ppermute | solution.py:561
  26.1 2.1 collective-permute-start.2
  30.2 6.8 %shard_map.240 = (f32[512,768]{1,0:T(8,128)}, bf16[8,128,384]{2,1,0:T(8,128)(2,1)}, bf16[8,128,384]{2,1,0:T(8,128)(2,1)}) custom-call(s32[4]{0:T(128)} %pad_add_fusion.place_ref.core_ref, bf16[512,768]{1,0:T(8,128)(2,1)} %tokens_ref.7, bf16[512,192]{1,0:T(8,128)(2,1)} %get-tuple-element.92.a0_ref.attended_ref, bf16[512,192]{1,0:T(8,128)(2,1)} %copy-done.31, ...), custom_call_target="tpu_custom_call" | custom-call | flops 2000000000 | bytes 8000000 | tf_op jit(solution)/shard_map/pallas_call | solution.py:41
  37.1 5.4 %all-to-all-start.1 = ((bf16[8,128,384]{2,1,0:T(8,128)(2,1)}), bf16[8,128,384]{2,1,0:T(8,128)(2,1)S(1)}, u32[]{:S(2)}, u32[]{:S(2)}) async-start(bf16[8,128,384]{2,1,0:T(8,128)(2,1)} %get-tuple-element.96), calls=%async_computation.1 | async-start | bytes 1572864 | tf_op jit(solution)/shard_map/all_to_all | solution.py:568
  43.3 1.8 collective-permute-done.6.oth_ref
  46.0 6.4 %shard_map.241 = (bf16[4,256,768]{2,1,0:T(8,128)(2,1)}, bf16[4,256,768]{2,1,0:T(8,128)(2,1)}, bf16[4,256,64]{2,1,0:T(8,128)(2,1)}) custom-call(s32[4]{0:T(128)} %pad_add_fusion.place_ref.core_ref, bf16[8,144,384]{2,1,0:T(8,128)(2,1)} %copy-done, bf16[8,144,384]{2,1,0:T(8,128)(2,1)} %copy-done, bf16[8,144,384]{2,1,0:T(8,128)(2,1)} %copy-done.10, ...), custom_call_target="tpu_custom_call" | custom-call | flops 1207959552 | bytes 10000000 | tf_op jit(solution)/shard_map/pallas_call | solution.py:638
  52.5 9.3 %all-to-all-done.1.n_own_ref.refs_0_ = bf16[8,128,384]{2,1,0:T(8,128)(2,1)S(1)} async-done(((bf16[8,128,384]{2,1,0:T(8,128)(2,1)}), bf16[8,128,384]{2,1,0:T(8,128)(2,1)S(1)}, u32[]{:S(2)}, u32[]{:S(2)}) %all-to-all-start.1) | async-done | bytes 786464 | tf_op jit(solution)/shard_map/all_to_all | solution.py:568
  61.8 1.7 collective-permute-start.7
  63.6 3.5 %all-to-all-start.2 = ((bf16[8,128,384]{2,1,0:T(8,128)(2,1)}), bf16[8,128,384]{2,1,0:T(8,128)(2,1)S(1)}, u32[]{:S(2)}, u32[]{:S(2)}) async-start(bf16[8,128,384]{2,1,0:T(8,128)(2,1)} %get-tuple-element.105), calls=%async_computation.2 | async-start | bytes 1572864 | tf_op jit(solution)/shard_map/all_to_all | solution.py:568
  67.2 12.0 %shard_map.242 = (bf16[8,128,384]{2,1,0:T(8,128)(2,1)}, bf16[8,128,384]{2,1,0:T(8,128)(2,1)}, bf16[4,256,768]{2,1,0:T(8,128)(2,1)}, bf16[4,256,768]{2,1,0:T(8,12...) custom-call(s32[4]{0:T(128)} %pad_add_fusion.place_ref.core_ref, ...), custom_call_target="tpu_custom_call" | custom-call | flops 3623878656 | bytes 17500000 | tf_op jit(solution)/shard_map/pallas_call | solution.py:638
  79.8 2.2 collective-permute-done.9
  82.0 2.2 add_convert_fusion.4
  85.1 6.4 %shard_map.243 = (bf16[4,256,768]{2,1,0:T(8,128)(2,1)}, bf16[4,256,768]{2,1,0:T(8,128)(2,1)}, bf16[4,256,64]{2,1,0:T(8,128)(2,1)}) custom-call(s32[4]{0:T(128)} %pad_add_fusion.place_ref.core_ref, bf16[8,144,384]{2,1,0:T(8,128)(2,1)} %copy-done.5, bf16[8,144,384]{2,1,0:T(8,128)(2,1)} %copy-done.5, bf16[8,144,384]{2,1,0:T(8,128)(2,1)} %copy-done.9, ...), custom_call_target="tpu_custom_call" | custom-call | flops 1207959552 | bytes 10000000 | tf_op jit(solution)/shard_map/pallas_call | solution.py:638
  91.8 5.7 %all-to-all-start.3 = ((bf16[8,128,384]{2,1,0:T(8,128)(2,1)}), bf16[8,128,384]{2,1,0:T(8,128)(2,1)S(1)}, u32[]{:S(2)}, u32[]{:S(2)}) async-start(bf16[8,128,384]{2,1,0:T(8,128)(2,1)} %add_convert_fusion.4), calls=%async_computation.3 | async-start | bytes 1572864 | tf_op jit(solution)/shard_map/all_to_all | solution.py:568
  98.3 12.1 %shard_map.244 = (bf16[8,128,384]{2,1,0:T(8,128)(2,1)}, bf16[8,128,384]{2,1,0:T(8,128)(2,1)}, bf16[4,256,768]{2,1,0:T(8,128)(2,1)}, bf16[4,256,768]{2,1,0:T(8,12...) custom-call(s32[4]{0:T(128)} %pad_add_fusion.place_ref.core_ref, ...), custom_call_target="tpu_custom_call" | custom-call | flops 3623878656 | bytes 17500000 | tf_op jit(solution)/shard_map/pallas_call | solution.py:638
  110.9 2.1 collective-permute-done.12
  113.0 2.3 add_convert_fusion.3
  115.3 2.0 all-to-all-done.3.rows_ref
  118.5 3.5 %all-to-all-start.4 = ((bf16[8,128,384]{2,1,0:T(8,128)(2,1)}), bf16[8,128,384]{2,1,0:T(8,128)(2,1)S(1)}, u32[]{:S(2)}, u32[]{:S(2)}) async-start(bf16[8,128,384]{2,1,0:T(8,128)(2,1)} %add_convert_fusion.3), calls=%async_computation.4 | async-start | bytes 1572864 | tf_op jit(solution)/shard_map/all_to_all | solution.py:568
  123.8 3.8 %shard_map.246.refs_0_ = f32[512,384]{1,0:T(8,128)} custom-call(s32[4]{0:T(128)} %pad_add_fusion.place_ref.core_ref, bf16[8,2,128,512]{3,2,1,0:T(8,128)(2,1)} %bitcast.13, bf16[8,128,384]{2,1,0:T(8,128)(2,1)} %copy-done.12), custom_call_target="tpu_custom_call" | custom-call | flops 1000000000 | bytes 4000000 | tf_op jit(solution)/shard_map/pallas_call | solution.py:723
  127.6 3.3 %shard_map.245.refs_1_ = f32[64,768]{1,0:T(8,128)} custom-call(s32[4]{0:T(128)} %pad_add_fusion.place_ref.core_ref, bf16[8,128,384]{2,1,0:T(8,128)(2,1)} %copy-done.1, bf16[8,128,384]{2,1,0:T(8,128)(2,1)} %collective-permute-done.7.n_oth_ref.refs_1_, bf16[4,256,64]{2,1,0:T(8,128)(2,1)} %get-tuple-element.119.refs_2_, bf16[8,128,384]{2,1,0:T(8,128)(2,1)} %copy-done.2, ...), custom_call_target="tpu_custom_call" | custom-call | flops 1000000000 | bytes 4000000 | tf_op jit(solution)/shard_map/pallas_call | solution.py:41
  130.9 11.2 %all-to-all-done.4.rows_ref = bf16[8,128,384]{2,1,0:T(8,128)(2,1)S(1)} async-done(((bf16[8,128,384]{2,1,0:T(8,128)(2,1)}), bf16[8,128,384]{2,1,0:T(8,128)(2,1)S(1)}, u32[]{:S(2)}, u32[]{:S(2)}) %all-to-all-start.4) | async-done | bytes 786464 | tf_op jit(solution)/shard_map/all_to_all | solution.py:568
  143.0 3.9 %shard_map.247.z0_ref = bf16[640,384]{1,0:T(8,128)(2,1)} custom-call(s32[4]{0:T(128)} %pad_add_fusion.place_ref.core_ref, bf16[8,2,128,512]{3,2,1,0:T(8,128)(2,1)} %bitcast.14, bf16[8,128,384]{2,1,0:T(8,128)(2,1)} %copy-done.7, f32[512,384]{1,0:T(8,128)} %shard_map.246.refs_0_, f32[64,768]{1,0:T(8,128)} %shard_map.245.refs_1_), custom_call_target="tpu_custom_call" | custom-call | flops 1000000000 | bytes 4000000 | tf_op jit(solution)/shard_map/pallas_call | solution.py:723
  148.4 4.0 %all-to-all-start.5 = ((bf16[8,128,384]{2,1,0:T(8,128)(2,1)}), bf16[8,128,384]{2,1,0:T(8,128)(2,1)S(1)}, u32[]{:S(2)}, u32[]{:S(2)}) async-start(bf16[8,128,384]{2,1,0:T(8,128)(2,1)} %add_convert_fusion), calls=%async_computation.5 | async-start | bytes 1572864 | tf_op jit(solution)/shard_map/all_to_all | solution.py:568
  153.5 5.5 %collective-permute-done.16.z2_ref = bf16[640,384]{1,0:T(8,128)(2,1)} collective-permute-done((bf16[640,384]{1,0:T(8,128)(2,1)}, bf16[640,384]{1,0:T(8,128)(2,1)}, u32[]{:S(2)}, u32[]{:S(2)}) %collective-permute-start.16) | collective-permute-done | bytes 491552 | tf_op jit(solution)/shard_map/ppermute | solution.py:561
  158.9 1.9 collective-permute-start.17
  160.9 1.7 collective-permute-done.17.z3_ref
  163.3 11.0 %shard_map.248 = (f32[512,768]{1,0:T(8,128)}, bf16[8,112,768]{2,1,0:T(8,128)(2,1)}, bf16[3,512,192]{2,1,0:T(8,128)(2,1)}) custom-call(s32[4]{0:T(128)} %pad_add_fusion.place_ref.core_ref, bf16[640,384]{1,0:T(8,128)(2,1)} %shard_map.247.z0_ref, bf16[640,384]{1,0:T(8,128)(2,1)} %copy-done.24, bf16[640,384]{1,0:T(8,128)(2,1)} %collective-permute-done.16.z2_ref, ...), custom_call_target="tpu_custom_call" | custom-call | flops 4600000000 | bytes 12000000 | tf_op jit(solution)/shard_map/pallas_call | solution.py:41
  174.3 3.9 %all-to-all-start.6 = ((bf16[8,112,768]{2,1,0:T(8,128)(2,1)}), bf16[8,112,768]{2,1,0:T(8,128)(2,1)S(1)}, u32[]{:S(2)}, u32[]{:S(2)}) async-start(bf16[8,112,768]{2,1,0:T(8,128)(2,1)} %get-tuple-element.140), calls=%async_computation.6 | async-start | bytes 2752512 | tf_op jit(solution)/shard_map/all_to_all | solution.py:568
  178.2 3.2 %shard_map.249 = (f32[512,384]{1,0:T(8,128)}, bf16[512,384]{1,0:T(8,128)(2,1)}) custom-call(s32[4]{0:T(128)} %pad_add_fusion.place_ref.core_ref, bf16[3,512,192]{2,1,0:T(8,128)(2,1)} %get-tuple-element.142.low_ref, bf16[192,768]{1,0:T(8,128)(2,1)} %bitcast.22, bf16[192,768]{1,0:T(8,128)(2,1)} %bitcast.24, bf16[192,768]{1,0:T(8,128)(2,1)} %bitcast.26), custom_call_target="tpu_custom_call" | custom-call | flops 1000000000 | bytes 4000000 | tf_op jit(solution)/shard_map/pallas_call | solution.py:41
  182.1 1.6 collective-permute-done.19
  185.9 9.4 %collective-permute-done.21.u2_ref = bf16[512,384]{1,0:T(8,128)(2,1)S(1)} collective-permute-done((bf16[512,384]{1,0:T(8,128)(2,1)S(1)}, bf16[512,384]{1,0:T(8,128)(2,1)S(1)}, u32[]{:S(2)}, u32[]{:S(2)}) %collective-permute-start.21) | collective-permute-done | bytes 393248 | tf_op jit(solution)/shard_map/ppermute | solution.py:561
  196.5 1.3 collective-permute-done.22.u3_ref
  198.6 4.2 %shard_map.250 = (f32[512,768]{1,0:T(8,128)}, bf16[16,768]{1,0:T(8,128)(2,1)}) custom-call(s32[4]{0:T(128)} %pad_add_fusion.place_ref.core_ref, bf16[512,384]{1,0:T(8,128)(2,1)} %copy-done.8, bf16[512,384]{1,0:T(8,128)(2,1)} %copy-done.21, bf16[512,384]{1,0:T(8,128)(2,1)} %copy-done.20, bf16[512,384]{1,0:T(8,128)(2,1)} %copy-done.22, ...), custom_call_target="tpu_custom_call" | custom-call | flops 10000000 | bytes 6000000 | tf_op jit(solution)/shard_map/pallas_call | solution.py:41
  202.8 3.6 %shard_map.251.y0_ref = bf16[512,384]{1,0:T(8,128)(2,1)} custom-call(s32[4]{0:T(128)} %pad_add_fusion.place_ref.core_ref, bf16[8,2,128,512]{3,2,1,0:T(8,128)(2,1)} %bitcast.15, bf16[8,128,384]{2,1,0:T(8,128)(2,1)} %copy-done.11), custom_call_target="tpu_custom_call" | custom-call | flops 1000000000 | bytes 4000000 | tf_op jit(solution)/shard_map/pallas_call | solution.py:723
  206.4 4.1 %all-to-all-done.6.rows_ref = bf16[8,112,768]{2,1,0:T(8,128)(2,1)S(1)} async-done(((bf16[8,112,768]{2,1,0:T(8,128)(2,1)}), bf16[8,112,768]{2,1,0:T(8,128)(2,1)S(1)}, u32[]{:S(2)}, u32[]{:S(2)}) %all-to-all-start.6) | async-done | bytes 1376288 | tf_op jit(solution)/shard_map/all_to_all | solution.py:568
  211.6 2.6 %shard_map.253 = bf16[8,112,768]{2,1,0:T(8,128)(2,1)} custom-call(bf16[8,112,768]{2,1,0:T(8,128)(2,1)} %copy-done.4, bf16[16,768]{1,0:T(8,128)(2,1)} %get-tuple-element.153.norm_row_ref), custom_call_target="tpu_custom_call" | custom-call | flops 10000000 | bytes 3000000 | tf_op jit(solution)/shard_map/pallas_call | solution.py:41
  214.2 4.5 %all-to-all-start.7 = ((bf16[8,112,768]{2,1,0:T(8,128)(2,1)}), bf16[8,112,768]{2,1,0:T(8,128)(2,1)S(1)}, u32[]{:S(2)}, u32[]{:S(2)}) async-start(bf16[8,112,768]{2,1,0:T(8,128)(2,1)} %shard_map.253), calls=%async_computation.7 | async-start | bytes 2752512 | tf_op jit(solution)/shard_map/all_to_all | solution.py:568
  220.0 8.6 %collective-permute-done.24.y2_ref = bf16[512,384]{1,0:T(8,128)(2,1)S(1)} collective-permute-done((bf16[512,384]{1,0:T(8,128)(2,1)S(1)}, bf16[512,384]{1,0:T(8,128)(2,1)S(1)}, u32[]{:S(2)}, u32[]{:S(2)}) %collective-permute-start.24) | collective-permute-done | bytes 393248 | tf_op jit(solution)/shard_map/ppermute | solution.py:561
  228.6 1.7 collective-permute-start.25
  230.3 18.7 %shard_map.255 = (f32[8,768,768]{2,1,0:T(8,128)}, f32[8,768,768]{2,1,0:T(8,128)}) custom-call(s32[4]{0:T(128)} %pad_add_fusion.place_ref.core_ref, bf16[8,128,384]{2,1,0:T(8,128)(2,1)} %copy-done.1, bf16[8,128,384]{2,1,0:T(8,128)(2,1)} %collective-permute-done.7.n_oth_ref.refs_1_, bf16[4,256,768]{2,1,0:T(8,128)(2,1)} %get-tuple-element.162.refs_2_, ...), custom_call_target="tpu_custom_call" | custom-call | flops 4831838208 | bytes 55000000 | tf_op jit(solution)/shard_map/pallas_call | solution.py:638
  250.5 3.0 %shard_map.252 = bf16[512,768]{1,0:T(8,128)(2,1)} custom-call(s32[4]{0:T(128)} %pad_add_fusion.place_ref.core_ref, bf16[512,384]{1,0:T(8,128)(2,1)} %shard_map.251.y0_ref, bf16[512,384]{1,0:T(8,128)(2,1)} %copy-done.18, bf16[512,384]{1,0:T(8,128)(2,1)} %copy-done.17, bf16[512,384]{1,0:T(8,128)(2,1)} %copy-done.19, f32[512,768]{1,0:T(8,128)} %get-tuple-element.131.hidden_ref), custom_call_target="tpu_custom_call" | custom-call | flops 10000000 | bytes 4000000 | tf_op jit(solution)/shard_map/pallas_call | solution.py:41
  254.6 2.9 %shard_map.254 = (f32[768]{0:T(1024)}, f32[192,768]{1,0:T(8,128)}, f32[192,768]{1,0:T(8,128)}, f32[192,768]{1,0:T(8,128)}, f32[192,768]{1,0:T(8,128)}, /*index=5...) custom-call(bf16[8,112,768]{2,1,0:T(8,128)(2,1)} %copy-done.3), custom_call_target="tpu_custom_call" | custom-call | flops 10000000 | bytes 5000000 | tf_op jit(solution)/shard_map/pallas_call | solution.py:41
  (111 shorter events, 25.8 us)
Async XLA Ops:
  5.4 6.5 %copy-start.26 = (bf16[192,768]{1,0:T(8,128)(2,1)S(1)}, bf16[192,768]{1,0:T(8,128)(2,1)}, u32[]{:S(2)}) copy-start(bf16[192,768]{1,0:T(8,128)(2,1)} %wo_ref.1) | copy-start | bytes 884740
  5.4 7.8 %copy-start.23 = (s32[384]{0:T(512)S(1)}, s32[384]{0:T(512)}, u32[]{:S(2)}) copy-start(s32[384]{0:T(512)} %param.18) | copy-start | bytes 4612
  5.4 31.7 %all-to-all-start = ((bf16[8,144,384]{2,1,0:T(8,128)(2,1)}), bf16[8,144,384]{2,1,0:T(8,128)(2,1)S(1)}, u32[]{:S(2)}, u32[]{:S(2)}) async-start(bf16[8,144,384]{2,1,0:T(8,128)(2,1)} %get-tuple-element.95), calls=%async_computation | async-start | bytes 1769472 | tf_op jit(solution)/shard_map/all_to_all | solution.py:568
  11.9 9.2 %collective-permute-start.4 = (bf16[192,768]{1,0:T(8,128)(2,1)S(1)}, bf16[192,768]{1,0:T(8,128)(2,1)S(1)}, u32[]{:S(2)}, u32[]{:S(2)}) collective-permute-start(bf16[192,768]{1,0:T(8,128)(2,1)S(1)} %copy-done.26), channel_id=1, source_target_pairs={{0,2},{1,3},{2,0},{3,1},{4,6},{5,7},{6,4},{7,5},{8,10},{9,11},{10,... | collective-permute-start | bytes 884744 | tf_op jit(solution)/shard_map/ppermute | solution.py:561
  19.3 6.8 %collective-permute-start.1 = (bf16[512,192]{1,0:T(8,128)(2,1)}, bf16[512,192]{1,0:T(8,128)(2,1)S(1)}, u32[]{:S(2)}, u32[]{:S(2)}) collective-permute-start(bf16[512,192]{1,0:T(8,128)(2,1)} %get-tuple-element.92.a0_ref.attended_ref), channel_id=1, source_target_pairs={{0,2},{1,3},{2,0},{3,1},{4,6},{5,7},{6,4},{7,5},{8,10},{9,11},{10,... | collective-permute-start | bytes 589832 | tf_op jit(solution)/shard_map/ppermute | solution.py:561
  19.6 8.7 %collective-permute-start.3 = (bf16[192,768]{1,0:T(8,128)(2,1)S(1)}, bf16[192,768]{1,0:T(8,128)(2,1)S(1)}, u32[]{:S(2)}, u32[]{:S(2)}) collective-permute-start(bf16[192,768]{1,0:T(8,128)(2,1)S(1)} %copy-done.26), channel_id=1, source_target_pairs={{0,1},{1,0},{2,3},{3,2},{4,5},{5,4},{6,7},{7,6},{8,9},{9,8},{10,11... | collective-permute-start | bytes 884744 | tf_op jit(solution)/shard_map/ppermute | solution.py:561
  21.1 8.4 %copy-start.27 = (bf16[192,768]{1,0:T(8,128)(2,1)}, bf16[192,768]{1,0:T(8,128)(2,1)S(1)}, u32[]{:S(2)}) copy-start(bf16[192,768]{1,0:T(8,128)(2,1)S(1)} %collective-permute-done.4.w2_ref) | copy-start | bytes 884740
  21.1 8.3 %collective-permute-start.5 = (bf16[192,768]{1,0:T(8,128)(2,1)S(1)}, bf16[192,768]{1,0:T(8,128)(2,1)S(1)}, u32[]{:S(2)}, u32[]{:S(2)}) collective-permute-start(bf16[192,768]{1,0:T(8,128)(2,1)S(1)} %collective-permute-done.4.w2_ref), channel_id=1, source_target_pairs={{0,1},{1,0},{2,3},{3,2},{4,5},{5,4},{6,7},{7,6},{8,9},{9,8},{10,11... | collective-permute-start | bytes 884744 | tf_op jit(solution)/shard_map/ppermute | solution.py:561
  21.4 6.9 %collective-permute-start = (bf16[512,192]{1,0:T(8,128)(2,1)}, bf16[512,192]{1,0:T(8,128)(2,1)S(1)}, u32[]{:S(2)}, u32[]{:S(2)}) collective-permute-start(bf16[512,192]{1,0:T(8,128)(2,1)} %get-tuple-element.92.a0_ref.attended_ref), channel_id=1, source_target_pairs={{0,1},{1,0},{2,3},{3,2},{4,5},{5,4},{6,7},{7,6},{8,9},{9,8},{10,11... | collective-permute-start | bytes 589832 | tf_op jit(solution)/shard_map/ppermute | solution.py:561
  26.1 3.3 %collective-permute-start.2 = (bf16[512,192]{1,0:T(8,128)(2,1)S(1)}, bf16[512,192]{1,0:T(8,128)(2,1)S(1)}, u32[]{:S(2)}, u32[]{:S(2)}) collective-permute-start(bf16[512,192]{1,0:T(8,128)(2,1)S(1)} %collective-permute-done.1.a2_ref), channel_id=1, source_target_pairs={{0,1},{1,0},{2,3},{3,2},{4,5},{5,4},{6,7},{7,6},{8,9},{9,8},{10,11... | collective-permute-start | bytes 589832 | tf_op jit(solution)/shard_map/ppermute | solution.py:561
  37.1 8.1 %copy-start = (bf16[8,144,384]{2,1,0:T(8,128)(2,1)}, bf16[8,144,384]{2,1,0:T(8,128)(2,1)S(1)}, u32[]{:S(2)}) copy-start(bf16[8,144,384]{2,1,0:T(8,128)(2,1)S(1)} %all-to-all-done.ids_ref.own_ref) | copy-start | bytes 2654212
  37.1 24.7 %all-to-all-start.1 = ((bf16[8,128,384]{2,1,0:T(8,128)(2,1)}), bf16[8,128,384]{2,1,0:T(8,128)(2,1)S(1)}, u32[]{:S(2)}, u32[]{:S(2)}) async-start(bf16[8,128,384]{2,1,0:T(8,128)(2,1)} %get-tuple-element.96), calls=%async_computation.1 | async-start | bytes 1572864 | tf_op jit(solution)/shard_map/all_to_all | solution.py:568
  42.5 2.7 %collective-permute-start.6 = (bf16[8,144,384]{2,1,0:T(8,128)(2,1)S(1)}, bf16[8,144,384]{2,1,0:T(8,128)(2,1)S(1)}, u32[]{:S(2)}, u32[]{:S(2)}) collective-permute-start(bf16[8,144,384]{2,1,0:T(8,128)(2,1)S(1)} %all-to-all-done.ids_ref.own_ref), channel_id=1, source_target_pairs={{0,1},{1,0},{2,3},{3,2},{4,5},{5,4},{6,7},{7,6},{8,9},{9,8},{10,11... | collective-permute-start | bytes 2654216 | tf_op jit(solution)/shard_map/ppermute | solution.py:561
  43.1 24.0 %collective-permute-start.8 = (bf16[8,144,384]{2,1,0:T(8,128)(2,1)S(1)}, bf16[8,144,384]{2,1,0:T(8,128)(2,1)S(1)}, u32[]{:S(2)}, u32[]{:S(2)}) collective-permute-start(bf16[8,144,384]{2,1,0:T(8,128)(2,1)S(1)} %all-to-all-done.ids_ref.own_ref), channel_id=1, source_target_pairs={{0,2},{1,3},{2,0},{3,1},{4,6},{5,7},{6,4},{7,5},{8,10},{9,11},{10,... | collective-permute-start | bytes 2654216 | tf_op jit(solution)/shard_map/ppermute | solution.py:561
  61.8 5.3 %copy-start.1 = (bf16[8,128,384]{2,1,0:T(8,128)(2,1)}, bf16[8,128,384]{2,1,0:T(8,128)(2,1)S(1)}, u32[]{:S(2)}) copy-start(bf16[8,128,384]{2,1,0:T(8,128)(2,1)S(1)} %all-to-all-done.1.n_own_ref.refs_0_) | copy-start | bytes 2359300
  61.8 5.3 %collective-permute-start.7 = (bf16[8,128,384]{2,1,0:T(8,128)(2,1)S(1)}, bf16[8,128,384]{2,1,0:T(8,128)(2,1)}, u32[]{:S(2)}, u32[]{:S(2)}) collective-permute-start(bf16[8,128,384]{2,1,0:T(8,128)(2,1)S(1)} %all-to-all-done.1.n_own_ref.refs_0_), channel_id=1, source_target_pairs={{0,1},{1,0},{2,3},{3,2},{4,5},{5,4},{6,7},{7,6},{8,9},{9,8},{10,11... | collective-permute-start | bytes 2359304 | tf_op jit(solution)/shard_map/ppermute | solution.py:561
  63.6 28.0 %all-to-all-start.2 = ((bf16[8,128,384]{2,1,0:T(8,128)(2,1)}), bf16[8,128,384]{2,1,0:T(8,128)(2,1)S(1)}, u32[]{:S(2)}, u32[]{:S(2)}) async-start(bf16[8,128,384]{2,1,0:T(8,128)(2,1)} %get-tuple-element.105), calls=%async_computation.2 | async-start | bytes 1572864 | tf_op jit(solution)/shard_map/all_to_all | solution.py:568
  67.1 12.2 %copy-start.5 = (bf16[8,144,384]{2,1,0:T(8,128)(2,1)}, bf16[8,144,384]{2,1,0:T(8,128)(2,1)S(1)}, u32[]{:S(2)}) copy-start(bf16[8,144,384]{2,1,0:T(8,128)(2,1)S(1)} %collective-permute-done.8.ids_ref.own_ref) | copy-start | bytes 2654212
  79.2 2.8 %collective-permute-start.9 = (bf16[8,128,384]{2,1,0:T(8,128)(2,1)}, bf16[8,128,384]{2,1,0:T(8,128)(2,1)S(1)}, u32[]{:S(2)}, u32[]{:S(2)}) collective-permute-start(bf16[8,128,384]{2,1,0:T(8,128)(2,1)} %get-tuple-element.104), channel_id=1, source_target_pairs={{0,1},{1,0},{2,3},{3,2},{4,5},{5,4},{6,7},{7,6},{8,9},{9,8},{10,11... | collective-permute-start | bytes 2359304 | tf_op jit(solution)/shard_map/ppermute | solution.py:561
  79.3 4.9 %collective-permute-start.10 = (bf16[8,144,384]{2,1,0:T(8,128)(2,1)S(1)}, bf16[8,144,384]{2,1,0:T(8,128)(2,1)S(1)}, u32[]{:S(2)}, u32[]{:S(2)}) collective-permute-start(bf16[8,144,384]{2,1,0:T(8,128)(2,1)S(1)} %collective-permute-done.8.ids_ref.own_ref), channel_id=1, source_target_pairs={{0,1},{1,0},{2,3},{3,2},{4,5},{5,4},{6,7},{7,6},{8,9},{9,8},{10,11... | collective-permute-start | bytes 2654216 | tf_op jit(solution)/shard_map/ppermute | solution.py:561
  91.6 5.9 %copy-start.2 = (bf16[8,128,384]{2,1,0:T(8,128)(2,1)}, bf16[8,128,384]{2,1,0:T(8,128)(2,1)S(1)}, u32[]{:S(2)}) copy-start(bf16[8,128,384]{2,1,0:T(8,128)(2,1)S(1)} %all-to-all-done.2.n_own_ref.refs_3_.refs_5_) | copy-start | bytes 2359300
  91.6 5.9 %collective-permute-start.11 = (bf16[8,128,384]{2,1,0:T(8,128)(2,1)S(1)}, bf16[8,128,384]{2,1,0:T(8,128)(2,1)S(1)}, u32[]{:S(2)}, u32[]{:S(2)}) collective-permute-start(bf16[8,128,384]{2,1,0:T(8,128)(2,1)S(1)} %all-to-all-done.2.n_own_ref.refs_3_.refs_5_), channel_id=1, source_target_pairs={{0,1},{1,0},{2,3},{3,2},{4,5},{5,4},{6,7},{7,6},{8,9},{9,8},{10,11... | collective-permute-start | bytes 2359304 | tf_op jit(solution)/shard_map/ppermute | solution.py:561
  91.8 25.5 %all-to-all-start.3 = ((bf16[8,128,384]{2,1,0:T(8,128)(2,1)}), bf16[8,128,384]{2,1,0:T(8,128)(2,1)S(1)}, u32[]{:S(2)}, u32[]{:S(2)}) async-start(bf16[8,128,384]{2,1,0:T(8,128)(2,1)} %add_convert_fusion.4), calls=%async_computation.3 | async-start | bytes 1572864 | tf_op jit(solution)/shard_map/all_to_all | solution.py:568
  110.4 2.6 %collective-permute-start.12 = (bf16[8,128,384]{2,1,0:T(8,128)(2,1)}, bf16[8,128,384]{2,1,0:T(8,128)(2,1)S(1)}, u32[]{:S(2)}, u32[]{:S(2)}) collective-permute-start(bf16[8,128,384]{2,1,0:T(8,128)(2,1)} %get-tuple-element.112), channel_id=1, source_target_pairs={{0,1},{1,0},{2,3},{3,2},{4,5},{5,4},{6,7},{7,6},{8,9},{9,8},{10,11... | collective-permute-start | bytes 2359304 | tf_op jit(solution)/shard_map/ppermute | solution.py:561
  113.0 9.1 %copy-start.14 = (bf16[8,128,384]{2,1,0:T(8,128)(2,1)S(1)}, bf16[8,128,384]{2,1,0:T(8,128)(2,1)}, u32[]{:S(2)}) copy-start(bf16[8,128,384]{2,1,0:T(8,128)(2,1)} %get-tuple-element.121) | copy-start | bytes 2359300
  117.3 5.9 %copy-start.12 = (bf16[8,128,384]{2,1,0:T(8,128)(2,1)}, bf16[8,128,384]{2,1,0:T(8,128)(2,1)S(1)}, u32[]{:S(2)}) copy-start(bf16[8,128,384]{2,1,0:T(8,128)(2,1)S(1)} %all-to-all-done.3.rows_ref) | copy-start | bytes 2359300
  117.3 4.8 %collective-permute-start.13 = (bf16[8,128,384]{2,1,0:T(8,128)(2,1)}, bf16[8,128,384]{2,1,0:T(8,128)(2,1)S(1)}, u32[]{:S(2)}, u32[]{:S(2)}) collective-permute-start(bf16[8,128,384]{2,1,0:T(8,128)(2,1)} %get-tuple-element.122), channel_id=1, source_target_pairs={{0,1},{1,0},{2,3},{3,2},{4,5},{5,4},{6,7},{7,6},{8,9},{9,8},{10,11... | collective-permute-start | bytes 2359304 | tf_op jit(solution)/shard_map/ppermute | solution.py:561
  118.5 23.6 %all-to-all-start.4 = ((bf16[8,128,384]{2,1,0:T(8,128)(2,1)}), bf16[8,128,384]{2,1,0:T(8,128)(2,1)S(1)}, u32[]{:S(2)}, u32[]{:S(2)}) async-start(bf16[8,128,384]{2,1,0:T(8,128)(2,1)} %add_convert_fusion.3), calls=%async_computation.4 | async-start | bytes 1572864 | tf_op jit(solution)/shard_map/all_to_all | solution.py:568
  123.2 23.7 %collective-permute-start.14 = (bf16[8,128,384]{2,1,0:T(8,128)(2,1)}, bf16[8,128,384]{2,1,0:T(8,128)(2,1)S(1)}, u32[]{:S(2)}, u32[]{:S(2)}) collective-permute-start(bf16[8,128,384]{2,1,0:T(8,128)(2,1)} %add_convert_fusion.2), channel_id=1, source_target_pairs={{0,2},{1,3},{2,0},{3,1},{4,6},{5,7},{6,4},{7,5},{8,10},{9,11},{10,... | collective-permute-start | bytes 2359304 | tf_op jit(solution)/shard_map/ppermute | solution.py:561
  123.5 23.7 %collective-permute-start.18 = (bf16[8,128,384]{2,1,0:T(8,128)(2,1)}, bf16[8,128,384]{2,1,0:T(8,128)(2,1)S(1)}, u32[]{:S(2)}, u32[]{:S(2)}) collective-permute-start(bf16[8,128,384]{2,1,0:T(8,128)(2,1)} %get-tuple-element.138), channel_id=1, source_target_pairs={{0,1},{1,0},{2,3},{3,2},{4,5},{5,4},{6,7},{7,6},{8,9},{9,8},{10,11... | collective-permute-start | bytes 2359304 | tf_op jit(solution)/shard_map/ppermute | solution.py:561
  130.9 16.2 %copy-start.13 = (bf16[8,128,384]{2,1,0:T(8,128)(2,1)S(1)}, bf16[8,128,384]{2,1,0:T(8,128)(2,1)}, u32[]{:S(2)}) copy-start(bf16[8,128,384]{2,1,0:T(8,128)(2,1)} %get-tuple-element.137) | copy-start | bytes 2359300
  146.9 12.0 %collective-permute-start.16 = (bf16[640,384]{1,0:T(8,128)(2,1)}, bf16[640,384]{1,0:T(8,128)(2,1)}, u32[]{:S(2)}, u32[]{:S(2)}) collective-permute-start(bf16[640,384]{1,0:T(8,128)(2,1)} %shard_map.247.z0_ref), channel_id=1, source_target_pairs={{0,2},{1,3},{2,0},{3,1},{4,6},{5,7},{6,4},{7,5},{8,10},{9,11},{10,... | collective-permute-start | bytes 1474568 | tf_op jit(solution)/shard_map/ppermute | solution.py:561
  148.4 26.0 %all-to-all-start.5 = ((bf16[8,128,384]{2,1,0:T(8,128)(2,1)}), bf16[8,128,384]{2,1,0:T(8,128)(2,1)S(1)}, u32[]{:S(2)}, u32[]{:S(2)}) async-start(bf16[8,128,384]{2,1,0:T(8,128)(2,1)} %add_convert_fusion), calls=%async_computation.5 | async-start | bytes 1572864 | tf_op jit(solution)/shard_map/all_to_all | solution.py:568
  152.4 8.5 %collective-permute-start.15 = (bf16[640,384]{1,0:T(8,128)(2,1)S(1)}, bf16[640,384]{1,0:T(8,128)(2,1)S(1)}, u32[]{:S(2)}, u32[]{:S(2)}) collective-permute-start(bf16[640,384]{1,0:T(8,128)(2,1)S(1)} %copy-done.15), channel_id=1, source_target_pairs={{0,1},{1,0},{2,3},{3,2},{4,5},{5,4},{6,7},{7,6},{8,9},{9,8},{10,11... | collective-permute-start | bytes 1474568 | tf_op jit(solution)/shard_map/ppermute | solution.py:561
  158.9 3.6 %collective-permute-start.17 = (bf16[640,384]{1,0:T(8,128)(2,1)}, bf16[640,384]{1,0:T(8,128)(2,1)S(1)}, u32[]{:S(2)}, u32[]{:S(2)}) collective-permute-start(bf16[640,384]{1,0:T(8,128)(2,1)} %collective-permute-done.16.z2_ref), channel_id=1, source_target_pairs={{0,1},{1,0},{2,3},{3,2},{4,5},{5,4},{6,7},{7,6},{8,9},{9,8},{10,11... | collective-permute-start | bytes 1474568 | tf_op jit(solution)/shard_map/ppermute | solution.py:561
  174.3 7.1 %copy-start.11 = (bf16[8,128,384]{2,1,0:T(8,128)(2,1)}, bf16[8,128,384]{2,1,0:T(8,128)(2,1)S(1)}, u32[]{:S(2)}) copy-start(bf16[8,128,384]{2,1,0:T(8,128)(2,1)S(1)} %all-to-all-done.5.rows_ref) | copy-start | bytes 2359300
  174.3 36.2 %all-to-all-start.6 = ((bf16[8,112,768]{2,1,0:T(8,128)(2,1)}), bf16[8,112,768]{2,1,0:T(8,128)(2,1)S(1)}, u32[]{:S(2)}, u32[]{:S(2)}) async-start(bf16[8,112,768]{2,1,0:T(8,128)(2,1)} %get-tuple-element.140), calls=%async_computation.6 | async-start | bytes 2752512 | tf_op jit(solution)/shard_map/all_to_all | solution.py:568
  181.5 2.2 collective-permute-start.19
  184.9 13.0 %copy-start.8 = (bf16[512,384]{1,0:T(8,128)(2,1)}, bf16[512,384]{1,0:T(8,128)(2,1)S(1)}, u32[]{:S(2)}) copy-start(bf16[512,384]{1,0:T(8,128)(2,1)S(1)} %add_convert_fusion.5.u0_ref) | copy-start | bytes 1179652
  184.9 10.4 %collective-permute-start.21 = (bf16[512,384]{1,0:T(8,128)(2,1)S(1)}, bf16[512,384]{1,0:T(8,128)(2,1)S(1)}, u32[]{:S(2)}, u32[]{:S(2)}) collective-permute-start(bf16[512,384]{1,0:T(8,128)(2,1)S(1)} %add_convert_fusion.5.u0_ref), channel_id=1, source_target_pairs={{0,2},{1,3},{2,0},{3,1},{4,6},{5,7},{6,4},{7,5},{8,10},{9,11},{10,... | collective-permute-start | bytes 1179656 | tf_op jit(solution)/shard_map/ppermute | solution.py:561
  185.2 11.3 %collective-permute-start.20 = (bf16[512,384]{1,0:T(8,128)(2,1)S(1)}, bf16[512,384]{1,0:T(8,128)(2,1)S(1)}, u32[]{:S(2)}, u32[]{:S(2)}) collective-permute-start(bf16[512,384]{1,0:T(8,128)(2,1)S(1)} %add_convert_fusion.5.u0_ref), channel_id=1, source_target_pairs={{0,1},{1,0},{2,3},{3,2},{4,5},{5,4},{6,7},{7,6},{8,9},{9,8},{10,11... | collective-permute-start | bytes 1179656 | tf_op jit(solution)/shard_map/ppermute | solution.py:561
  195.3 2.6 collective-permute-start.22
  214.2 4.5 %copy-start.16 = (bf16[512,384]{1,0:T(8,128)(2,1)S(1)}, bf16[512,384]{1,0:T(8,128)(2,1)}, u32[]{:S(2)}) copy-start(bf16[512,384]{1,0:T(8,128)(2,1)} %shard_map.251.y0_ref) | copy-start | bytes 1179652
  214.2 39.3 %all-to-all-start.7 = ((bf16[8,112,768]{2,1,0:T(8,128)(2,1)}), bf16[8,112,768]{2,1,0:T(8,128)(2,1)S(1)}, u32[]{:S(2)}, u32[]{:S(2)}) async-start(bf16[8,112,768]{2,1,0:T(8,128)(2,1)} %shard_map.253), calls=%async_computation.7 | async-start | bytes 2752512 | tf_op jit(solution)/shard_map/all_to_all | solution.py:568
  218.7 9.9 %collective-permute-start.24 = (bf16[512,384]{1,0:T(8,128)(2,1)S(1)}, bf16[512,384]{1,0:T(8,128)(2,1)S(1)}, u32[]{:S(2)}, u32[]{:S(2)}) collective-permute-start(bf16[512,384]{1,0:T(8,128)(2,1)S(1)} %copy-done.16), channel_id=1, source_target_pairs={{0,2},{1,3},{2,0},{3,1},{4,6},{5,7},{6,4},{7,5},{8,10},{9,11},{10,... | collective-permute-start | bytes 1179656 | tf_op jit(solution)/shard_map/ppermute | solution.py:561
  219.0 30.0 %collective-permute-start.23 = (bf16[512,384]{1,0:T(8,128)(2,1)S(1)}, bf16[512,384]{1,0:T(8,128)(2,1)S(1)}, u32[]{:S(2)}, u32[]{:S(2)}) collective-permute-start(bf16[512,384]{1,0:T(8,128)(2,1)S(1)} %copy-done.16), channel_id=1, source_target_pairs={{0,1},{1,0},{2,3},{3,2},{4,5},{5,4},{6,7},{7,6},{8,9},{9,8},{10,11... | collective-permute-start | bytes 1179656 | tf_op jit(solution)/shard_map/ppermute | solution.py:561
  228.6 20.3 %copy-start.17 = (bf16[512,384]{1,0:T(8,128)(2,1)}, bf16[512,384]{1,0:T(8,128)(2,1)S(1)}, u32[]{:S(2)}) copy-start(bf16[512,384]{1,0:T(8,128)(2,1)S(1)} %collective-permute-done.24.y2_ref) | copy-start | bytes 1179652
  228.6 20.4 %collective-permute-start.25 = (bf16[512,384]{1,0:T(8,128)(2,1)S(1)}, bf16[512,384]{1,0:T(8,128)(2,1)S(1)}, u32[]{:S(2)}, u32[]{:S(2)}) collective-permute-start(bf16[512,384]{1,0:T(8,128)(2,1)S(1)} %collective-permute-done.24.y2_ref), channel_id=1, source_target_pairs={{0,1},{1,0},{2,3},{3,2},{4,5},{5,4},{6,7},{7,6},{8,9},{9,8},{10,11... | collective-permute-start | bytes 1179656 | tf_op jit(solution)/shard_map/ppermute | solution.py:561
  (19 other events, 25.6 us)
